TPU v7x, 256 devices: a whole 4x4x8 slice. The times are simulated.
256 devices in a mesh: rep: 8 (over x, z_hi), fsdp: 32 (over z_lo, y, core).
Axes of the slice: x: 4, y: 4, z: 8 (z_hi: 2, z_lo: 4; z = z_hi * 4 + z_lo), core: 2. Of those that a mesh axis runs over, the one named last changes fastest.
Arguments:
- tokens: bfloat16 [4096, 4096], P(('rep', 'fsdp')), may hold values from -6 to 6
- upstream: bfloat16 [4096, 14336], P(('rep', 'fsdp')), may hold values from -6 to 6
- blocks: bfloat16 [224, 16, 128, 128], P('fsdp'), may hold values from -0.125 to 0.125
- keep_mask: int32 [32, 112], replicated, may hold values from 0 to 1, as said below
- panel_owner: int32 [112], replicated, may hold values from 0 to 31, as said below
Outputs:
- activation: bfloat16 [4096, 14336], P(('rep', 'fsdp'))
- input_grad: bfloat16 [4096, 4096], P(('rep', 'fsdp'))
- block_grad: bfloat16 [224, 16, 128, 128], P('fsdp')
Inputs may be any that keep to these rules, and one draw needn't show every extreme that they name: `keep_mask`: every column panel keeps exactly 16 of its 32 blocks. `panel_owner`: non-decreasing over the panels; a shard owns at most 7 panels, some shard owns exactly 7, and some shard owns none.
All inputs are finite; a program needn't handle non-finite values.
Results may differ from a plain program's by a relative error of at most 0.005.
Values may be sent and summed in bfloat16 or wider, within the bound.
No kernel may reach another device: no remote copies, remote signals or barrier semaphores. Data moves between devices by JAX's collectives and lax.ppermute only.
A program may use at most 128 MiB of HBM per device.

v0:
```python
import math

import jax
import jax.numpy as jnp
from jax import lax
from jax.sharding import PartitionSpec as P


def per_device(tokens, upstream, blocks, keep_mask, panel_owner):
    shard_count = lax.axis_size("fsdp")
    own_index = lax.axis_index("fsdp")
    tok_dev = tokens.shape[0]
    model_width = tokens.shape[1]
    slot_count = blocks.shape[0]
    keep_count = blocks.shape[1]
    block_size = blocks.shape[3]
    row_blocks = keep_mask.shape[0]
    panel_count = panel_owner.shape[0]
    group_rows = tok_dev * shard_count
    shard_ids = jnp.arange(shard_count, dtype=jnp.int32)
    member = (panel_owner[:, None] == shard_ids[None, :]).astype(jnp.int32)
    counts = jnp.sum(member, axis=0)
    first_panel = jnp.cumsum(counts) - counts
    slot_ids = jnp.arange(slot_count, dtype=jnp.int32)
    panel_table = jnp.clip(first_panel[:, None] + slot_ids[None, :], 0, panel_count - 1)
    is_mine = shard_ids == own_index
    own_first = jnp.sum(jnp.where(is_mine, first_panel, 0))
    own_count = jnp.sum(jnp.where(is_mine, counts, 0))
    own_live = slot_ids < own_count
    own_panels = jnp.clip(own_first + slot_ids, 0, panel_count - 1)
    panel_ids = jnp.arange(panel_count, dtype=jnp.int32)
    panel_pick = (panel_ids[None, :] == own_panels[:, None]).astype(jnp.int32)
    running = jnp.cumsum(keep_mask, axis=0)
    own_running = jnp.sum(panel_pick[:, None, :] * running[None, :, :], axis=2)
    pick_ids = jnp.arange(keep_count, dtype=jnp.int32)
    own_rows = jnp.sum(
        (own_running[:, :, None] <= pick_ids[None, None, :]).astype(jnp.int32), axis=1
    )
    upstream_panels = jnp.transpose(upstream.reshape(tok_dev, panel_count, block_size), (1, 0, 2))
    outgoing = jnp.take(upstream_panels, panel_table.reshape(-1), axis=0)
    incoming = lax.all_to_all(outgoing, "fsdp", split_axis=0, concat_axis=1, tiled=True)
    group_tokens = lax.all_gather(tokens, "fsdp", axis=0, tiled=True)
    token_blocks = group_tokens.reshape(group_rows, row_blocks, block_size)

    def panel_step(nothing, panel_item):
        row_ids, weights, cotangent, is_live = panel_item
        chosen = jnp.take(token_blocks, row_ids, axis=1).reshape(
            group_rows, keep_count * block_size
        )
        flat_weights = weights.reshape(keep_count * block_size, block_size)
        preact = jnp.dot(chosen, flat_weights, preferred_element_type=jnp.float32)
        activation = jax.nn.silu(preact).astype(jnp.bfloat16)
        sigmoid_z = jax.nn.sigmoid(preact)
        slope = sigmoid_z * (1.0 + preact * (1.0 - sigmoid_z))
        dpre = jnp.where(is_live, cotangent.astype(jnp.float32) * slope, 0.0).astype(jnp.bfloat16)
        weight_grad = lax.dot_general(
            chosen, dpre, (((0,), (0,)), ((), ())), preferred_element_type=jnp.float32
        )
        return (
            nothing,
            (activation, weight_grad.reshape(keep_count, block_size, block_size), dpre),
        )

    panel_items = (own_rows, blocks, incoming, own_live)
    nothing, (activations, weight_grads, dpres) = lax.scan(
        panel_step, jnp.zeros((), jnp.float32), panel_items
    )
    dense_panels = jnp.zeros((slot_count, row_blocks, block_size, block_size), blocks.dtype)
    dense_panels = dense_panels.at[slot_ids[:, None], own_rows].set(blocks)
    backward = lax.dot_general(
        dpres, dense_panels, (((0, 2), (0, 3)), ((), ())), preferred_element_type=jnp.float32
    )
    input_grad = lax.psum_scatter(
        backward.reshape(dpres.shape[1], model_width), "fsdp", scatter_dimension=0, tiled=True
    ).astype(jnp.bfloat16)
    returned = lax.all_to_all(activations, "fsdp", split_axis=1, concat_axis=0, tiled=True)
    panel_first = jnp.sum(member * first_panel[None, :], axis=1)
    panel_slot = panel_owner * slot_count + panel_ids - panel_first
    act_panels = jnp.take(returned, panel_slot, axis=0)
    activation_out = jnp.transpose(act_panels, (1, 0, 2)).reshape(tok_dev, panel_count * block_size)
    scale = 1.0 / math.sqrt(group_rows * lax.axis_size("rep"))
    summed = lax.psum(weight_grads, "rep")
    block_grad = (summed * scale).astype(jnp.bfloat16)
    return (activation_out, input_grad, block_grad)


def solution(mesh):
    return jax.shard_map(
        per_device,
        mesh=mesh,
        in_specs=(
            P(("rep", "fsdp"), None),
            P(("rep", "fsdp"), None),
            P("fsdp", None, None, None),
            P(),
            P(),
        ),
        out_specs=(P(("rep", "fsdp"), None), P(("rep", "fsdp"), None), P("fsdp", None, None, None)),
        check_vma=False,
    )
```

profile of v0, /device:TPU:1, one launch (start us, length us, event | category | flops | bytes accessed | tf_op | source)
XLA Modules:
  0.0 1007.5 jit_solution(1712467014050605099)
XLA Ops:
  12.1 10.2 %all-to-all-start = ((bf16[224,16,128]{2,1,0:T(8,128)(2,1)}), bf16[224,16,128]{2,1,0:T(8,128)(2,1)S(1)}, u32[]{:S(2)}, u32[]{:S(2)}) async-start(bf16[224,16,128]{2,1,0:T(8,128)(2,1)} %broadcast_select_fusion.1), calls=%async_computation | async-start | bytes 1835008 | tf_op jit(solution)/shard_map/all_to_all | solution.py:41
  24.2 28.0 %all-to-all-done = bf16[224,16,128]{2,1,0:T(8,128)(2,1)S(1)} async-done(((bf16[224,16,128]{2,1,0:T(8,128)(2,1)}), bf16[224,16,128]{2,1,0:T(8,128)(2,1)S(1)}, u32[]{:S(2)}, u32[]{:S(2)}) %all-to-all-start) | async-done | bytes 917536 | tf_op jit(solution)/shard_map/all_to_all | solution.py:41
  52.3 33.2 %all-gather.2.cloned.1.call-done = bf16[512,4096]{1,0:T(8,128)(2,1)} async-done(((bf16[16,4096]{1,0:T(8,128)(2,1)}), bf16[512,4096]{1,0:T(8,128)(2,1)}) %all-gather.2.cloned.1.call-update) | async-done | bytes 4194320 | tf_op jit(solution)/shard_map/all_gather | solution.py:42
  85.5 6.5 copy.41
  92.1 6.4 copy.44
  98.5 146.6 %while.14 = (s32[]{:T(128)}, bf16[7,512,128]{2,1,0:T(8,128)(2,1)}, f32[7,16,128,128]{3,2,1,0:T(8,128)}, bf16[7,512,128]{2,1,0:T(8,128)(2,1)}, s32[7,16]{1,0:T(8,...) while((s32[]{:T(128)}, bf16[7,512,128]{2,1,0:T(8,128)(2,1)}, ...), condition=%wide.region_9.10_spmd, body=%wide.region_8.9_spmd.sunk | while | flops 540542080 | bytes 28847080 | solution.py:65
  98.5 3.1 gather_fusion
  103.3 3.9 copy.59
  108.9 3.7 bitcast_dynamic-update-slice_fusion.3
  119.4 3.1 gather_fusion
  124.2 3.9 copy.59
  129.8 3.7 bitcast_dynamic-update-slice_fusion.3
  140.5 3.1 gather_fusion
  145.2 3.9 copy.59
  150.8 3.7 bitcast_dynamic-update-slice_fusion.3
  166.1 3.9 copy.59
  171.7 3.7 bitcast_dynamic-update-slice_fusion.3
  187.0 3.9 copy.59
  192.6 3.7 bitcast_dynamic-update-slice_fusion.3
  208.0 3.9 copy.59
  213.6 3.7 bitcast_dynamic-update-slice_fusion.3
  229.0 3.9 copy.59
  234.6 3.7 bitcast_dynamic-update-slice_fusion.3
  245.3 4.8 broadcast_in_dim.89
  250.1 18.3 %scatter_fusion = bf16[7,32,128,128]{3,2,1,0:T(8,128)(2,1)} fusion(bf16[7,32,128,128]{3,2,1,0:T(8,128)(2,1)} %broadcast_in_dim.89, s32[112]{0:T(128)S(1)} %reshape.254, bf16[112,128,128]{2,1,0:T(8,128)(2,1)} %bitcast.126), kind=kCustom, calls=%fused_computation.3 | custom fusion | bytes 11010944 | tf_op jit(solution)/shard_map/scatter | solution.py:69
  268.5 10.0 fusion.6
  278.4 8.9 copy.50
  290.1 5.2 all-to-all-start.1
  295.5 261.8 %all-to-all-done.1 = bf16[7,512,128]{2,0,1:T(8,128)(2,1)S(1)} async-done(((bf16[7,512,128]{2,0,1:T(8,128)(2,1)}), bf16[7,512,128]{2,0,1:T(8,128)(2,1)S(1)}, u32[]{:S(2)}, u32[]{:S(2)}) %all-to-all-start.1) | async-done | bytes 917536 | tf_op jit(solution)/shard_map/all_to_all | solution.py:76
  559.1 288.4 %all-reduce.2.cloned.1.call-done = f32[7,16,128,128]{3,2,1,0:T(8,128)} async-done(((f32[7,16,128,128]{3,2,1,0:T(8,128)}), f32[7,16,128,128]{3,2,1,0:T(8,128)}) %all-reduce.2.cloned.1.call-update) | async-done | bytes 7340048 | tf_op jit(solution)/shard_map/psum | solution.py:82
  847.4 5.9 multiply_convert_fusion.1
  853.3 146.0 %reduce-scatter.2.cloned.1.call-done = f32[16,4096]{1,0:T(8,128)} async-done(((f32[512,4096]{1,0:T(8,128)}), f32[16,4096]{1,0:T(8,128)}) %reduce-scatter.2.cloned.1.call-update) | async-done | bytes 262160 | tf_op jit(solution)/shard_map/reduce_scatter | solution.py:73
  (126 shorter events, 96.8 us)
Async XLA Ops:
  7.2 2.8 copy-start
  7.2 15.2 %copy-start.3 = (s32[32,112]{1,0:T(8,128)S(1)}, s32[32,112]{1,0:T(8,128)}, u32[]{:S(2)}) copy-start(s32[32,112]{1,0:T(8,128)} %param.10) | copy-start | bytes 43012
  7.2 78.4 %all-gather.2.cloned.1.call-start = ((), (), s32[]{:S(2)}) async-start(), calls=%async_computation.3 | async-start | bytes 4325376 | tf_op jit(solution)/shard_map/all_gather | solution.py:42
  12.1 40.1 %all-to-all-start = ((bf16[224,16,128]{2,1,0:T(8,128)(2,1)}), bf16[224,16,128]{2,1,0:T(8,128)(2,1)S(1)}, u32[]{:S(2)}, u32[]{:S(2)}) async-start(bf16[224,16,128]{2,1,0:T(8,128)(2,1)} %broadcast_select_fusion.1), calls=%async_computation | async-start | bytes 1835008 | tf_op jit(solution)/shard_map/all_to_all | solution.py:41
  22.3 825.1 %all-reduce.2.cloned.1.call-start = ((), (), s32[]{:S(2)}) async-start(), calls=%async_computation.5 | async-start | bytes 14680064 | tf_op jit(solution)/shard_map/psum | solution.py:82
  245.2 754.2 %reduce-scatter.2.cloned.1.call-start = ((), (), s32[]{:S(2)}) async-start(), calls=%async_computation.4 | async-start | bytes 8650752 | tf_op jit(solution)/shard_map/reduce_scatter | solution.py:73
  250.1 18.3 %copy-start.5 = (bf16[7,512,128]{2,1,0:T(8,128)(2,1)S(1)}, bf16[7,512,128]{2,1,0:T(8,128)(2,1)}, u32[]{:S(2)}) copy-start(bf16[7,512,128]{2,1,0:T(8,128)(2,1)} %get-tuple-element.53) | copy-start | bytes 2752516
  287.4 1.2 copy-start.2
  287.4 7.9 copy-start.4
  290.1 267.1 %all-to-all-start.1 = ((bf16[7,512,128]{2,0,1:T(8,128)(2,1)}), bf16[7,512,128]{2,0,1:T(8,128)(2,1)S(1)}, u32[]{:S(2)}, u32[]{:S(2)}) async-start(bf16[7,512,128]{2,0,1:T(8,128)(2,1)} %copy.45), calls=%async_computation.1 | async-start | bytes 2097152 | tf_op jit(solution)/shard_map/all_to_all | solution.py:76
  558.1 442.9 %copy-start.1 = (bf16[16,14336]{1,0:T(8,128)(2,1)S(1)}, bf16[16,14336]{1,0:T(8,128)(2,1)}, u32[]{:S(2)}) copy-start(bf16[16,14336]{1,0:T(8,128)(2,1)} %param.8) | copy-start | bytes 1376260
Sparse Core Ops, SparseCore 0:
  9.9 75.6 all-gather.1
  245.3 602.1 all-reduce.1
  850.0 149.3 reduce-scatter.1
where the time goes:
time: 1010 us
  waiting for transfers between devices  758 us (75%)
  local copies, waits for them, and re-layouts  130 us (13%)
  matrix products  53 us (5%)
  other arithmetic  37 us (4%)
  starting transfers between devices  15.5 us (2%)
  between operations  14 us (1%)
    psum x1, waiting for transfers between devices, per_device(): summed = lax.psum(weight_grads, 'rep')  288 us
    all_to_all x1, waiting for transfers between devices, per_device(): lax.all_to_all(activations, 'fsdp', split_axis=1, concat_axis=0, tiled=True)  262 us
    reduce_scatter x1, waiting for transfers between devices, per_device(): lax.psum_scatter(backward.reshape(dpres.shape[1], model_width), 'fsdp', s...  146 us
    gather x14, local copies, waits for them, and re-layouts, panel_step(): jnp.take(token_blocks, row_ids, axis=1)  40 us
    all_gather x1, waiting for transfers between devices, per_device(): group_tokens = lax.all_gather(tokens, 'fsdp', axis=0, tiled=True)  33.2 us
    all_to_all x1, waiting for transfers between devices, per_device(): lax.all_to_all(outgoing, 'fsdp', split_axis=0, concat_axis=1, tiled=True)  28 us
    select_n x7, local copies, waits for them, and re-layouts, panel_step(): jnp.take(token_blocks, row_ids, axis=1)  27.5 us
    dot_general x7, matrix products, panel_step(): preact = jnp.dot(chosen, flat_weights, preferred_element_type=jnp.float32)  26 us
  transfers between devices with their start and end apart: 5, of which 5 were waited for; matrix products, arithmetic and copies ran while one was open for 6% of the time, Pallas kernels for 0%

commit v1 on v0

v1 whole, which is shorter than its diff:
```python
import functools
import math

import jax
import jax.numpy as jnp
from jax import lax
from jax.experimental import pallas as pl
from jax.experimental.pallas import tpu as pltpu
from jax.sharding import PartitionSpec as P

NZ, NY, NC = 4, 4, 2
NX, NH = 4, 2
GROUP = 16


def shift_zl(distance):
    return [
        ((z * NY + y) * NC + c, (((z + distance) % NZ) * NY + y) * NC + c)
        for z in range(NZ)
        for y in range(NY)
        for c in range(NC)
    ]


def shift_y(distance):
    return [
        ((z * NY + y) * NC + c, (z * NY + (y + distance) % NY) * NC + c)
        for z in range(NZ)
        for y in range(NY)
        for c in range(NC)
    ]


def swap_c():
    return [(k, k ^ 1) for k in range(NZ * NY * NC)]


def shift_x(distance):
    return [
        (x * NH + h, ((x + distance) % NX) * NH + h) for x in range(NX) for h in range(NH)
    ]


def swap_h():
    return [(r, r ^ 1) for r in range(NX * NH)]


def build_dense(rows_ref, blocks_ref, dense_ref):
    slots, keep, bs = blocks_ref.shape[0], blocks_ref.shape[1], blocks_ref.shape[2]
    dense_ref[...] = jnp.zeros_like(dense_ref)
    for p in range(slots):
        for j in range(keep):
            at = pl.multiple_of(rows_ref[p * keep + j] * bs, bs)
            dense_ref[pl.ds(at, bs), p * bs : (p + 1) * bs] = blocks_ref[p, j]


def forward_kernel(
    rows_ref,
    rank_ref,
    live_ref,
    source_ref,
    own_ref,
    sib_ref,
    blocks_ref,
    ups_ref,
    act_ref,
    dz_ref,
    *rest,
):
    chunk_refs = rest[:NX]
    dense_ref, grads_ref, sems = rest[NX:]
    slots, keep, bs = blocks_ref.shape[0], blocks_ref.shape[1], blocks_ref.shape[2]
    half = own_ref.shape[0]
    row_blocks = own_ref.shape[1] // bs
    tile = 128
    build_dense(rows_ref, blocks_ref, dense_ref)

    for which, tok_ref in enumerate((own_ref, sib_ref)):

        def step(t, carry, which=which, tok_ref=tok_ref):
            row = pl.multiple_of(t * tile, tile)
            z = jnp.dot(
                tok_ref[pl.ds(row, tile), :], dense_ref[...], preferred_element_type=jnp.float32
            )
            sig = jax.nn.sigmoid(z)
            act = (z * sig).astype(jnp.bfloat16)
            slope = sig * (1.0 + z * (1.0 - sig))
            for g in range(tile // GROUP):
                src = source_ref[which * (half // GROUP) + t * (tile // GROUP) + g]
                lo = g * GROUP
                for p in range(slots):
                    cols = slice(p * bs, (p + 1) * bs)
                    act_ref[src, p] = act[lo : lo + GROUP, cols]
                    up = ups_ref[src, p].astype(jnp.float32) * slope[lo : lo + GROUP, cols]
                    up = jnp.where(live_ref[p] == 1, up, 0.0)
                    dz_ref[pl.ds(which * half + row + lo, GROUP), cols] = up.astype(jnp.bfloat16)
            return carry

        lax.fori_loop(0, half // tile, step, 0)

    chunk = slots * keep // NX

    def grad_step(r, carry):
        at = pl.multiple_of(r * bs, bs)
        left = jnp.concatenate([own_ref[:, pl.ds(at, bs)], sib_ref[:, pl.ds(at, bs)]], axis=0)
        grad = lax.dot_general(
            left, dz_ref[...], (((0,), (0,)), ((), ())), preferred_element_type=jnp.float32
        ).astype(jnp.bfloat16)
        for p in range(slots):
            rank = rank_ref[p * row_blocks + r]

            @pl.when(rank >= 0)
            def _(p=p, rank=rank):
                grads_ref[rank] = grad[:, p * bs : (p + 1) * bs]

        return carry

    lax.fori_loop(0, row_blocks, grad_step, 0)
    copies = [
        pltpu.make_async_copy(
            grads_ref.at[pl.ds(d * chunk, chunk)], chunk_refs[d], sems.at[d]
        )
        for d in range(NX)
    ]
    for copy in copies:
        copy.start()
    for copy in copies:
        copy.wait()


def backward_kernel(rows_ref, blocks_ref, dz_ref, own_ref, sib_ref, dense_ref):
    half = own_ref.shape[0]
    tile = 128
    build_dense(rows_ref, blocks_ref, dense_ref)
    for which, out_ref in enumerate((own_ref, sib_ref)):

        def step(t, carry, which=which, out_ref=out_ref):
            row = pl.multiple_of(t * tile, tile)
            grad = lax.dot_general(
                dz_ref[pl.ds(which * half + row, tile), :],
                dense_ref[...],
                (((1,), (1,)), ((), ())),
                preferred_element_type=jnp.float32,
            )
            out_ref[pl.ds(row, tile), :] = grad.astype(jnp.bfloat16)
            return carry

        lax.fori_loop(0, half // tile, step, 0)


def whole():
    return pl.BlockSpec(memory_space=pltpu.VMEM)


def scalars():
    return pl.BlockSpec(memory_space=pltpu.SMEM)


def per_device(tokens, upstream, blocks, keep_mask, panel_owner):
    shard_count = lax.axis_size("fsdp")
    own_index = lax.axis_index("fsdp")
    x_index = lax.axis_index("rep") // NH
    tok_dev, model_width = tokens.shape
    slot_count, keep_count, block_size = blocks.shape[0], blocks.shape[1], blocks.shape[3]
    row_blocks = keep_mask.shape[0]
    panel_count = panel_owner.shape[0]
    half = tok_dev * NZ * NY
    f32, bf16 = jnp.float32, jnp.bfloat16

    shard_ids = jnp.arange(shard_count, dtype=jnp.int32)
    member = (panel_owner[:, None] == shard_ids[None, :]).astype(jnp.int32)
    counts = jnp.sum(member, axis=0)
    first_panel = jnp.cumsum(counts) - counts
    slot_ids = jnp.arange(slot_count, dtype=jnp.int32)
    panel_table = jnp.clip(first_panel[:, None] + slot_ids[None, :], 0, panel_count - 1)
    is_mine = shard_ids == own_index
    own_first = jnp.sum(jnp.where(is_mine, first_panel, 0))
    own_count = jnp.sum(jnp.where(is_mine, counts, 0))
    own_live = (slot_ids < own_count).astype(jnp.int32)
    own_panels = jnp.clip(own_first + slot_ids, 0, panel_count - 1)
    panel_ids = jnp.arange(panel_count, dtype=jnp.int32)
    panel_pick = (panel_ids[None, :] == own_panels[:, None]).astype(jnp.int32)
    running = jnp.cumsum(keep_mask, axis=0)
    own_running = jnp.sum(panel_pick[:, None, :] * running[None, :, :], axis=2)
    own_keep = jnp.sum(panel_pick[:, None, :] * keep_mask[None, :, :], axis=2)
    pick_ids = jnp.arange(keep_count, dtype=jnp.int32)
    own_rows = jnp.sum(
        (own_running[:, :, None] <= pick_ids[None, None, :]).astype(jnp.int32), axis=1
    )
    chunk = slot_count * keep_count // NX
    flat = slot_ids[:, None] * keep_count + own_running - 1
    place = ((flat // chunk - x_index) % NX) * chunk + flat % chunk
    rank = jnp.where(own_keep == 1, place, -1).astype(jnp.int32)
    my_z, my_y, my_c = own_index // (NY * NC), (own_index // NC) % NY, own_index % NC
    away_c = jnp.arange(2, dtype=jnp.int32)[:, None, None]
    away_y = jnp.arange(NY, dtype=jnp.int32)[None, :, None]
    away_z = jnp.arange(NZ, dtype=jnp.int32)[None, None, :]
    source = (((my_z - away_z) % NZ) * NY + (my_y - away_y) % NY) * NC + (my_c + away_c) % NC
    source = source.reshape(-1).astype(jnp.int32)

    along_z = [tokens] + [lax.ppermute(tokens, "fsdp", shift_zl(d)) for d in range(1, NZ)]
    line = jnp.concatenate(along_z, axis=0)
    along_y = [line] + [lax.ppermute(line, "fsdp", shift_y(d)) for d in range(1, NY)]
    tok_own = jnp.concatenate(along_y, axis=0)
    tok_sib = lax.ppermute(tok_own, "fsdp", swap_c())

    upstream_panels = jnp.transpose(upstream.reshape(tok_dev, panel_count, block_size), (1, 0, 2))
    outgoing = jnp.take(upstream_panels, panel_table.reshape(-1), axis=0)
    outgoing = outgoing.reshape(shard_count, slot_count, tok_dev, block_size)
    incoming = lax.all_to_all(outgoing, "fsdp", split_axis=0, concat_axis=0, tiled=True)

    wide = slot_count * block_size
    flops = 2 * 2 * half * model_width * wide
    outs = pl.pallas_call(
        forward_kernel,
        out_shape=(
            jax.ShapeDtypeStruct(incoming.shape, bf16),
            jax.ShapeDtypeStruct((2 * half, wide), bf16),
        )
        + tuple(
            jax.ShapeDtypeStruct((chunk, block_size, block_size), bf16) for _ in range(NX)
        ),
        in_specs=[scalars()] * 4 + [whole()] * 4,
        out_specs=(whole(), whole()) + (pl.BlockSpec(memory_space=pl.ANY),) * NX,
        scratch_shapes=[
            pltpu.VMEM((model_width, wide), bf16),
            pltpu.VMEM((NX * chunk, block_size, block_size), bf16),
            pltpu.SemaphoreType.DMA((NX,)),
        ],
        compiler_params=pltpu.CompilerParams(vmem_limit_bytes=52 * 2**20),
        cost_estimate=pl.CostEstimate(
            flops=2 * flops, bytes_accessed=20 * 2**20, transcendentals=0
        ),
        name="forward_and_weight_grad",
    )(
        own_rows.reshape(-1).astype(jnp.int32),
        rank.reshape(-1),
        own_live,
        source,
        tok_own,
        tok_sib,
        blocks,
        incoming,
    )
    acts, dz, pieces = outs[0], outs[1], outs[2:]

    got = [lax.ppermute(pieces[d], "rep", shift_x(d)) for d in range(1, NX)]

    returned = lax.all_to_all(acts, "fsdp", split_axis=0, concat_axis=0, tiled=True)
    panel_first = jnp.sum(member * first_panel[None, :], axis=1)
    panel_slot = panel_owner * slot_count + panel_ids - panel_first
    act_panels = jnp.take(
        returned.reshape(shard_count * slot_count, tok_dev, block_size), panel_slot, axis=0
    )
    activation_out = jnp.transpose(act_panels, (1, 0, 2)).reshape(tok_dev, panel_count * block_size)

    grad_own, grad_sib = pl.pallas_call(
        backward_kernel,
        out_shape=(jax.ShapeDtypeStruct((half, model_width), bf16),) * 2,
        in_specs=[scalars()] + [whole()] * 2,
        out_specs=(whole(), whole()),
        scratch_shapes=[pltpu.VMEM((model_width, wide), bf16)],
        compiler_params=pltpu.CompilerParams(vmem_limit_bytes=40 * 2**20),
        cost_estimate=pl.CostEstimate(flops=flops, bytes_accessed=10 * 2**20, transcendentals=0),
        name="input_grad",
    )(own_rows.reshape(-1).astype(jnp.int32), blocks, dz)

    from_sib = lax.ppermute(grad_sib, "fsdp", swap_c())
    pair = (grad_own.astype(f32) + from_sib.astype(f32)).astype(bf16)
    pair = pair.reshape(NY, NZ * tok_dev, model_width)
    parts = [lax.ppermute(pair[d], "fsdp", shift_y(-d)) for d in range(1, NY)]
    total = pair[0].astype(f32)
    for part in parts:
        total = total + part.astype(f32)
    total = total.astype(bf16).reshape(NZ, tok_dev, model_width)
    parts = [lax.ppermute(total[d], "fsdp", shift_zl(-d)) for d in range(1, NZ)]
    input_grad = total[0].astype(f32)
    for part in parts:
        input_grad = input_grad + part.astype(f32)
    input_grad = input_grad.astype(bf16)

    along_x = pieces[0].astype(f32)
    for part in got:
        along_x = along_x + part.astype(f32)
    along_x = along_x.astype(bf16)
    other = lax.ppermute(along_x, "rep", swap_h())
    scale = 1.0 / math.sqrt(2 * half * lax.axis_size("rep"))
    mine = ((along_x.astype(f32) + other.astype(f32)) * scale).astype(bf16)
    block_grad = lax.all_gather(
        mine,
        "rep",
        axis=0,
        tiled=True,
        axis_index_groups=[[x * NH + h for x in range(NX)] for h in range(NH)],
    )
    return (activation_out, input_grad, block_grad.reshape(blocks.shape))


def solution(mesh):
    return jax.shard_map(
        per_device,
        mesh=mesh,
        in_specs=(
            P(("rep", "fsdp"), None),
            P(("rep", "fsdp"), None),
            P("fsdp", None, None, None),
            P(),
            P(),
        ),
        out_specs=(P(("rep", "fsdp"), None), P(("rep", "fsdp"), None), P("fsdp", None, None, None)),
        check_vma=False,
    )
```

time: 1010 us -> 262 us (0.26)
  waiting for transfers between devices: 758 us -> 116 us
  local copies, waits for them, and re-layouts: 130 us -> 16.5 us
  matrix products: 53 us -> 0 us
  starting transfers between devices: 15.5 us -> 60.3 us
  Pallas kernels: 0 us -> 38.4 us
  other arithmetic: 37 us -> 15.8 us
    all_to_all x2, waiting for transfers between devices: 290 us -> 0.01 us  [the longest x1 0.01 us: per_device(): lax.all_to_all(outgoing, 'fsdp', split_axis=0, concat_axis=0, tiled=True)]
    psum x1 -> x0, waiting for transfers between devices: 288 us -> none  [per_device(): summed = lax.psum(weight_grads, 'rep')]
    reduce_scatter x1 -> x0, waiting for transfers between devices: 146 us -> none  [per_device(): lax.psum_scatter(backward.reshape(dpres.shape[1], model_width), 'fsdp', s...]
    ppermute x0 -> x18, waiting for transfers between devices: none -> 81.6 us  [the longest x3 34.1 us: per_device(): got = [lax.ppermute(pieces[d], 'rep', shift_x(d)) for d in range(1, NX)]]
    dot_general x15 -> x0, matrix products: 53 us -> none  [the longest x7 26 us: panel_step(): preact = jnp.dot(chosen, flat_weights, preferred_element_type=jnp.float32)]
    ppermute x0 -> x18, starting transfers between devices: none -> 44.5 us  [the longest x3 16.2 us: per_device(): parts = [lax.ppermute(total[d], 'fsdp', shift_zl(-d)) for d in range(1, NZ)]]
    gather x15 -> x1, local copies, waits for them, and re-layouts: 40.7 us -> 1.87 us  [per_device(): jnp.take(returned.reshape(shard_count * slot_count, tok_dev, block_size),...]
    pallas_call x0 -> x2, Pallas kernels: none -> 38.4 us  [the longest x1 25.6 us: per_device(): pl.pallas_call(forward_kernel, out_shape=(jax.ShapeDtypeStruct(incoming.s...]
  transfers between devices with their start and end apart: 5 -> 21, of which waited for: 5 -> 10; matrix products, arithmetic and copies ran while one was open for 6% -> 10% of each run, Pallas kernels for 0% -> 0%
where the time goes in v1:
time: 262 us; the launch traced here: 261 us
  waiting for transfers between devices  116 us (44%)
  starting transfers between devices  60.3 us (23%)
  Pallas kernels  38.4 us (15%)
  local copies, waits for them, and re-layouts  16.5 us (6%)
  other arithmetic  15.8 us (6%)
  between operations  14.3 us (5%)
    all_gather x1, waiting for transfers between devices, per_device(): lax.all_gather(mine, 'rep', axis=0, tiled=True, axis_index_groups=[[x * N...  34.1 us
    ppermute x3, waiting for transfers between devices, per_device(): got = [lax.ppermute(pieces[d], 'rep', shift_x(d)) for d in range(1, NX)]  34.1 us
    pallas_call x1, Pallas kernels, per_device(): pl.pallas_call(forward_kernel, out_shape=(jax.ShapeDtypeStruct(incoming.s...  25.6 us
    ppermute x3, waiting for transfers between devices, per_device(): lax.ppermute(line, 'fsdp', shift_y(d))  19.3 us
    ppermute x3, starting transfers between devices, per_device(): parts = [lax.ppermute(total[d], 'fsdp', shift_zl(-d)) for d in range(1, NZ)]  16.2 us
    pallas_call x1, Pallas kernels, per_device(): pl.pallas_call(backward_kernel, out_shape=(jax.ShapeDtypeStruct((half, mo...  12.8 us
    ppermute x1, waiting for transfers between devices, per_device(): other = lax.ppermute(along_x, 'rep', swap_h())  11.9 us
    unnamed x18, local copies, waits for them, and re-layouts  10.3 us
  transfers between devices with their start and end apart: 21, of which 10 were waited for; matrix products, arithmetic and copies ran while one was open for 10% of the time, Pallas kernels for 0%

profile of v1, /device:TPU:1, one launch (start us, length us, event | category | flops | bytes accessed | tf_op | source)
XLA Modules:
  0.0 261.1 jit_solution(9589759673015390600)
XLA Ops:
  7.2 2.5 collective-permute-start
  9.7 3.0 %collective-permute-start.1 = (bf16[16,4096]{1,0:T(8,128)(2,1)}, bf16[16,4096]{1,0:T(8,128)(2,1)S(1)}, u32[]{:S(2)}, u32[]{:S(2)}) collective-permute-start(bf16[16,4096]{1,0:T(8,128)(2,1)} %param.5), channel_id=1, source_target_pairs={{0,16},{1,17},{2,18},{3,19},{4,20},{5,21},{6,22},{7,23},{8,24},{9,... | collective-permute-start | bytes 393224 | tf_op jit(solution)/shard_map/ppermute | solution.py:201
  13.4 1.6 constant_dynamic-update-slice_fusion.3
  17.7 4.6 %collective-permute-done.1 = bf16[16,4096]{1,0:T(8,128)(2,1)S(1)} collective-permute-done((bf16[16,4096]{1,0:T(8,128)(2,1)}, bf16[16,4096]{1,0:T(8,128)(2,1)S(1)}, u32[]{:S(2)}, u32[]{:S(2)}) %collective-permute-start.1) | collective-permute-done | bytes 131104 | tf_op jit(solution)/shard_map/ppermute | solution.py:201
  25.8 2.7 %collective-permute-start.4 = (bf16[64,4096]{1,0:T(8,128)(2,1)S(1)}, bf16[64,4096]{1,0:T(8,128)(2,1)S(1)}, u32[]{:S(2)}, u32[]{:S(2)}) collective-permute-start(bf16[64,4096]{1,0:T(8,128)(2,1)S(1)} %get-tuple-element.31), channel_id=1, source_target_pairs={{0,4},{1,5},{2,6},{3,7},{4,0},{5,1},{6,2},{7,3},{8,12},{9,13},{10,... | collective-permute-start | bytes 1572872 | tf_op jit(solution)/shard_map/ppermute | solution.py:203
  29.7 7.4 %all-to-all-start = ((bf16[32,7,16,128]{3,2,1,0:T(8,128)(2,1)}), bf16[32,7,16,128]{3,2,1,0:T(8,128)(2,1)S(1)}, u32[]{:S(2)}, u32[]{:S(2)}) async-start(bf16[32,7,16,128]{3,2,1,0:T(8,128)(2,1)} %broadcast_select_fusion), calls=%async_computation | async-start | bytes 1835008 | tf_op jit(solution)/shard_map/all_to_all | solution.py:210
  37.2 2.7 %collective-permute-start.5 = (bf16[64,4096]{1,0:T(8,128)(2,1)S(1)}, bf16[64,4096]{1,0:T(8,128)(2,1)S(1)}, u32[]{:S(2)}, u32[]{:S(2)}) collective-permute-start(bf16[64,4096]{1,0:T(8,128)(2,1)S(1)} %get-tuple-element.31), channel_id=1, source_target_pairs={{0,6},{1,7},{2,0},{3,1},{4,2},{5,3},{6,4},{7,5},{8,14},{9,15},{10,... | collective-permute-start | bytes 1572872 | tf_op jit(solution)/shard_map/ppermute | solution.py:203
  40.7 15.9 %collective-permute-done.4 = bf16[64,4096]{1,0:T(8,128)(2,1)S(1)} collective-permute-done((bf16[64,4096]{1,0:T(8,128)(2,1)S(1)}, bf16[64,4096]{1,0:T(8,128)(2,1)S(1)}, u32[]{:S(2)}, u32[]{:S(2)}) %collective-permute-start.4) | collective-permute-done | bytes 524320 | tf_op jit(solution)/shard_map/ppermute | solution.py:203
  57.4 3.4 %collective-permute-done.5 = bf16[64,4096]{1,0:T(8,128)(2,1)S(1)} collective-permute-done((bf16[64,4096]{1,0:T(8,128)(2,1)S(1)}, bf16[64,4096]{1,0:T(8,128)(2,1)S(1)}, u32[]{:S(2)}, u32[]{:S(2)}) %collective-permute-start.5) | collective-permute-done | bytes 524320 | tf_op jit(solution)/shard_map/ppermute | solution.py:203
  66.8 25.6 %forward_and_weight_grad.1 = (bf16[32,7,16,128]{3,2,1,0:T(8,128)(2,1)}, bf16[512,896]{1,0:T(8,128)(2,1)S(1)}, bf16[28,128,128]{2,1,0:T(8,128)(2,1)}, bf16[28,128...) custom-call(s32[112]{0:T(128)S(1)} %reshape.278.rows_ref, ...), custom_call_target="tpu_custom_call" | custom-call | flops 7516192768 | bytes 20971520 | tf_op jit(solution)/shard_map/forward_and_weight_grad/pallas_call | solution.py:214
  92.5 12.8 %input_grad.1 = (bf16[256,4096]{1,0:T(8,128)(2,1)S(1)}, bf16[256,4096]{1,0:T(8,128)(2,1)}) custom-call(s32[112]{0:T(128)S(1)} %reshape.278.rows_ref, bf16[7,16,128,128]{3,2,1,0:T(8,128)(2,1)S(1)} %copy-done.1, bf16[512,896]{1,0:T(8,128)(2,1)S(1)} %get-tuple-element.12.dz_ref), custom_call_target="tpu_custom_call" | custom-call | flops 3758096384 | bytes 10485760 | tf_op jit(solution)/shard_map/input_grad/pallas_call | solution.py:257
  105.6 2.5 collective-permute-start.16
  109.3 8.2 %all-to-all-start.1 = ((bf16[32,7,16,128]{3,2,1,0:T(8,128)(2,1)}), bf16[32,7,16,128]{3,2,1,0:T(8,128)(2,1)}, u32[]{:S(2)}, u32[]{:S(2)}) async-start(bf16[32,7,16,128]{3,2,1,0:T(8,128)(2,1)} %get-tuple-element.11), calls=%async_computation.1 | async-start | bytes 1835008 | tf_op jit(solution)/shard_map/all_to_all | solution.py:249
  117.7 29.7 %collective-permute-done.16 = bf16[28,128,128]{2,1,0:T(8,128)(2,1)} collective-permute-done((bf16[28,128,128]{2,1,0:T(8,128)(2,1)}, bf16[28,128,128]{2,1,0:T(8,128)(2,1)}, u32[]{:S(2)}, u32[]{:S(2)}) %collective-permute-start.16) | collective-permute-done | bytes 917536 | tf_op jit(solution)/shard_map/ppermute | solution.py:247
  147.4 4.4 %collective-permute-done.14 = bf16[28,128,128]{2,1,0:T(8,128)(2,1)} collective-permute-done((bf16[28,128,128]{2,1,0:T(8,128)(2,1)}, bf16[28,128,128]{2,1,0:T(8,128)(2,1)}, u32[]{:S(2)}, u32[]{:S(2)}) %collective-permute-start.14) | collective-permute-done | bytes 917536 | tf_op jit(solution)/shard_map/ppermute | solution.py:247
  151.8 2.6 add_convert_fusion.1
  154.4 5.6 %collective-permute-start.17 = (bf16[28,128,128]{2,1,0:T(8,128)(2,1)S(1)}, bf16[28,128,128]{2,1,0:T(8,128)(2,1)}, u32[]{:S(2)}, u32[]{:S(2)}) collective-permute-start(bf16[28,128,128]{2,1,0:T(8,128)(2,1)S(1)} %add_convert_fusion.1), channel_id=1, source_target_pairs={{0,32},{32,0},{64,96},{96,64},{128,160},{160,128},{192,224},{224,1... | collective-permute-start | bytes 2752520 | tf_op jit(solution)/shard_map/ppermute | solution.py:286
  160.0 2.4 add_convert_fusion
  162.4 1.3 copy-done.2
  164.9 2.2 collective-permute-start.10
  167.1 1.3 collective-permute-start.9
  168.4 1.4 collective-permute-start.8
  169.8 1.9 gather_fusion.1
  171.7 11.9 %collective-permute-done.17 = bf16[28,128,128]{2,1,0:T(8,128)(2,1)} collective-permute-done((bf16[28,128,128]{2,1,0:T(8,128)(2,1)S(1)}, bf16[28,128,128]{2,1,0:T(8,128)(2,1)}, u32[]{:S(2)}, u32[]{:S(2)}) %collective-permute-start.17) | collective-permute-done | bytes 917536 | tf_op jit(solution)/shard_map/ppermute | solution.py:286
  183.6 2.5 multiply_convert_fusion
  186.1 5.0 %collective-permute-done.9 = bf16[64,4096]{1,0:T(8,128)(2,1)S(1)} collective-permute-done((bf16[64,4096]{1,0:T(8,128)(2,1)}, bf16[64,4096]{1,0:T(8,128)(2,1)S(1)}, u32[]{:S(2)}, u32[]{:S(2)}) %collective-permute-start.9) | collective-permute-done | bytes 524320 | tf_op jit(solution)/shard_map/ppermute | solution.py:271
  191.1 1.3 add_convert_fusion.2
  192.4 14.0 %collective-permute-start.13 = (bf16[16,4096]{1,0:T(8,128)(2,1)S(1)}, bf16[16,4096]{1,0:T(8,128)(2,1)S(1)}, u32[]{:S(2)}, u32[]{:S(2)}) collective-permute-start(bf16[16,4096]{1,0:T(8,128)(2,1)S(1)} %get-tuple-element.29), channel_id=1, source_target_pairs={{0,8},{1,9},{2,10},{3,11},{4,12},{5,13},{6,14},{7,15},{8,16},{9,17... | collective-permute-start | bytes 393224 | tf_op jit(solution)/shard_map/ppermute | solution.py:276
  206.5 2.2 collective-permute-start.11
  209.6 5.4 %collective-permute-done.12 = bf16[16,4096]{1,0:T(8,128)(2,1)S(1)} collective-permute-done((bf16[16,4096]{1,0:T(8,128)(2,1)S(1)}, bf16[16,4096]{1,0:T(8,128)(2,1)S(1)}, u32[]{:S(2)}, u32[]{:S(2)}) %collective-permute-start.12) | collective-permute-done | bytes 131104 | tf_op jit(solution)/shard_map/ppermute | solution.py:276
  215.7 34.1 %all-gather.2.cloned.1.call-done = bf16[112,128,128]{2,1,0:T(8,128)(2,1)} async-done(((bf16[28,128,128]{2,1,0:T(8,128)(2,1)}), bf16[112,128,128]{2,1,0:T(8,128)(2,1)}) %all-gather.2.cloned.1.call-update) | async-done | bytes 3670032 | tf_op jit(solution)/shard_map/all_gather | solution.py:289
  249.8 4.4 %copy.35 = bf16[7,16,128,128]{3,2,1,0:T(8,128)(2,1)} copy(bf16[7,16,128,128]{3,2,1,0:T(8,128)(2,1)} %bitcast.18) | data formatting | bytes 7340032
  (78 shorter events, 20.5 us)
Async XLA Ops:
  7.2 8.9 %copy-start = (bf16[16,14336]{1,0:T(8,128)(2,1)S(1)}, bf16[16,14336]{1,0:T(8,128)(2,1)}, u32[]{:S(2)}) copy-start(bf16[16,14336]{1,0:T(8,128)(2,1)} %param.6) | copy-start | bytes 1376260
  7.2 9.8 %collective-permute-start = (bf16[16,4096]{1,0:T(8,128)(2,1)}, bf16[16,4096]{1,0:T(8,128)(2,1)S(1)}, u32[]{:S(2)}, u32[]{:S(2)}) collective-permute-start(bf16[16,4096]{1,0:T(8,128)(2,1)} %param.5), channel_id=1, source_target_pairs={{0,8},{1,9},{2,10},{3,11},{4,12},{5,13},{6,14},{7,15},{8,16},{9,17... | collective-permute-start | bytes 393224 | tf_op jit(solution)/shard_map/ppermute | solution.py:201
  9.7 12.5 %collective-permute-start.1 = (bf16[16,4096]{1,0:T(8,128)(2,1)}, bf16[16,4096]{1,0:T(8,128)(2,1)S(1)}, u32[]{:S(2)}, u32[]{:S(2)}) collective-permute-start(bf16[16,4096]{1,0:T(8,128)(2,1)} %param.5), channel_id=1, source_target_pairs={{0,16},{1,17},{2,18},{3,19},{4,20},{5,21},{6,22},{7,23},{8,24},{9,... | collective-permute-start | bytes 393224 | tf_op jit(solution)/shard_map/ppermute | solution.py:201
  12.7 10.2 %collective-permute-start.2 = (bf16[16,4096]{1,0:T(8,128)(2,1)}, bf16[16,4096]{1,0:T(8,128)(2,1)S(1)}, u32[]{:S(2)}, u32[]{:S(2)}) collective-permute-start(bf16[16,4096]{1,0:T(8,128)(2,1)} %param.5), channel_id=1, source_target_pairs={{0,24},{1,25},{2,26},{3,27},{4,28},{5,29},{6,30},{7,31},{8,0},{9,1... | collective-permute-start | bytes 393224 | tf_op jit(solution)/shard_map/ppermute | solution.py:201
  23.6 16.3 %collective-permute-start.3 = (bf16[64,4096]{1,0:T(8,128)(2,1)S(1)}, bf16[64,4096]{1,0:T(8,128)(2,1)S(1)}, u32[]{:S(2)}, u32[]{:S(2)}) collective-permute-start(bf16[64,4096]{1,0:T(8,128)(2,1)S(1)} %get-tuple-element.31), channel_id=1, source_target_pairs={{0,2},{1,3},{2,4},{3,5},{4,6},{5,7},{6,0},{7,1},{8,10},{9,11},{10,... | collective-permute-start | bytes 1572872 | tf_op jit(solution)/shard_map/ppermute | solution.py:203
  25.7 11.5 %copy-start.4 = (s32[32,112]{1,0:T(8,128)S(1)}, s32[32,112]{1,0:T(8,128)}, u32[]{:S(2)}) copy-start(s32[32,112]{1,0:T(8,128)} %param.8) | copy-start | bytes 43012
  25.8 30.8 %collective-permute-start.4 = (bf16[64,4096]{1,0:T(8,128)(2,1)S(1)}, bf16[64,4096]{1,0:T(8,128)(2,1)S(1)}, u32[]{:S(2)}, u32[]{:S(2)}) collective-permute-start(bf16[64,4096]{1,0:T(8,128)(2,1)S(1)} %get-tuple-element.31), channel_id=1, source_target_pairs={{0,4},{1,5},{2,6},{3,7},{4,0},{5,1},{6,2},{7,3},{8,12},{9,13},{10,... | collective-permute-start | bytes 1572872 | tf_op jit(solution)/shard_map/ppermute | solution.py:203
  29.7 35.8 %all-to-all-start = ((bf16[32,7,16,128]{3,2,1,0:T(8,128)(2,1)}), bf16[32,7,16,128]{3,2,1,0:T(8,128)(2,1)S(1)}, u32[]{:S(2)}, u32[]{:S(2)}) async-start(bf16[32,7,16,128]{3,2,1,0:T(8,128)(2,1)} %broadcast_select_fusion), calls=%async_computation | async-start | bytes 1835008 | tf_op jit(solution)/shard_map/all_to_all | solution.py:210
  37.2 23.6 %collective-permute-start.5 = (bf16[64,4096]{1,0:T(8,128)(2,1)S(1)}, bf16[64,4096]{1,0:T(8,128)(2,1)S(1)}, u32[]{:S(2)}, u32[]{:S(2)}) collective-permute-start(bf16[64,4096]{1,0:T(8,128)(2,1)S(1)} %get-tuple-element.31), channel_id=1, source_target_pairs={{0,6},{1,7},{2,0},{3,1},{4,2},{5,3},{6,4},{7,5},{8,14},{9,15},{10,... | collective-permute-start | bytes 1572872 | tf_op jit(solution)/shard_map/ppermute | solution.py:203
  61.7 5.2 %collective-permute-start.6 = (bf16[256,4096]{1,0:T(8,128)(2,1)}, bf16[256,4096]{1,0:T(8,128)(2,1)}, u32[]{:S(2)}, u32[]{:S(2)}) collective-permute-start(bf16[256,4096]{1,0:T(8,128)(2,1)} %constant_dynamic-update-slice_fusion.4.own_ref), channel_id=1, source_target_pairs={{0,1},{1,0},{2,3},{3,2},{4,5},{5,4},{6,7},{7,6},{8,9},{9,8},{10,11... | collective-permute-start | bytes 6291464 | tf_op jit(solution)/shard_map/ppermute | solution.py:205
  65.5 1.3 copy-start.3
  65.5 26.9 %copy-start.1 = (bf16[7,16,128,128]{3,2,1,0:T(8,128)(2,1)S(1)}, bf16[7,16,128,128]{3,2,1,0:T(8,128)(2,1)}, u32[]{:S(2)}) copy-start(bf16[7,16,128,128]{3,2,1,0:T(8,128)(2,1)} %blocks_ref.3) | copy-start | bytes 11010052
  92.5 16.7 %copy-start.5 = (s32[112]{0:T(128)S(1)}, s32[112]{0:T(128)}, u32[]{:S(2)}) copy-start(s32[112]{0:T(128)} %param.9) | copy-start | bytes 1348
  105.3 54.7 %collective-permute-start.7 = (bf16[256,4096]{1,0:T(8,128)(2,1)}, bf16[256,4096]{1,0:T(8,128)(2,1)}, u32[]{:S(2)}, u32[]{:S(2)}) collective-permute-start(bf16[256,4096]{1,0:T(8,128)(2,1)} %get-tuple-element.14), channel_id=1, source_target_pairs={{0,1},{1,0},{2,3},{3,2},{4,5},{5,4},{6,7},{7,6},{8,9},{9,8},{10,11... | collective-permute-start | bytes 6291464 | tf_op jit(solution)/shard_map/ppermute | solution.py:268
  105.6 41.8 %collective-permute-start.16 = (bf16[28,128,128]{2,1,0:T(8,128)(2,1)}, bf16[28,128,128]{2,1,0:T(8,128)(2,1)}, u32[]{:S(2)}, u32[]{:S(2)}) collective-permute-start(bf16[28,128,128]{2,1,0:T(8,128)(2,1)} %get-tuple-element.18), channel_id=1, source_target_pairs={{0,192},{32,224},{64,0},{96,32},{128,64},{160,96},{192,128},{224,1... | collective-permute-start | bytes 2752520 | tf_op jit(solution)/shard_map/ppermute | solution.py:247
  108.1 39.3 %collective-permute-start.15 = (bf16[28,128,128]{2,1,0:T(8,128)(2,1)}, bf16[28,128,128]{2,1,0:T(8,128)(2,1)}, u32[]{:S(2)}, u32[]{:S(2)}) collective-permute-start(bf16[28,128,128]{2,1,0:T(8,128)(2,1)} %get-tuple-element.17), channel_id=1, source_target_pairs={{0,128},{32,160},{64,192},{96,224},{128,0},{160,32},{192,64},{224,... | collective-permute-start | bytes 2752520 | tf_op jit(solution)/shard_map/ppermute | solution.py:247
  108.6 43.2 %collective-permute-start.14 = (bf16[28,128,128]{2,1,0:T(8,128)(2,1)}, bf16[28,128,128]{2,1,0:T(8,128)(2,1)}, u32[]{:S(2)}, u32[]{:S(2)}) collective-permute-start(bf16[28,128,128]{2,1,0:T(8,128)(2,1)} %get-tuple-element.16), channel_id=1, source_target_pairs={{0,64},{32,96},{64,128},{96,160},{128,192},{160,224},{192,0},{224,... | collective-permute-start | bytes 2752520 | tf_op jit(solution)/shard_map/ppermute | solution.py:247
  109.3 60.6 %all-to-all-start.1 = ((bf16[32,7,16,128]{3,2,1,0:T(8,128)(2,1)}), bf16[32,7,16,128]{3,2,1,0:T(8,128)(2,1)}, u32[]{:S(2)}, u32[]{:S(2)}) async-start(bf16[32,7,16,128]{3,2,1,0:T(8,128)(2,1)} %get-tuple-element.11), calls=%async_computation.1 | async-start | bytes 1835008 | tf_op jit(solution)/shard_map/all_to_all | solution.py:249
  117.4 132.4 %all-gather.2.cloned.1.call-start = ((), (), s32[]{:S(2)}) async-start(), calls=%async_computation.2 | async-start | bytes 4587520 | tf_op jit(solution)/shard_map/all_gather | solution.py:289
  154.4 29.2 %collective-permute-start.17 = (bf16[28,128,128]{2,1,0:T(8,128)(2,1)S(1)}, bf16[28,128,128]{2,1,0:T(8,128)(2,1)}, u32[]{:S(2)}, u32[]{:S(2)}) collective-permute-start(bf16[28,128,128]{2,1,0:T(8,128)(2,1)S(1)} %add_convert_fusion.1), channel_id=1, source_target_pairs={{0,32},{32,0},{64,96},{96,64},{128,160},{160,128},{192,224},{224,1... | collective-permute-start | bytes 2752520 | tf_op jit(solution)/shard_map/ppermute | solution.py:286
  162.4 1.3 copy-start.2
  164.9 21.2 %collective-permute-start.10 = (bf16[64,4096]{1,0:T(8,128)(2,1)}, bf16[64,4096]{1,0:T(8,128)(2,1)S(1)}, u32[]{:S(2)}, u32[]{:S(2)}) collective-permute-start(bf16[64,4096]{1,0:T(8,128)(2,1)} %get-tuple-element.26), channel_id=1, source_target_pairs={{0,2},{1,3},{2,4},{3,5},{4,6},{5,7},{6,0},{7,1},{8,10},{9,11},{10,... | collective-permute-start | bytes 1572872 | tf_op jit(solution)/shard_map/ppermute | solution.py:271
  167.1 24.0 %collective-permute-start.9 = (bf16[64,4096]{1,0:T(8,128)(2,1)}, bf16[64,4096]{1,0:T(8,128)(2,1)S(1)}, u32[]{:S(2)}, u32[]{:S(2)}) collective-permute-start(bf16[64,4096]{1,0:T(8,128)(2,1)} %get-tuple-element.27), channel_id=1, source_target_pairs={{0,4},{1,5},{2,6},{3,7},{4,0},{5,1},{6,2},{7,3},{8,12},{9,13},{10,... | collective-permute-start | bytes 1572872 | tf_op jit(solution)/shard_map/ppermute | solution.py:271
  168.4 22.7 %collective-permute-start.8 = (bf16[64,4096]{1,0:T(8,128)(2,1)}, bf16[64,4096]{1,0:T(8,128)(2,1)S(1)}, u32[]{:S(2)}, u32[]{:S(2)}) collective-permute-start(bf16[64,4096]{1,0:T(8,128)(2,1)} %get-tuple-element.25), channel_id=1, source_target_pairs={{0,6},{1,7},{2,0},{3,1},{4,2},{5,3},{6,4},{7,5},{8,14},{9,15},{10,... | collective-permute-start | bytes 1572872 | tf_op jit(solution)/shard_map/ppermute | solution.py:271
  192.4 17.2 %collective-permute-start.13 = (bf16[16,4096]{1,0:T(8,128)(2,1)S(1)}, bf16[16,4096]{1,0:T(8,128)(2,1)S(1)}, u32[]{:S(2)}, u32[]{:S(2)}) collective-permute-start(bf16[16,4096]{1,0:T(8,128)(2,1)S(1)} %get-tuple-element.29), channel_id=1, source_target_pairs={{0,8},{1,9},{2,10},{3,11},{4,12},{5,13},{6,14},{7,15},{8,16},{9,17... | collective-permute-start | bytes 393224 | tf_op jit(solution)/shard_map/ppermute | solution.py:276
  206.5 8.5 %collective-permute-start.12 = (bf16[16,4096]{1,0:T(8,128)(2,1)S(1)}, bf16[16,4096]{1,0:T(8,128)(2,1)S(1)}, u32[]{:S(2)}, u32[]{:S(2)}) collective-permute-start(bf16[16,4096]{1,0:T(8,128)(2,1)S(1)} %get-tuple-element.30), channel_id=1, source_target_pairs={{0,16},{1,17},{2,18},{3,19},{4,20},{5,21},{6,22},{7,23},{8,24},{9,... | collective-permute-start | bytes 393224 | tf_op jit(solution)/shard_map/ppermute | solution.py:276
  206.5 8.5 %collective-permute-start.11 = (bf16[16,4096]{1,0:T(8,128)(2,1)S(1)}, bf16[16,4096]{1,0:T(8,128)(2,1)S(1)}, u32[]{:S(2)}, u32[]{:S(2)}) collective-permute-start(bf16[16,4096]{1,0:T(8,128)(2,1)S(1)} %get-tuple-element.28), channel_id=1, source_target_pairs={{0,24},{1,25},{2,26},{3,27},{4,28},{5,29},{6,30},{7,31},{8,0},{9,1... | collective-permute-start | bytes 393224 | tf_op jit(solution)/shard_map/ppermute | solution.py:276
Sparse Core Ops, SparseCore 0:
  186.2 63.5 all-gather.1

commit v2 on v0

v2 whole, which is shorter than its diff:
```python
import functools
import math

import jax
import jax.numpy as jnp
from jax import lax
from jax.experimental import pallas as pl
from jax.experimental.pallas import tpu as pltpu
from jax.sharding import PartitionSpec as P

NZ, NY, NC = 4, 4, 2
NX, NH = 4, 2
GROUP = 16


def shift_zl(distance):
    return [
        ((z * NY + y) * NC + c, (((z + distance) % NZ) * NY + y) * NC + c)
        for z in range(NZ)
        for y in range(NY)
        for c in range(NC)
    ]


def shift_y(distance):
    return [
        ((z * NY + y) * NC + c, (z * NY + (y + distance) % NY) * NC + c)
        for z in range(NZ)
        for y in range(NY)
        for c in range(NC)
    ]


def swap_c():
    return [(k, k ^ 1) for k in range(NZ * NY * NC)]


def shift_x(distance):
    return [
        (x * NH + h, ((x + distance) % NX) * NH + h) for x in range(NX) for h in range(NH)
    ]


def swap_h():
    return [(r, r ^ 1) for r in range(NX * NH)]


def build_dense(rows_ref, first, blocks_ref, dense_ref):
    slots, keep, bs = blocks_ref.shape[0], blocks_ref.shape[1], blocks_ref.shape[2]
    for p in range(slots):
        for j in range(keep):
            at = pl.multiple_of(rows_ref[(first + p) * keep + j] * bs, bs)
            dense_ref[pl.ds(at, bs), p * bs : (p + 1) * bs] = blocks_ref[p, j]


def forward_kernel(first, slots, pieces, rows_ref, place_ref, live_ref, source_ref, *rest):
    token_hbm = rest[:pieces]
    blocks_hbm, ups_hbm = rest[pieces : pieces + 2]
    outs = rest[pieces + 2 :]
    earlier_ref = None
    if first > 0:
        earlier_ref, outs = outs[0], outs[1:]
    act_ref, dz_ref = outs[:2]
    chunk_refs, outs = outs[2 : 2 + NX], outs[2 + NX :]
    if first > 0:
        back_refs, outs = outs[:2], outs[2:]
    tok_ref, blocks_ref, ups_ref, dense_ref, dzt_ref, dzs_ref, grads_ref, in_sems, out_sems = outs
    keep, bs = blocks_ref.shape[1], blocks_ref.shape[2]
    base = blocks_ref.shape[0] - slots
    rows, width = tok_ref.shape
    row_blocks = width // bs
    part = rows // pieces
    tile, span = 512, 1024

    get_blocks = pltpu.make_async_copy(
        blocks_hbm.at[pl.ds(first - base, base + slots)], blocks_ref, in_sems.at[0]
    )
    get_ups = pltpu.make_async_copy(ups_hbm.at[:, pl.ds(first, slots)], ups_ref, in_sems.at[1])
    get_tokens = [
        pltpu.make_async_copy(
            token_hbm[i], tok_ref.at[pl.ds(i * part, part)], in_sems.at[2 + i]
        )
        for i in range(pieces)
    ]
    get_blocks.start()
    for copy in get_tokens:
        copy.start()
    get_ups.start()
    dense_ref[...] = jnp.zeros_like(dense_ref)
    get_blocks.wait()
    build_dense(rows_ref, first - base, blocks_ref, dense_ref)
    get_ups.wait()
    for copy in get_tokens:
        copy.wait()

    def step(t, carry):
        row = pl.multiple_of(t * tile, tile)
        z = jnp.dot(
            tok_ref[pl.ds(row, tile), :],
            dense_ref[:, base * bs :],
            preferred_element_type=jnp.float32,
        )
        sig = jax.nn.sigmoid(z)
        act = (z * sig).astype(jnp.bfloat16)
        slope = sig * (1.0 + z * (1.0 - sig))
        for g in range(tile // GROUP):
            src = source_ref[t * (tile // GROUP) + g]
            lo = g * GROUP
            for p in range(slots):
                cols = slice(p * bs, (p + 1) * bs)
                act_ref[src, p] = act[lo : lo + GROUP, cols]
                up = ups_ref[src, p].astype(jnp.float32) * slope[lo : lo + GROUP, cols]
                up = jnp.where(live_ref[first + p] == 1, up, 0.0)
                dz_ref[pl.ds(row + lo, GROUP), cols] = up.astype(jnp.bfloat16)
        return carry

    lax.fori_loop(0, rows // tile, step, 0)

    dzt_ref[...] = dz_ref[...].T

    def grad_step(r, carry):
        at = pl.multiple_of(r * span, span)
        grad = jnp.dot(
            dzt_ref[...], tok_ref[:, pl.ds(at, span)], preferred_element_type=jnp.float32
        ).astype(jnp.bfloat16)
        for k in range(span // bs):
            for p in range(slots):
                place = place_ref[(first + p) * row_blocks + r * (span // bs) + k]
                grads_ref[place] = grad[p * bs : (p + 1) * bs, k * bs : (k + 1) * bs]
        return carry

    lax.fori_loop(0, width // span, grad_step, 0)
    chunk = slots * keep // NX
    copies = [
        pltpu.make_async_copy(
            grads_ref.at[pl.ds(d * chunk, chunk)], chunk_refs[d], out_sems.at[d]
        )
        for d in range(NX)
    ]
    for copy in copies:
        copy.start()
    if first > 0:
        dzs_ref[:, : base * bs] = earlier_ref[...]
        dzs_ref[:, base * bs :] = dz_ref[...]
        half, wide = rows // 2, 512

        def back_step(t, carry):
            at = pl.multiple_of(t * wide, wide)
            back = lax.dot_general(
                dzs_ref[...],
                dense_ref[pl.ds(at, wide), :],
                (((1,), (1,)), ((), ())),
                preferred_element_type=jnp.float32,
            ).astype(jnp.bfloat16)
            back_refs[0][:, pl.ds(at, wide)] = back[:half]
            back_refs[1][:, pl.ds(at, wide)] = back[half:]
            return carry

        lax.fori_loop(0, width // wide, back_step, 0)
    for copy in copies:
        copy.wait()


def add_kernel(*refs):
    out_ref = refs[-1]
    for i in range(out_ref.shape[0]):
        total = refs[0][i].astype(jnp.float32)
        for ref in refs[1:-1]:
            total = total + ref[i].astype(jnp.float32)
        out_ref[i] = total.T.astype(out_ref.dtype)


def place_kernel(count, *refs):
    start_ref = refs[0]
    part_refs, out_ref, sems = refs[1 : 1 + count], refs[-2], refs[-1]
    copies = [
        pltpu.make_async_copy(
            part, out_ref.at[pl.ds(start_ref[i], part.shape[0])], sems.at[i]
        )
        for i, part in enumerate(part_refs)
    ]
    for copy in copies:
        copy.start()
    for copy in copies:
        copy.wait()


SMALL = pl.CostEstimate(flops=1000, bytes_accessed=1000, transcendentals=0)


def anywhere():
    return pl.BlockSpec(memory_space=pl.ANY)


def add_transposed(arrays):
    return pl.pallas_call(
        add_kernel,
        out_shape=jax.ShapeDtypeStruct(arrays[0].shape, jnp.bfloat16),
        in_specs=[whole()] * len(arrays),
        out_specs=whole(),
        cost_estimate=SMALL,
        compiler_params=pltpu.CompilerParams(vmem_limit_bytes=16 * 2**20),
        name="add_along_x",
    )(*arrays)


def place(starts, total, parts, into=None):
    args = (starts, *parts) + (() if into is None else (into,))
    return pl.pallas_call(
        functools.partial(place_kernel, len(parts)),
        out_shape=jax.ShapeDtypeStruct((total,) + parts[0].shape[1:], parts[0].dtype),
        in_specs=[scalars()] + [anywhere()] * (len(args) - 1),
        out_specs=anywhere(),
        input_output_aliases={} if into is None else {len(args) - 1: 0},
        scratch_shapes=[pltpu.SemaphoreType.DMA((len(parts),))],
        cost_estimate=SMALL,
        compiler_params=pltpu.CompilerParams(vmem_limit_bytes=16 * 2**20),
        name="place_blocks",
    )(*args)


def whole():
    return pl.BlockSpec(memory_space=pltpu.VMEM)


def scalars():
    return pl.BlockSpec(memory_space=pltpu.SMEM)


def per_device(tokens, upstream, blocks, keep_mask, panel_owner):
    shard_count = lax.axis_size("fsdp")
    own_index = lax.axis_index("fsdp")
    x_index = lax.axis_index("rep") // NH
    tok_dev, model_width = tokens.shape
    slot_count, keep_count, block_size = blocks.shape[0], blocks.shape[1], blocks.shape[3]
    row_blocks = keep_mask.shape[0]
    panel_count = panel_owner.shape[0]
    half = tok_dev * NZ * NY
    f32, bf16 = jnp.float32, jnp.bfloat16

    shard_ids = jnp.arange(shard_count, dtype=jnp.int32)
    member = (panel_owner[:, None] == shard_ids[None, :]).astype(jnp.int32)
    counts = jnp.sum(member, axis=0)
    first_panel = jnp.cumsum(counts) - counts
    slot_ids = jnp.arange(slot_count, dtype=jnp.int32)
    panel_table = jnp.clip(first_panel[:, None] + slot_ids[None, :], 0, panel_count - 1)
    is_mine = shard_ids == own_index
    own_first = jnp.sum(jnp.where(is_mine, first_panel, 0))
    own_count = jnp.sum(jnp.where(is_mine, counts, 0))
    own_live = (slot_ids < own_count).astype(jnp.int32)
    own_panels = jnp.clip(own_first + slot_ids, 0, panel_count - 1)
    panel_ids = jnp.arange(panel_count, dtype=jnp.int32)
    panel_pick = (panel_ids[None, :] == own_panels[:, None]).astype(jnp.int32)
    running = jnp.cumsum(keep_mask, axis=0)
    own_running = jnp.sum(panel_pick[:, None, :] * running[None, :, :], axis=2)
    own_keep = jnp.sum(panel_pick[:, None, :] * keep_mask[None, :, :], axis=2)
    pick_ids = jnp.arange(keep_count, dtype=jnp.int32)
    own_rows = jnp.sum(
        (own_running[:, :, None] <= pick_ids[None, None, :]).astype(jnp.int32), axis=1
    )
    sets = ((0, slot_count // 2), (slot_count // 2, slot_count))
    places = []
    for lo, hi in sets:
        chunk = (hi - lo) * keep_count // NX
        flat = (slot_ids[lo:hi, None] - lo) * keep_count + own_running[lo:hi] - 1
        spot = ((flat // chunk - x_index) % NX) * chunk + flat % chunk
        places.append(jnp.where(own_keep[lo:hi] == 1, spot, (hi - lo) * keep_count))
    places = jnp.concatenate(places, axis=0).reshape(-1).astype(jnp.int32)
    rows_flat = own_rows.reshape(-1).astype(jnp.int32)
    my_z, my_y, my_c = own_index // (NY * NC), (own_index // NC) % NY, own_index % NC
    away_c = jnp.arange(2, dtype=jnp.int32)[:, None, None]
    away_y = jnp.arange(NY, dtype=jnp.int32)[None, :, None]
    away_z = jnp.arange(NZ, dtype=jnp.int32)[None, None, :]
    source = (((my_z - away_z) % NZ) * NY + (my_y - away_y) % NY) * NC + (my_c + away_c) % NC
    source = source.reshape(-1).astype(jnp.int32)

    upstream_panels = jnp.transpose(upstream.reshape(tok_dev, panel_count, block_size), (1, 0, 2))
    outgoing = jnp.take(upstream_panels, panel_table.reshape(-1), axis=0)
    outgoing = outgoing.reshape(shard_count, slot_count, tok_dev, block_size)
    outgoing, tokens = lax.optimization_barrier((outgoing, tokens))
    incoming = lax.all_to_all(outgoing, "fsdp", split_axis=0, concat_axis=0, tiled=True)

    along_z = [tokens] + [lax.ppermute(tokens, "fsdp", shift_zl(d)) for d in range(1, NZ)]
    line = jnp.concatenate(along_z, axis=0)
    along_y = [line] + [lax.ppermute(line, "fsdp", shift_y(d)) for d in range(1, NY)]
    along_y[1], incoming = lax.optimization_barrier((along_y[1], incoming))
    runs = along_y + [lax.ppermute(run, "fsdp", swap_c()) for run in along_y]

    acts, dzs, pieces = [], [], []
    for lo, hi in sets:
        slots = hi - lo
        wide = slots * block_size
        chunk = slots * keep_count // NX
        held = slots + len(dzs) * lo
        outs = pl.pallas_call(
            functools.partial(forward_kernel, lo, slots, len(runs)),
            out_shape=(
                jax.ShapeDtypeStruct((shard_count, slots, tok_dev, block_size), bf16),
                jax.ShapeDtypeStruct((2 * half, wide), bf16),
            )
            + tuple(
                jax.ShapeDtypeStruct((chunk, block_size, block_size), bf16) for _ in range(NX)
            )
            + (jax.ShapeDtypeStruct((half, model_width), bf16),) * 2 * len(dzs),
            in_specs=[scalars()] * 4 + [anywhere()] * (len(runs) + 2) + [whole()] * len(dzs),
            out_specs=(whole(), whole()) + (anywhere(),) * NX + (whole(),) * 2 * len(dzs),
            scratch_shapes=[
                pltpu.VMEM((2 * half, model_width), bf16),
                pltpu.VMEM((held, keep_count, block_size, block_size), bf16),
                pltpu.VMEM((shard_count, slots, tok_dev, block_size), bf16),
                pltpu.VMEM((model_width, held * block_size), bf16),
                pltpu.VMEM((wide, 2 * half), bf16),
                pltpu.VMEM((2 * half, held * block_size), bf16),
                pltpu.VMEM((NX * chunk + 1, block_size, block_size), bf16),
                pltpu.SemaphoreType.DMA((len(runs) + 2,)),
                pltpu.SemaphoreType.DMA((NX,)),
            ],
            compiler_params=pltpu.CompilerParams(vmem_limit_bytes=40 * 2**20),
            cost_estimate=SMALL,
            name="forward_and_grads" if dzs else "forward_and_block_grad",
        )(rows_flat, places, own_live, source, *runs, blocks, incoming, *dzs)
        acts.append(outs[0])
        dzs.append(outs[1])
        pieces.append(outs[2 : 2 + NX])
    grad_own, grad_sib = outs[2 + NX :]
    got = [[lax.ppermute(piece[d], "rep", shift_x(d)) for d in range(1, NX)] for piece in pieces]

    scale = 1.0 / math.sqrt(2 * half * lax.axis_size("rep"))
    along = [add_transposed([piece[0]] + parts) for piece, parts in zip(pieces, got)]
    grad_sib, along[0] = lax.optimization_barrier((grad_sib, along[0]))
    other = [lax.ppermute(part, "rep", swap_h()) for part in along]
    other[0], along[1] = lax.optimization_barrier((other[0], along[1]))
    mines = [
        ((part.astype(f32) + more.astype(f32)) * scale).astype(bf16)
        for part, more in zip(along, other)
    ]
    gathered = lax.all_gather(
        mines[0],
        "rep",
        axis=0,
        tiled=True,
        axis_index_groups=[[x * NH + h for x in range(NX)] for h in range(NH)],
    )
    rest = [mines[1]] + [lax.ppermute(mines[1], "rep", shift_x(d)) for d in range(1, NX)]
    acts = jnp.concatenate(acts, axis=1)
    acts, along[0] = lax.optimization_barrier((acts, along[0]))
    returned = lax.all_to_all(acts, "fsdp", split_axis=0, concat_axis=0, tiled=True)
    from_sib = lax.ppermute(grad_sib, "fsdp", swap_c())
    pair = (grad_own.astype(f32) + from_sib.astype(f32)).astype(bf16)
    pair = pair.reshape(NY, NZ * tok_dev, model_width)
    parts = [lax.ppermute(pair[d], "fsdp", shift_y(-d)) for d in range(1, NY)]
    total = pair[0].astype(f32)
    for part in parts:
        total = total + part.astype(f32)
    total = total.astype(bf16).reshape(NZ, tok_dev, model_width)
    total, gathered, returned = lax.optimization_barrier((total, gathered, returned))
    parts = [lax.ppermute(total[d], "fsdp", shift_zl(-d)) for d in range(1, NZ)]
    input_grad = total[0].astype(f32)
    for part in parts:
        input_grad = input_grad + part.astype(f32)
    input_grad = input_grad.astype(bf16)

    panel_first = jnp.sum(member * first_panel[None, :], axis=1)
    panel_slot = panel_owner * slot_count + panel_ids - panel_first
    act_panels = jnp.take(
        returned.reshape(shard_count * slot_count, tok_dev, block_size), panel_slot, axis=0
    )
    activation_out = jnp.transpose(act_panels, (1, 0, 2)).reshape(tok_dev, panel_count * block_size)

    blocks_all = slot_count * keep_count
    block_grad = place(jnp.zeros((1,), jnp.int32), blocks_all, [gathered])
    away = jnp.arange(NX, dtype=jnp.int32)
    starts = sets[1][0] * keep_count + ((x_index - away) % NX) * rest[0].shape[0]
    block_grad = place(starts.astype(jnp.int32), blocks_all, rest, block_grad)
    return (activation_out, input_grad, block_grad.reshape(blocks.shape))


def solution(mesh):
    return jax.shard_map(
        per_device,
        mesh=mesh,
        in_specs=(
            P(("rep", "fsdp"), None),
            P(("rep", "fsdp"), None),
            P("fsdp", None, None, None),
            P(),
            P(),
        ),
        out_specs=(P(("rep", "fsdp"), None), P(("rep", "fsdp"), None), P("fsdp", None, None, None)),
        check_vma=False,
    )
```

time: 1010 us -> 238 us (0.24)
  waiting for transfers between devices: 758 us -> 52.8 us
  local copies, waits for them, and re-layouts: 130 us -> 15.2 us
  Pallas kernels: 0 us -> 60.5 us
  starting transfers between devices: 15.5 us -> 75 us
  matrix products: 53 us -> 0 us
  other arithmetic: 37 us -> 17.1 us
    all_to_all x2, waiting for transfers between devices: 290 us -> 0.37 us  [the longest x1 0.37 us: per_device(): lax.all_to_all(acts, 'fsdp', split_axis=0, concat_axis=0, tiled=True)]
    psum x1 -> x0, waiting for transfers between devices: 288 us -> none  [per_device(): summed = lax.psum(weight_grads, 'rep')]
    reduce_scatter x1 -> x0, waiting for transfers between devices: 146 us -> none  [per_device(): lax.psum_scatter(backward.reshape(dpres.shape[1], model_width), 'fsdp', s...]
    pallas_call x0 -> x6, Pallas kernels: none -> 60.5 us  [the longest x2 34.6 us: place(): pl.pallas_call(functools.partial(place_kernel, len(parts)), out_shape=jax...]
    ppermute x0 -> x28, starting transfers between devices: none -> 58.5 us  [the longest x3 14.5 us: per_device(): lax.ppermute(mines[1], 'rep', shift_x(d))]
    dot_general x15 -> x0, matrix products: 53 us -> none  [the longest x7 26 us: panel_step(): preact = jnp.dot(chosen, flat_weights, preferred_element_type=jnp.float32)]
    ppermute x0 -> x28, waiting for transfers between devices: none -> 50 us  [the longest x3 25 us: per_device(): lax.ppermute(line, 'fsdp', shift_y(d))]
    gather x15 -> x1, local copies, waits for them, and re-layouts: 40.7 us -> 1.86 us  [per_device(): jnp.take(returned.reshape(shard_count * slot_count, tok_dev, block_size),...]
  transfers between devices with their start and end apart: 5 -> 31, of which waited for: 5 -> 11; matrix products, arithmetic and copies ran while one was open for 6% -> 6% of each run, Pallas kernels for 0% -> 22%
where the time goes in v2:
time: 238 us; the launch traced here: 235 us
  starting transfers between devices  75 us (32%)
  Pallas kernels  60.5 us (25%)
  waiting for transfers between devices  52.8 us (22%)
  other arithmetic  17.1 us (7%)
  local copies, waits for them, and re-layouts  15.2 us (6%)
  between operations  14.5 us (6%)
    pallas_call x2, Pallas kernels, place(): pl.pallas_call(functools.partial(place_kernel, len(parts)), out_shape=jax...  34.6 us
    pallas_call x2, Pallas kernels, per_device(): pl.pallas_call(functools.partial(forward_kernel, lo, slots, len(runs)), o...  25.3 us
    ppermute x3, waiting for transfers between devices, per_device(): lax.ppermute(line, 'fsdp', shift_y(d))  25 us
    ppermute x3, starting transfers between devices, per_device(): lax.ppermute(mines[1], 'rep', shift_x(d))  14.5 us
    ppermute x2, starting transfers between devices, per_device(): other = [lax.ppermute(part, 'rep', swap_h()) for part in along]  10.4 us
    unnamed x33, local copies, waits for them, and re-layouts  10 us
    ppermute x6, waiting for transfers between devices, per_device(): lax.ppermute(piece[d], 'rep', shift_x(d))  9.37 us
    all_to_all x1, starting transfers between devices, per_device(): lax.all_to_all(outgoing, 'fsdp', split_axis=0, concat_axis=0, tiled=True)  8.56 us
  transfers between devices with their start and end apart: 31, of which 11 were waited for; matrix products, arithmetic and copies ran while one was open for 6% of the time, Pallas kernels for 22%

profile of v2, /device:TPU:1, one launch (start us, length us, event | category | flops | bytes accessed | tf_op | source)
XLA Modules:
  0.0 235.1 jit_solution(10102556090130939994)
XLA Ops:
  12.8 5.2 %collective-permute-start.2 = (bf16[16,4096]{1,0:T(8,128)(2,1)S(1)}, bf16[16,4096]{1,0:T(8,128)(2,1)S(1)}, u32[]{:S(2)}, u32[]{:S(2)}) collective-permute-start(bf16[16,4096]{1,0:T(8,128)(2,1)S(1)} %copy-done.13), channel_id=1, source_target_pairs={{0,24},{1,25},{2,26},{3,27},{4,28},{5,29},{6,30},{7,31},{8,0},{9,1... | collective-permute-start | bytes 393224 | tf_op jit(solution)/shard_map/ppermute | solution.py:283
  18.3 8.6 %all-to-all-start = ((bf16[32,7,16,128]{3,2,1,0:T(8,128)(2,1)}), bf16[32,7,16,128]{3,2,1,0:T(8,128)(2,1)S(1)}, u32[]{:S(2)}, u32[]{:S(2)}) async-start(bf16[32,7,16,128]{3,2,1,0:T(8,128)(2,1)} %broadcast_select_fusion), calls=%async_computation | async-start | bytes 1835008 | tf_op jit(solution)/shard_map/all_to_all | solution.py:281
  29.0 2.8 %collective-permute-start.5 = (bf16[64,4096]{1,0:T(8,128)(2,1)S(1)}, bf16[64,4096]{1,0:T(8,128)(2,1)S(1)}, u32[]{:S(2)}, u32[]{:S(2)}) collective-permute-start(bf16[64,4096]{1,0:T(8,128)(2,1)S(1)} %constant_dynamic-update-slice_fusion.rest_0_), channel_id=1, source_target_pairs={{0,6},{1,7},{2,0},{3,1},{4,2},{5,3},{6,4},{7,5},{8,14},{9,15},{10,... | collective-permute-start | bytes 1572872 | tf_op jit(solution)/shard_map/ppermute | solution.py:285
  33.3 2.1 collective-permute-start.6
  35.4 14.4 %collective-permute-done.5.rest_3_ = bf16[64,4096]{1,0:T(8,128)(2,1)S(1)} collective-permute-done((bf16[64,4096]{1,0:T(8,128)(2,1)S(1)}, bf16[64,4096]{1,0:T(8,128)(2,1)S(1)}, u32[]{:S(2)}, u32[]{:S(2)}) %collective-permute-start.5) | collective-permute-done | bytes 524320 | tf_op jit(solution)/shard_map/ppermute | solution.py:285
  49.8 1.7 collective-permute-start.9
  51.5 1.3 collective-permute-done.4.rest_2_
  52.8 1.9 collective-permute-start.8
  54.8 9.2 %collective-permute-done.3.rest_1_ = bf16[64,4096]{1,0:T(8,128)(2,1)S(1)} collective-permute-done((bf16[64,4096]{1,0:T(8,128)(2,1)S(1)}, bf16[64,4096]{1,0:T(8,128)(2,1)S(1)}, u32[]{:S(2)}, u32[]{:S(2)}) %collective-permute-start.3) | collective-permute-done | bytes 524320 | tf_op jit(solution)/shard_map/ppermute | solution.py:285
  66.3 2.0 copy-done.1
  68.4 8.4 %forward_and_block_grad.1 = (bf16[32,3,16,128]{3,2,1,0:T(8,128)(2,1)S(1)}, bf16[512,384]{1,0:T(8,128)(2,1)S(1)}, bf16[12,128,128]{2,1,0:T(8,128)(2,1)S(1)}, bf16...) custom-call(s32[112]{0:T(128)S(1)} %reshape.260.rows_ref, ...), custom_call_target="tpu_custom_call" | custom-call | flops 1000 | bytes 1000 | tf_op jit(solution)/shard_map/forward_and_block_grad/pallas_call | solution.py:295
  76.8 1.5 collective-permute-start.10
  78.3 2.5 %collective-permute-start.11 = (bf16[12,128,128]{2,1,0:T(8,128)(2,1)S(1)}, bf16[12,128,128]{2,1,0:T(8,128)(2,1)S(1)}, u32[]{:S(2)}, u32[]{:S(2)}) collective-permute-start(bf16[12,128,128]{2,1,0:T(8,128)(2,1)S(1)} %get-tuple-element.37), channel_id=1, source_target_pairs={{0,128},{32,160},{64,192},{96,224},{128,0},{160,32},{192,64},{224,... | collective-permute-start | bytes 1179656 | tf_op jit(solution)/shard_map/ppermute | solution.py:326
  81.9 16.8 %forward_and_grads.1 = (bf16[32,4,16,128]{3,2,1,0:T(8,128)(2,1)S(1)}, bf16[512,512]{1,0:T(8,128)(2,1)}, bf16[16,128,128]{2,1,0:T(8,128)(2,1)S(1)}, bf16[16,128,1...) custom-call(s32[112]{0:T(128)S(1)} %reshape.260.rows_ref, ...), custom_call_target="tpu_custom_call" | custom-call | flops 1000 | bytes 1000 | tf_op jit(solution)/shard_map/forward_and_grads/pallas_call | solution.py:295
  98.7 1.3 copy-done.2
  102.8 1.6 collective-permute-start.20
  104.4 5.2 %collective-permute-start.17 = (bf16[12,128,128]{2,1,0:T(8,128)(2,1)S(1)}, bf16[12,128,128]{2,1,0:T(8,128)(2,1)}, u32[]{:S(2)}, u32[]{:S(2)}) collective-permute-start(bf16[12,128,128]{2,1,0:T(8,128)(2,1)S(1)} %add_along_x.2), channel_id=1, source_target_pairs={{0,32},{32,0},{64,96},{96,64},{128,160},{160,128},{192,224},{224,1... | collective-permute-start | bytes 1179656 | tf_op jit(solution)/shard_map/ppermute | solution.py:331
  110.6 7.8 %all-to-all-start.1 = ((bf16[32,7,16,128]{3,2,1,0:T(8,128)(2,1)}), bf16[32,7,16,128]{3,2,1,0:T(8,128)(2,1)}, u32[]{:S(2)}, u32[]{:S(2)}) async-start(bf16[32,7,16,128]{3,2,1,0:T(8,128)(2,1)} %pad_maximum_fusion), calls=%async_computation.1 | async-start | bytes 1835008 | tf_op jit(solution)/shard_map/all_to_all | solution.py:347
  118.4 9.4 %collective-permute-done.18.refs_1_ = bf16[16,128,128]{2,1,0:T(8,128)(2,1)S(1)} collective-permute-done((bf16[16,128,128]{2,1,0:T(8,128)(2,1)}, bf16[16,128,128]{2,1,0:T(8,128)(2,1)S(1)}, u32[]{:S(2)}, u32[]{:S(2)}) %collective-permute-start.18) | collective-permute-done | bytes 524320 | tf_op jit(solution)/shard_map/ppermute | solution.py:326
  134.8 5.2 %collective-permute-start.24 = (bf16[16,128,128]{2,1,0:T(8,128)(2,1)S(1)}, bf16[16,128,128]{2,1,0:T(8,128)(2,1)}, u32[]{:S(2)}, u32[]{:S(2)}) collective-permute-start(bf16[16,128,128]{2,1,0:T(8,128)(2,1)S(1)} %add_along_x.3), channel_id=1, source_target_pairs={{0,32},{32,0},{64,96},{96,64},{128,160},{160,128},{192,224},{224,1... | collective-permute-start | bytes 1572872 | tf_op jit(solution)/shard_map/ppermute | solution.py:331
  140.0 1.9 multiply_convert_fusion.1
  141.9 2.4 %add_convert_fusion = bf16[256,4096]{1,0:T(8,128)(2,1)S(1)} fusion(bf16[256,4096]{1,0:T(8,128)(2,1)} %collective-permute-done.13, bf16[256,4096]{1,0:T(8,128)(2,1)S(1)} %copy-done.3), kind=kLoop, calls=%fused_computation.2 | loop fusion | flops 4194304 | bytes 6291456 | tf_op jit(solution)/shard_map/convert_element_type | solution.py:349
  146.8 7.0 %collective-permute-done.24 = bf16[16,128,128]{2,1,0:T(8,128)(2,1)} collective-permute-done((bf16[16,128,128]{2,1,0:T(8,128)(2,1)S(1)}, bf16[16,128,128]{2,1,0:T(8,128)(2,1)}, u32[]{:S(2)}, u32[]{:S(2)}) %collective-permute-start.24) | collective-permute-done | bytes 524320 | tf_op jit(solution)/shard_map/ppermute | solution.py:331
  156.0 12.8 %collective-permute-start.26 = (bf16[16,128,128]{2,1,0:T(8,128)(2,1)S(1)}, bf16[16,128,128]{2,1,0:T(8,128)(2,1)}, u32[]{:S(2)}, u32[]{:S(2)}) collective-permute-start(bf16[16,128,128]{2,1,0:T(8,128)(2,1)S(1)} %multiply_convert_fusion.refs_1_), channel_id=1, source_target_pairs={{0,128},{32,160},{64,192},{96,224},{128,0},{160,32},{192,64},{224,... | collective-permute-start | bytes 1572872 | tf_op jit(solution)/shard_map/ppermute | solution.py:344
  171.6 2.4 %all-gather.2.cloned.1.call-done.refs_1_ = bf16[48,128,128]{2,1,0:T(8,128)(2,1)} async-done(((bf16[12,128,128]{2,1,0:T(8,128)(2,1)}), bf16[48,128,128]{2,1,0:T(8,128)(2,1)}) %all-gather.2.cloned.1.call-update) | async-done | bytes 1572880 | tf_op jit(solution)/shard_map/all_gather | solution.py:337
  174.0 1.9 slice_bitcast_fusion.2
  175.9 1.5 collective-permute-start.23
  177.4 1.9 gather_fusion.1
  179.3 5.0 %collective-permute-start.22 = (bf16[16,4096]{1,0:T(8,128)(2,1)}, bf16[16,4096]{1,0:T(8,128)(2,1)S(1)}, u32[]{:S(2)}, u32[]{:S(2)}) collective-permute-start(bf16[16,4096]{1,0:T(8,128)(2,1)} %get-tuple-element.64), channel_id=1, source_target_pairs={{0,16},{1,17},{2,18},{3,19},{4,20},{5,21},{6,22},{7,23},{8,24},{9,... | collective-permute-start | bytes 393224 | tf_op jit(solution)/shard_map/ppermute | solution.py:357
  186.4 6.6 %collective-permute-done.25.refs_2_ = bf16[16,128,128]{2,1,0:T(8,128)(2,1)} collective-permute-done((bf16[16,128,128]{2,1,0:T(8,128)(2,1)S(1)}, bf16[16,128,128]{2,1,0:T(8,128)(2,1)}, u32[]{:S(2)}, u32[]{:S(2)}) %collective-permute-start.25) | collective-permute-done | bytes 524320 | tf_op jit(solution)/shard_map/ppermute | solution.py:344
  193.0 33.4 %place_blocks.3 = bf16[112,128,128]{2,1,0:T(8,128)(2,1)} custom-call(s32[4]{0:T(128)S(1)} %fusion.19.refs_0_, bf16[16,128,128]{2,1,0:T(8,128)(2,1)S(1)} %multiply_convert_fusion.refs_1_, bf16[16,128,128]{2,1,0:T(8,128)(2,1)} %collective-permute-done.25.refs_2_, ...), custom_call_target="tpu_custom_call", output_to_operand_aliasing={{}: (5, {})} | custom-call | flops 1000 | bytes 1000 | tf_op jit(solution)/shard_map/place_blocks/pallas_call | solution.py:209
  226.5 1.8 fusion.2
  (117 shorter events, 33.2 us)
Async XLA Ops:
  11.5 16.4 %copy-start.14 = (s32[32,112]{1,0:T(8,128)S(1)}, s32[32,112]{1,0:T(8,128)}, u32[]{:S(2)}) copy-start(s32[32,112]{1,0:T(8,128)} %param.8) | copy-start | bytes 43012
  12.8 16.2 %collective-permute-start.2 = (bf16[16,4096]{1,0:T(8,128)(2,1)S(1)}, bf16[16,4096]{1,0:T(8,128)(2,1)S(1)}, u32[]{:S(2)}, u32[]{:S(2)}) collective-permute-start(bf16[16,4096]{1,0:T(8,128)(2,1)S(1)} %copy-done.13), channel_id=1, source_target_pairs={{0,24},{1,25},{2,26},{3,27},{4,28},{5,29},{6,30},{7,31},{8,0},{9,1... | collective-permute-start | bytes 393224 | tf_op jit(solution)/shard_map/ppermute | solution.py:283
  18.0 11.0 %collective-permute-start.1 = (bf16[16,4096]{1,0:T(8,128)(2,1)S(1)}, bf16[16,4096]{1,0:T(8,128)(2,1)S(1)}, u32[]{:S(2)}, u32[]{:S(2)}) collective-permute-start(bf16[16,4096]{1,0:T(8,128)(2,1)S(1)} %copy-done.13), channel_id=1, source_target_pairs={{0,16},{1,17},{2,18},{3,19},{4,20},{5,21},{6,22},{7,23},{8,24},{9,... | collective-permute-start | bytes 393224 | tf_op jit(solution)/shard_map/ppermute | solution.py:283
  18.0 10.1 %collective-permute-start = (bf16[16,4096]{1,0:T(8,128)(2,1)S(1)}, bf16[16,4096]{1,0:T(8,128)(2,1)S(1)}, u32[]{:S(2)}, u32[]{:S(2)}) collective-permute-start(bf16[16,4096]{1,0:T(8,128)(2,1)S(1)} %copy-done.13), channel_id=1, source_target_pairs={{0,8},{1,9},{2,10},{3,11},{4,12},{5,13},{6,14},{7,15},{8,16},{9,17... | collective-permute-start | bytes 393224 | tf_op jit(solution)/shard_map/ppermute | solution.py:283
  18.3 45.7 %all-to-all-start = ((bf16[32,7,16,128]{3,2,1,0:T(8,128)(2,1)}), bf16[32,7,16,128]{3,2,1,0:T(8,128)(2,1)S(1)}, u32[]{:S(2)}, u32[]{:S(2)}) async-start(bf16[32,7,16,128]{3,2,1,0:T(8,128)(2,1)} %broadcast_select_fusion), calls=%async_computation | async-start | bytes 1835008 | tf_op jit(solution)/shard_map/all_to_all | solution.py:281
  29.0 20.8 %collective-permute-start.5 = (bf16[64,4096]{1,0:T(8,128)(2,1)S(1)}, bf16[64,4096]{1,0:T(8,128)(2,1)S(1)}, u32[]{:S(2)}, u32[]{:S(2)}) collective-permute-start(bf16[64,4096]{1,0:T(8,128)(2,1)S(1)} %constant_dynamic-update-slice_fusion.rest_0_), channel_id=1, source_target_pairs={{0,6},{1,7},{2,0},{3,1},{4,2},{5,3},{6,4},{7,5},{8,14},{9,15},{10,... | collective-permute-start | bytes 1572872 | tf_op jit(solution)/shard_map/ppermute | solution.py:285
  31.8 21.0 %collective-permute-start.4 = (bf16[64,4096]{1,0:T(8,128)(2,1)S(1)}, bf16[64,4096]{1,0:T(8,128)(2,1)S(1)}, u32[]{:S(2)}, u32[]{:S(2)}) collective-permute-start(bf16[64,4096]{1,0:T(8,128)(2,1)S(1)} %constant_dynamic-update-slice_fusion.rest_0_), channel_id=1, source_target_pairs={{0,4},{1,5},{2,6},{3,7},{4,0},{5,1},{6,2},{7,3},{8,12},{9,13},{10,... | collective-permute-start | bytes 1572872 | tf_op jit(solution)/shard_map/ppermute | solution.py:285
  32.2 31.8 %collective-permute-start.3 = (bf16[64,4096]{1,0:T(8,128)(2,1)S(1)}, bf16[64,4096]{1,0:T(8,128)(2,1)S(1)}, u32[]{:S(2)}, u32[]{:S(2)}) collective-permute-start(bf16[64,4096]{1,0:T(8,128)(2,1)S(1)} %constant_dynamic-update-slice_fusion.rest_0_), channel_id=1, source_target_pairs={{0,2},{1,3},{2,4},{3,5},{4,6},{5,7},{6,0},{7,1},{8,10},{9,11},{10,... | collective-permute-start | bytes 1572872 | tf_op jit(solution)/shard_map/ppermute | solution.py:285
  33.3 32.5 %collective-permute-start.6 = (bf16[64,4096]{1,0:T(8,128)(2,1)S(1)}, bf16[64,4096]{1,0:T(8,128)(2,1)}, u32[]{:S(2)}, u32[]{:S(2)}) collective-permute-start(bf16[64,4096]{1,0:T(8,128)(2,1)S(1)} %constant_dynamic-update-slice_fusion.rest_0_), channel_id=1, source_target_pairs={{0,1},{1,0},{2,3},{3,2},{4,5},{5,4},{6,7},{7,6},{8,9},{9,8},{10,11... | collective-permute-start | bytes 1572872 | tf_op jit(solution)/shard_map/ppermute | solution.py:287
  49.8 16.0 %collective-permute-start.9 = (bf16[64,4096]{1,0:T(8,128)(2,1)S(1)}, bf16[64,4096]{1,0:T(8,128)(2,1)}, u32[]{:S(2)}, u32[]{:S(2)}) collective-permute-start(bf16[64,4096]{1,0:T(8,128)(2,1)S(1)} %collective-permute-done.5.rest_3_), channel_id=1, source_target_pairs={{0,1},{1,0},{2,3},{3,2},{4,5},{5,4},{6,7},{7,6},{8,9},{9,8},{10,11... | collective-permute-start | bytes 1572872 | tf_op jit(solution)/shard_map/ppermute | solution.py:287
  52.8 13.0 %collective-permute-start.8 = (bf16[64,4096]{1,0:T(8,128)(2,1)S(1)}, bf16[64,4096]{1,0:T(8,128)(2,1)}, u32[]{:S(2)}, u32[]{:S(2)}) collective-permute-start(bf16[64,4096]{1,0:T(8,128)(2,1)S(1)} %collective-permute-done.4.rest_2_), channel_id=1, source_target_pairs={{0,1},{1,0},{2,3},{3,2},{4,5},{5,4},{6,7},{7,6},{8,9},{9,8},{10,11... | collective-permute-start | bytes 1572872 | tf_op jit(solution)/shard_map/ppermute | solution.py:287
  64.0 2.3 collective-permute-start.7
  76.8 23.3 %collective-permute-start.10 = (bf16[12,128,128]{2,1,0:T(8,128)(2,1)S(1)}, bf16[12,128,128]{2,1,0:T(8,128)(2,1)S(1)}, u32[]{:S(2)}, u32[]{:S(2)}) collective-permute-start(bf16[12,128,128]{2,1,0:T(8,128)(2,1)S(1)} %get-tuple-element.36), channel_id=1, source_target_pairs={{0,64},{32,96},{64,128},{96,160},{128,192},{160,224},{192,0},{224,... | collective-permute-start | bytes 1179656 | tf_op jit(solution)/shard_map/ppermute | solution.py:326
  78.3 21.8 %collective-permute-start.11 = (bf16[12,128,128]{2,1,0:T(8,128)(2,1)S(1)}, bf16[12,128,128]{2,1,0:T(8,128)(2,1)S(1)}, u32[]{:S(2)}, u32[]{:S(2)}) collective-permute-start(bf16[12,128,128]{2,1,0:T(8,128)(2,1)S(1)} %get-tuple-element.37), channel_id=1, source_target_pairs={{0,128},{32,160},{64,192},{96,224},{128,0},{160,32},{192,64},{224,... | collective-permute-start | bytes 1179656 | tf_op jit(solution)/shard_map/ppermute | solution.py:326
  80.7 19.3 %collective-permute-start.12 = (bf16[12,128,128]{2,1,0:T(8,128)(2,1)S(1)}, bf16[12,128,128]{2,1,0:T(8,128)(2,1)S(1)}, u32[]{:S(2)}, u32[]{:S(2)}) collective-permute-start(bf16[12,128,128]{2,1,0:T(8,128)(2,1)S(1)} %get-tuple-element.38), channel_id=1, source_target_pairs={{0,192},{32,224},{64,0},{96,32},{128,64},{160,96},{192,128},{224,1... | collective-permute-start | bytes 1179656 | tf_op jit(solution)/shard_map/ppermute | solution.py:326
  100.4 41.5 %collective-permute-start.13 = (bf16[256,4096]{1,0:T(8,128)(2,1)}, bf16[256,4096]{1,0:T(8,128)(2,1)}, u32[]{:S(2)}, u32[]{:S(2)}) collective-permute-start(bf16[256,4096]{1,0:T(8,128)(2,1)} %get-tuple-element.39), channel_id=1, source_target_pairs={{0,1},{1,0},{2,3},{3,2},{4,5},{5,4},{6,7},{7,6},{8,9},{9,8},{10,11... | collective-permute-start | bytes 6291464 | tf_op jit(solution)/shard_map/ppermute | solution.py:348
  101.7 26.1 %collective-permute-start.18 = (bf16[16,128,128]{2,1,0:T(8,128)(2,1)}, bf16[16,128,128]{2,1,0:T(8,128)(2,1)S(1)}, u32[]{:S(2)}, u32[]{:S(2)}) collective-permute-start(bf16[16,128,128]{2,1,0:T(8,128)(2,1)} %get-tuple-element.42), channel_id=1, source_target_pairs={{0,64},{32,96},{64,128},{96,160},{128,192},{160,224},{192,0},{224,... | collective-permute-start | bytes 1572872 | tf_op jit(solution)/shard_map/ppermute | solution.py:326
  102.0 26.6 %collective-permute-start.19 = (bf16[16,128,128]{2,1,0:T(8,128)(2,1)}, bf16[16,128,128]{2,1,0:T(8,128)(2,1)S(1)}, u32[]{:S(2)}, u32[]{:S(2)}) collective-permute-start(bf16[16,128,128]{2,1,0:T(8,128)(2,1)} %get-tuple-element.43), channel_id=1, source_target_pairs={{0,128},{32,160},{64,192},{96,224},{128,0},{160,32},{192,64},{224,... | collective-permute-start | bytes 1572872 | tf_op jit(solution)/shard_map/ppermute | solution.py:326
  102.8 26.6 %collective-permute-start.20 = (bf16[16,128,128]{2,1,0:T(8,128)(2,1)}, bf16[16,128,128]{2,1,0:T(8,128)(2,1)S(1)}, u32[]{:S(2)}, u32[]{:S(2)}) collective-permute-start(bf16[16,128,128]{2,1,0:T(8,128)(2,1)} %get-tuple-element.44), channel_id=1, source_target_pairs={{0,192},{32,224},{64,0},{96,32},{128,64},{160,96},{192,128},{224,1... | collective-permute-start | bytes 1572872 | tf_op jit(solution)/shard_map/ppermute | solution.py:326
  104.4 35.6 %collective-permute-start.17 = (bf16[12,128,128]{2,1,0:T(8,128)(2,1)S(1)}, bf16[12,128,128]{2,1,0:T(8,128)(2,1)}, u32[]{:S(2)}, u32[]{:S(2)}) collective-permute-start(bf16[12,128,128]{2,1,0:T(8,128)(2,1)S(1)} %add_along_x.2), channel_id=1, source_target_pairs={{0,32},{32,0},{64,96},{96,64},{128,160},{160,128},{192,224},{224,1... | collective-permute-start | bytes 1179656 | tf_op jit(solution)/shard_map/ppermute | solution.py:331
  110.6 61.0 %all-to-all-start.1 = ((bf16[32,7,16,128]{3,2,1,0:T(8,128)(2,1)}), bf16[32,7,16,128]{3,2,1,0:T(8,128)(2,1)}, u32[]{:S(2)}, u32[]{:S(2)}) async-start(bf16[32,7,16,128]{3,2,1,0:T(8,128)(2,1)} %pad_maximum_fusion), calls=%async_computation.1 | async-start | bytes 1835008 | tf_op jit(solution)/shard_map/all_to_all | solution.py:347
  118.4 55.6 %all-gather.2.cloned.1.call-start = ((), (), s32[]{:S(2)}) async-start(), calls=%async_computation.2 | async-start | bytes 1966080 | tf_op jit(solution)/shard_map/all_gather | solution.py:337
  134.8 19.1 %collective-permute-start.24 = (bf16[16,128,128]{2,1,0:T(8,128)(2,1)S(1)}, bf16[16,128,128]{2,1,0:T(8,128)(2,1)}, u32[]{:S(2)}, u32[]{:S(2)}) collective-permute-start(bf16[16,128,128]{2,1,0:T(8,128)(2,1)S(1)} %add_along_x.3), channel_id=1, source_target_pairs={{0,32},{32,0},{64,96},{96,64},{128,160},{160,128},{192,224},{224,1... | collective-permute-start | bytes 1572872 | tf_op jit(solution)/shard_map/ppermute | solution.py:331
  144.4 24.3 %collective-permute-start.14 = (bf16[64,4096]{1,0:T(8,128)(2,1)S(1)}, bf16[64,4096]{1,0:T(8,128)(2,1)S(1)}, u32[]{:S(2)}, u32[]{:S(2)}) collective-permute-start(bf16[64,4096]{1,0:T(8,128)(2,1)S(1)} %get-tuple-element.59), channel_id=1, source_target_pairs={{0,6},{1,7},{2,0},{3,1},{4,2},{5,3},{6,4},{7,5},{8,14},{9,15},{10,... | collective-permute-start | bytes 1572872 | tf_op jit(solution)/shard_map/ppermute | solution.py:351
  145.6 23.9 %collective-permute-start.16 = (bf16[64,4096]{1,0:T(8,128)(2,1)S(1)}, bf16[64,4096]{1,0:T(8,128)(2,1)S(1)}, u32[]{:S(2)}, u32[]{:S(2)}) collective-permute-start(bf16[64,4096]{1,0:T(8,128)(2,1)S(1)} %get-tuple-element.60), channel_id=1, source_target_pairs={{0,2},{1,3},{2,4},{3,5},{4,6},{5,7},{6,0},{7,1},{8,10},{9,11},{10,... | collective-permute-start | bytes 1572872 | tf_op jit(solution)/shard_map/ppermute | solution.py:351
  146.2 24.0 %collective-permute-start.15 = (bf16[64,4096]{1,0:T(8,128)(2,1)S(1)}, bf16[64,4096]{1,0:T(8,128)(2,1)S(1)}, u32[]{:S(2)}, u32[]{:S(2)}) collective-permute-start(bf16[64,4096]{1,0:T(8,128)(2,1)S(1)} %get-tuple-element.61), channel_id=1, source_target_pairs={{0,4},{1,5},{2,6},{3,7},{4,0},{5,1},{6,2},{7,3},{8,12},{9,13},{10,... | collective-permute-start | bytes 1572872 | tf_op jit(solution)/shard_map/ppermute | solution.py:351
  155.0 24.2 %collective-permute-start.27 = (bf16[16,128,128]{2,1,0:T(8,128)(2,1)S(1)}, bf16[16,128,128]{2,1,0:T(8,128)(2,1)S(1)}, u32[]{:S(2)}, u32[]{:S(2)}) collective-permute-start(bf16[16,128,128]{2,1,0:T(8,128)(2,1)S(1)} %multiply_convert_fusion.refs_1_), channel_id=1, source_target_pairs={{0,192},{32,224},{64,0},{96,32},{128,64},{160,96},{192,128},{224,1... | collective-permute-start | bytes 1572872 | tf_op jit(solution)/shard_map/ppermute | solution.py:344
  156.0 30.4 %collective-permute-start.26 = (bf16[16,128,128]{2,1,0:T(8,128)(2,1)S(1)}, bf16[16,128,128]{2,1,0:T(8,128)(2,1)}, u32[]{:S(2)}, u32[]{:S(2)}) collective-permute-start(bf16[16,128,128]{2,1,0:T(8,128)(2,1)S(1)} %multiply_convert_fusion.refs_1_), channel_id=1, source_target_pairs={{0,128},{32,160},{64,192},{96,224},{128,0},{160,32},{192,64},{224,... | collective-permute-start | bytes 1572872 | tf_op jit(solution)/shard_map/ppermute | solution.py:344
  168.7 24.3 %collective-permute-start.25 = (bf16[16,128,128]{2,1,0:T(8,128)(2,1)S(1)}, bf16[16,128,128]{2,1,0:T(8,128)(2,1)}, u32[]{:S(2)}, u32[]{:S(2)}) collective-permute-start(bf16[16,128,128]{2,1,0:T(8,128)(2,1)S(1)} %multiply_convert_fusion.refs_1_), channel_id=1, source_target_pairs={{0,64},{32,96},{64,128},{96,160},{128,192},{160,224},{192,0},{224,... | collective-permute-start | bytes 1572872 | tf_op jit(solution)/shard_map/ppermute | solution.py:344
  175.9 50.5 %collective-permute-start.21 = (bf16[16,4096]{1,0:T(8,128)(2,1)}, bf16[16,4096]{1,0:T(8,128)(2,1)}, u32[]{:S(2)}, u32[]{:S(2)}) collective-permute-start(bf16[16,4096]{1,0:T(8,128)(2,1)} %get-tuple-element.62), channel_id=1, source_target_pairs={{0,24},{1,25},{2,26},{3,27},{4,28},{5,29},{6,30},{7,31},{8,0},{9,1... | collective-permute-start | bytes 393224 | tf_op jit(solution)/shard_map/ppermute | solution.py:357
  175.9 50.5 %collective-permute-start.23 = (bf16[16,4096]{1,0:T(8,128)(2,1)}, bf16[16,4096]{1,0:T(8,128)(2,1)}, u32[]{:S(2)}, u32[]{:S(2)}) collective-permute-start(bf16[16,4096]{1,0:T(8,128)(2,1)} %get-tuple-element.63), channel_id=1, source_target_pairs={{0,8},{1,9},{2,10},{3,11},{4,12},{5,13},{6,14},{7,15},{8,16},{9,17... | collective-permute-start | bytes 393224 | tf_op jit(solution)/shard_map/ppermute | solution.py:357
  179.3 47.2 %collective-permute-start.22 = (bf16[16,4096]{1,0:T(8,128)(2,1)}, bf16[16,4096]{1,0:T(8,128)(2,1)S(1)}, u32[]{:S(2)}, u32[]{:S(2)}) collective-permute-start(bf16[16,4096]{1,0:T(8,128)(2,1)} %get-tuple-element.64), channel_id=1, source_target_pairs={{0,16},{1,17},{2,18},{3,19},{4,20},{5,21},{6,22},{7,23},{8,24},{9,... | collective-permute-start | bytes 393224 | tf_op jit(solution)/shard_map/ppermute | solution.py:357
  (14 other events, 37.0 us)
Sparse Core Ops, SparseCore 0:
  142.0 31.9 all-gather.1

commit v3 on v2

--- a/solution.py
+++ b/solution.py
@@ -209,7 +209,7 @@
     return pl.pallas_call(
         functools.partial(place_kernel, len(parts)),
         out_shape=jax.ShapeDtypeStruct((total,) + parts[0].shape[1:], parts[0].dtype),
-        in_specs=[scalars()] + [anywhere()] * (len(args) - 1),
+        in_specs=[scalars()] + [whole()] * len(parts) + [anywhere()] * (len(args) - 1 - len(parts)),
         out_specs=anywhere(),
         input_output_aliases={} if into is None else {len(args) - 1: 0},
         scratch_shapes=[pltpu.SemaphoreType.DMA((len(parts),))],
@@ -329,7 +329,6 @@
     along = [add_transposed([piece[0]] + parts) for piece, parts in zip(pieces, got)]
     grad_sib, along[0] = lax.optimization_barrier((grad_sib, along[0]))
     other = [lax.ppermute(part, "rep", swap_h()) for part in along]
-    other[0], along[1] = lax.optimization_barrier((other[0], along[1]))
     mines = [
         ((part.astype(f32) + more.astype(f32)) * scale).astype(bf16)
         for part, more in zip(along, other)
@@ -343,7 +342,7 @@
     )
     rest = [mines[1]] + [lax.ppermute(mines[1], "rep", shift_x(d)) for d in range(1, NX)]
     acts = jnp.concatenate(acts, axis=1)
-    acts, along[0] = lax.optimization_barrier((acts, along[0]))
+    acts, mines[0] = lax.optimization_barrier((acts, mines[0]))
     returned = lax.all_to_all(acts, "fsdp", split_axis=0, concat_axis=0, tiled=True)
     from_sib = lax.ppermute(grad_sib, "fsdp", swap_c())
     pair = (grad_own.astype(f32) + from_sib.astype(f32)).astype(bf16)

time: 238 us -> 206 us (0.87); the launches traced: 235 us -> 206 us
  Pallas kernels: 60.5 us -> 29.7 us
  waiting for transfers between devices: 52.8 us -> 73.3 us
  starting transfers between devices: 75 us -> 64.7 us
  local copies, waits for them, and re-layouts: 15.2 us -> 7.31 us
    pallas_call x2, Pallas kernels: 34.6 us -> 3.71 us  [place(): pl.pallas_call(functools.partial(place_kernel, len(parts)), out_shape=jax...]
    ppermute x3, waiting for transfers between devices: 0.68 us -> 25.9 us  [per_device(): parts = [lax.ppermute(pair[d], 'fsdp', shift_y(-d)) for d in range(1, NY)]]
    ppermute x3, starting transfers between devices: 14.5 us -> 3.66 us  [per_device(): lax.ppermute(mines[1], 'rep', shift_x(d))]
    unnamed x33 -> x17, local copies, waits for them, and re-layouts: 10 us -> 2.1 us
    ppermute x6, waiting for transfers between devices: 9.37 us -> 16.5 us  [per_device(): lax.ppermute(piece[d], 'rep', shift_x(d))]
    ppermute x2, waiting for transfers between devices: 6.96 us -> 0.01 us  [per_device(): other = [lax.ppermute(part, 'rep', swap_h()) for part in along]]
    ppermute x3, waiting for transfers between devices: 6.61 us -> 0.01 us  [per_device(): lax.ppermute(mines[1], 'rep', shift_x(d))]
    ppermute x3, waiting for transfers between devices: 0.01 us -> 4.62 us  [per_device(): parts = [lax.ppermute(total[d], 'fsdp', shift_zl(-d)) for d in range(1, NZ)]]
  transfers between devices with their start and end apart: 31 -> 31, of which waited for: 11 -> 12; matrix products, arithmetic and copies ran while one was open for 6% -> 7% of each run, Pallas kernels for 22% -> 10%
where the time goes in v3:
time: 206 us
  waiting for transfers between devices  73.3 us (36%)
  starting transfers between devices  64.7 us (31%)
  Pallas kernels  29.7 us (14%)
  other arithmetic  16.1 us (8%)
  between operations  14.5 us (7%)
  local copies, waits for them, and re-layouts  7.31 us (4%)
    ppermute x3, waiting for transfers between devices, per_device(): parts = [lax.ppermute(pair[d], 'fsdp', shift_y(-d)) for d in range(1, NY)]  25.9 us
    pallas_call x2, Pallas kernels, per_device(): pl.pallas_call(functools.partial(forward_kernel, lo, slots, len(runs)), o...  25.4 us
    ppermute x3, waiting for transfers between devices, per_device(): lax.ppermute(line, 'fsdp', shift_y(d))  25 us
    ppermute x6, waiting for transfers between devices, per_device(): lax.ppermute(piece[d], 'rep', shift_x(d))  16.5 us
    ppermute x2, starting transfers between devices, per_device(): other = [lax.ppermute(part, 'rep', swap_h()) for part in along]  10.4 us
    ppermute x6, starting transfers between devices, per_device(): lax.ppermute(piece[d], 'rep', shift_x(d))  8.68 us
    all_to_all x1, starting transfers between devices, per_device(): lax.all_to_all(outgoing, 'fsdp', split_axis=0, concat_axis=0, tiled=True)  8.56 us
    all_to_all x1, starting transfers between devices, per_device(): lax.all_to_all(acts, 'fsdp', split_axis=0, concat_axis=0, tiled=True)  8.29 us
  transfers between devices with their start and end apart: 31, of which 12 were waited for; matrix products, arithmetic and copies ran while one was open for 7% of the time, Pallas kernels for 10%

profile of v3, /device:TPU:1, one launch (start us, length us, event | category | flops | bytes accessed | tf_op | source)
XLA Modules:
  0.0 205.7 jit_solution(10595859146360067728)
XLA Ops:
  12.8 5.2 %collective-permute-start.2 = (bf16[16,4096]{1,0:T(8,128)(2,1)S(1)}, bf16[16,4096]{1,0:T(8,128)(2,1)S(1)}, u32[]{:S(2)}, u32[]{:S(2)}) collective-permute-start(bf16[16,4096]{1,0:T(8,128)(2,1)S(1)} %copy-done.5), channel_id=1, source_target_pairs={{0,24},{1,25},{2,26},{3,27},{4,28},{5,29},{6,30},{7,31},{8,0},{9,1... | collective-permute-start | bytes 393224 | tf_op jit(solution)/shard_map/ppermute | solution.py:283
  18.3 8.6 %all-to-all-start = ((bf16[32,7,16,128]{3,2,1,0:T(8,128)(2,1)}), bf16[32,7,16,128]{3,2,1,0:T(8,128)(2,1)S(1)}, u32[]{:S(2)}, u32[]{:S(2)}) async-start(bf16[32,7,16,128]{3,2,1,0:T(8,128)(2,1)} %broadcast_select_fusion), calls=%async_computation | async-start | bytes 1835008 | tf_op jit(solution)/shard_map/all_to_all | solution.py:281
  29.0 2.8 %collective-permute-start.5 = (bf16[64,4096]{1,0:T(8,128)(2,1)S(1)}, bf16[64,4096]{1,0:T(8,128)(2,1)S(1)}, u32[]{:S(2)}, u32[]{:S(2)}) collective-permute-start(bf16[64,4096]{1,0:T(8,128)(2,1)S(1)} %constant_dynamic-update-slice_fusion.rest_0_), channel_id=1, source_target_pairs={{0,6},{1,7},{2,0},{3,1},{4,2},{5,3},{6,4},{7,5},{8,14},{9,15},{10,... | collective-permute-start | bytes 1572872 | tf_op jit(solution)/shard_map/ppermute | solution.py:285
  33.3 2.1 %collective-permute-start.6 = (bf16[64,4096]{1,0:T(8,128)(2,1)S(1)}, bf16[64,4096]{1,0:T(8,128)(2,1)}, u32[]{:S(2)}, u32[]{:S(2)}) collective-permute-start(bf16[64,4096]{1,0:T(8,128)(2,1)S(1)} %constant_dynamic-update-slice_fusion.rest_0_), channel_id=1, source_target_pairs={{0,1},{1,0},{2,3},{3,2},{4,5},{5,4},{6,7},{7,6},{8,9},{9,8},{10,11... | collective-permute-start | bytes 1572872 | tf_op jit(solution)/shard_map/ppermute | solution.py:287
  35.4 14.4 %collective-permute-done.5.rest_3_ = bf16[64,4096]{1,0:T(8,128)(2,1)S(1)} collective-permute-done((bf16[64,4096]{1,0:T(8,128)(2,1)S(1)}, bf16[64,4096]{1,0:T(8,128)(2,1)S(1)}, u32[]{:S(2)}, u32[]{:S(2)}) %collective-permute-start.5) | collective-permute-done | bytes 524320 | tf_op jit(solution)/shard_map/ppermute | solution.py:285
  49.8 1.7 collective-permute-start.9
  52.8 1.9 collective-permute-start.8
  54.8 9.2 %collective-permute-done.3.rest_1_ = bf16[64,4096]{1,0:T(8,128)(2,1)S(1)} collective-permute-done((bf16[64,4096]{1,0:T(8,128)(2,1)S(1)}, bf16[64,4096]{1,0:T(8,128)(2,1)S(1)}, u32[]{:S(2)}, u32[]{:S(2)}) %collective-permute-start.3) | collective-permute-done | bytes 524320 | tf_op jit(solution)/shard_map/ppermute | solution.py:285
  66.3 2.0 copy-done.1
  68.4 8.4 %forward_and_block_grad.1 = (bf16[32,3,16,128]{3,2,1,0:T(8,128)(2,1)S(1)}, bf16[512,384]{1,0:T(8,128)(2,1)S(1)}, bf16[12,128,128]{2,1,0:T(8,128)(2,1)S(1)}, bf16...) custom-call(s32[112]{0:T(128)S(1)} %reshape.260.rows_ref, ...), custom_call_target="tpu_custom_call" | custom-call | flops 1000 | bytes 1000 | tf_op jit(solution)/shard_map/forward_and_block_grad/pallas_call | solution.py:295
  78.3 2.5 %collective-permute-start.11 = (bf16[12,128,128]{2,1,0:T(8,128)(2,1)S(1)}, bf16[12,128,128]{2,1,0:T(8,128)(2,1)S(1)}, u32[]{:S(2)}, u32[]{:S(2)}) collective-permute-start(bf16[12,128,128]{2,1,0:T(8,128)(2,1)S(1)} %get-tuple-element.35), channel_id=1, source_target_pairs={{0,128},{32,160},{64,192},{96,224},{128,0},{160,32},{192,64},{224,... | collective-permute-start | bytes 1179656 | tf_op jit(solution)/shard_map/ppermute | solution.py:326
  81.9 16.9 %forward_and_grads.1 = (bf16[32,4,16,128]{3,2,1,0:T(8,128)(2,1)S(1)}, bf16[512,512]{1,0:T(8,128)(2,1)}, bf16[16,128,128]{2,1,0:T(8,128)(2,1)S(1)}, bf16[16,128,1...) custom-call(s32[112]{0:T(128)S(1)} %reshape.260.rows_ref, ...), custom_call_target="tpu_custom_call" | custom-call | flops 1000 | bytes 1000 | tf_op jit(solution)/shard_map/forward_and_grads/pallas_call | solution.py:295
  100.8 2.0 collective-permute-start.22
  104.1 5.2 %collective-permute-start.17 = (bf16[12,128,128]{2,1,0:T(8,128)(2,1)S(1)}, bf16[12,128,128]{2,1,0:T(8,128)(2,1)S(1)}, u32[]{:S(2)}, u32[]{:S(2)}) collective-permute-start(bf16[12,128,128]{2,1,0:T(8,128)(2,1)S(1)} %add_along_x.2), channel_id=1, source_target_pairs={{0,32},{32,0},{64,96},{96,64},{128,160},{160,128},{192,224},{224,1... | collective-permute-start | bytes 1179656 | tf_op jit(solution)/shard_map/ppermute | solution.py:331
  110.2 5.3 %collective-permute-done.21.refs_1_ = bf16[16,128,128]{2,1,0:T(8,128)(2,1)S(1)} collective-permute-done((bf16[16,128,128]{2,1,0:T(8,128)(2,1)S(1)}, bf16[16,128,128]{2,1,0:T(8,128)(2,1)S(1)}, u32[]{:S(2)}, u32[]{:S(2)}) %collective-permute-start.21) | collective-permute-done | bytes 524320 | tf_op jit(solution)/shard_map/ppermute | solution.py:326
  115.5 10.5 %collective-permute-done.22.refs_2_ = bf16[16,128,128]{2,1,0:T(8,128)(2,1)S(1)} collective-permute-done((bf16[16,128,128]{2,1,0:T(8,128)(2,1)S(1)}, bf16[16,128,128]{2,1,0:T(8,128)(2,1)S(1)}, u32[]{:S(2)}, u32[]{:S(2)}) %collective-permute-start.22) | collective-permute-done | bytes 524320 | tf_op jit(solution)/shard_map/ppermute | solution.py:326
  127.0 5.2 %collective-permute-start.24 = (bf16[16,128,128]{2,1,0:T(8,128)(2,1)S(1)}, bf16[16,128,128]{2,1,0:T(8,128)(2,1)}, u32[]{:S(2)}, u32[]{:S(2)}) collective-permute-start(bf16[16,128,128]{2,1,0:T(8,128)(2,1)S(1)} %add_along_x.3), channel_id=1, source_target_pairs={{0,32},{32,0},{64,96},{96,64},{128,160},{160,128},{192,224},{224,1... | collective-permute-start | bytes 1572872 | tf_op jit(solution)/shard_map/ppermute | solution.py:331
  133.2 8.3 %all-to-all-start.1 = ((bf16[32,7,16,128]{3,2,1,0:T(8,128)(2,1)}), bf16[32,7,16,128]{3,2,1,0:T(8,128)(2,1)}, u32[]{:S(2)}, u32[]{:S(2)}) async-start(bf16[32,7,16,128]{3,2,1,0:T(8,128)(2,1)} %pad_maximum_fusion), calls=%async_computation.1 | async-start | bytes 1835008 | tf_op jit(solution)/shard_map/all_to_all | solution.py:346
  141.5 2.4 %add_convert_fusion = bf16[256,4096]{1,0:T(8,128)(2,1)S(1)} fusion(bf16[256,4096]{1,0:T(8,128)(2,1)} %collective-permute-done.13, bf16[256,4096]{1,0:T(8,128)(2,1)S(1)} %copy-done.3), kind=kLoop, calls=%fused_computation.2 | loop fusion | flops 4194304 | bytes 6291456 | tf_op jit(solution)/shard_map/convert_element_type | solution.py:348
  144.0 2.9 %collective-permute-start.14 = (bf16[64,4096]{1,0:T(8,128)(2,1)S(1)}, bf16[64,4096]{1,0:T(8,128)(2,1)S(1)}, u32[]{:S(2)}, u32[]{:S(2)}) collective-permute-start(bf16[64,4096]{1,0:T(8,128)(2,1)S(1)} %get-tuple-element.55), channel_id=1, source_target_pairs={{0,6},{1,7},{2,0},{3,1},{4,2},{5,3},{6,4},{7,5},{8,14},{9,15},{10,... | collective-permute-start | bytes 1572872 | tf_op jit(solution)/shard_map/ppermute | solution.py:350
  146.9 1.8 collective-permute-start.15
  149.9 2.4 %collective-permute-start.27 = (bf16[16,128,128]{2,1,0:T(8,128)(2,1)S(1)}, bf16[16,128,128]{2,1,0:T(8,128)(2,1)S(1)}, u32[]{:S(2)}, u32[]{:S(2)}) collective-permute-start(bf16[16,128,128]{2,1,0:T(8,128)(2,1)S(1)} %multiply_convert_fusion.refs_1_), channel_id=1, source_target_pairs={{0,192},{32,224},{64,0},{96,32},{128,64},{160,96},{192,128},{224,1... | collective-permute-start | bytes 1572872 | tf_op jit(solution)/shard_map/ppermute | solution.py:343
  152.6 7.4 %collective-permute-done.14 = bf16[64,4096]{1,0:T(8,128)(2,1)S(1)} collective-permute-done((bf16[64,4096]{1,0:T(8,128)(2,1)S(1)}, bf16[64,4096]{1,0:T(8,128)(2,1)S(1)}, u32[]{:S(2)}, u32[]{:S(2)}) %collective-permute-start.14) | collective-permute-done | bytes 524320 | tf_op jit(solution)/shard_map/ppermute | solution.py:350
  161.0 3.6 %collective-permute-done.16 = bf16[64,4096]{1,0:T(8,128)(2,1)S(1)} collective-permute-done((bf16[64,4096]{1,0:T(8,128)(2,1)S(1)}, bf16[64,4096]{1,0:T(8,128)(2,1)S(1)}, u32[]{:S(2)}, u32[]{:S(2)}) %collective-permute-start.16) | collective-permute-done | bytes 524320 | tf_op jit(solution)/shard_map/ppermute | solution.py:350
  164.5 14.9 %collective-permute-done.15 = bf16[64,4096]{1,0:T(8,128)(2,1)S(1)} collective-permute-done((bf16[64,4096]{1,0:T(8,128)(2,1)S(1)}, bf16[64,4096]{1,0:T(8,128)(2,1)S(1)}, u32[]{:S(2)}, u32[]{:S(2)}) %collective-permute-start.15) | collective-permute-done | bytes 524320 | tf_op jit(solution)/shard_map/ppermute | solution.py:350
  180.5 1.9 slice_bitcast_fusion.2
  182.4 1.8 collective-permute-start.18
  184.2 1.9 gather_fusion.1
  186.0 1.7 collective-permute-start.19
  189.9 2.6 %place_blocks.3 = bf16[112,128,128]{2,1,0:T(8,128)(2,1)} custom-call(s32[4]{0:T(128)S(1)} %fusion.19.refs_0_, bf16[16,128,128]{2,1,0:T(8,128)(2,1)S(1)} %multiply_convert_fusion.refs_1_, bf16[16,128,128]{2,1,0:T(8,128)(2,1)} %collective-permute-done.25.refs_2_, ...), custom_call_target="tpu_custom_call", output_to_operand_aliasing={{}: (5, {})} | custom-call | flops 1000 | bytes 1000 | tf_op jit(solution)/shard_map/place_blocks/pallas_call | solution.py:209
  192.5 4.6 %collective-permute-done.19 = bf16[16,4096]{1,0:T(8,128)(2,1)S(1)} collective-permute-done((bf16[16,4096]{1,0:T(8,128)(2,1)}, bf16[16,4096]{1,0:T(8,128)(2,1)S(1)}, u32[]{:S(2)}, u32[]{:S(2)}) %collective-permute-start.19) | collective-permute-done | bytes 131104 | tf_op jit(solution)/shard_map/ppermute | solution.py:356
  197.1 1.8 fusion.2
  (101 shorter events, 27.4 us)
Async XLA Ops:
  12.8 16.2 %collective-permute-start.2 = (bf16[16,4096]{1,0:T(8,128)(2,1)S(1)}, bf16[16,4096]{1,0:T(8,128)(2,1)S(1)}, u32[]{:S(2)}, u32[]{:S(2)}) collective-permute-start(bf16[16,4096]{1,0:T(8,128)(2,1)S(1)} %copy-done.5), channel_id=1, source_target_pairs={{0,24},{1,25},{2,26},{3,27},{4,28},{5,29},{6,30},{7,31},{8,0},{9,1... | collective-permute-start | bytes 393224 | tf_op jit(solution)/shard_map/ppermute | solution.py:283
  18.0 11.0 %collective-permute-start.1 = (bf16[16,4096]{1,0:T(8,128)(2,1)S(1)}, bf16[16,4096]{1,0:T(8,128)(2,1)S(1)}, u32[]{:S(2)}, u32[]{:S(2)}) collective-permute-start(bf16[16,4096]{1,0:T(8,128)(2,1)S(1)} %copy-done.5), channel_id=1, source_target_pairs={{0,16},{1,17},{2,18},{3,19},{4,20},{5,21},{6,22},{7,23},{8,24},{9,... | collective-permute-start | bytes 393224 | tf_op jit(solution)/shard_map/ppermute | solution.py:283
  18.0 10.1 %collective-permute-start = (bf16[16,4096]{1,0:T(8,128)(2,1)S(1)}, bf16[16,4096]{1,0:T(8,128)(2,1)S(1)}, u32[]{:S(2)}, u32[]{:S(2)}) collective-permute-start(bf16[16,4096]{1,0:T(8,128)(2,1)S(1)} %copy-done.5), channel_id=1, source_target_pairs={{0,8},{1,9},{2,10},{3,11},{4,12},{5,13},{6,14},{7,15},{8,16},{9,17... | collective-permute-start | bytes 393224 | tf_op jit(solution)/shard_map/ppermute | solution.py:283
  18.3 45.7 %all-to-all-start = ((bf16[32,7,16,128]{3,2,1,0:T(8,128)(2,1)}), bf16[32,7,16,128]{3,2,1,0:T(8,128)(2,1)S(1)}, u32[]{:S(2)}, u32[]{:S(2)}) async-start(bf16[32,7,16,128]{3,2,1,0:T(8,128)(2,1)} %broadcast_select_fusion), calls=%async_computation | async-start | bytes 1835008 | tf_op jit(solution)/shard_map/all_to_all | solution.py:281
  26.8 153.7 %all-gather.2.cloned.1.call-start = ((), (), s32[]{:S(2)}) async-start(), calls=%async_computation.2 | async-start | bytes 1966080 | tf_op jit(solution)/shard_map/all_gather | solution.py:336
  29.0 20.8 %collective-permute-start.5 = (bf16[64,4096]{1,0:T(8,128)(2,1)S(1)}, bf16[64,4096]{1,0:T(8,128)(2,1)S(1)}, u32[]{:S(2)}, u32[]{:S(2)}) collective-permute-start(bf16[64,4096]{1,0:T(8,128)(2,1)S(1)} %constant_dynamic-update-slice_fusion.rest_0_), channel_id=1, source_target_pairs={{0,6},{1,7},{2,0},{3,1},{4,2},{5,3},{6,4},{7,5},{8,14},{9,15},{10,... | collective-permute-start | bytes 1572872 | tf_op jit(solution)/shard_map/ppermute | solution.py:285
  31.8 21.0 %collective-permute-start.4 = (bf16[64,4096]{1,0:T(8,128)(2,1)S(1)}, bf16[64,4096]{1,0:T(8,128)(2,1)S(1)}, u32[]{:S(2)}, u32[]{:S(2)}) collective-permute-start(bf16[64,4096]{1,0:T(8,128)(2,1)S(1)} %constant_dynamic-update-slice_fusion.rest_0_), channel_id=1, source_target_pairs={{0,4},{1,5},{2,6},{3,7},{4,0},{5,1},{6,2},{7,3},{8,12},{9,13},{10,... | collective-permute-start | bytes 1572872 | tf_op jit(solution)/shard_map/ppermute | solution.py:285
  32.2 31.8 %collective-permute-start.3 = (bf16[64,4096]{1,0:T(8,128)(2,1)S(1)}, bf16[64,4096]{1,0:T(8,128)(2,1)S(1)}, u32[]{:S(2)}, u32[]{:S(2)}) collective-permute-start(bf16[64,4096]{1,0:T(8,128)(2,1)S(1)} %constant_dynamic-update-slice_fusion.rest_0_), channel_id=1, source_target_pairs={{0,2},{1,3},{2,4},{3,5},{4,6},{5,7},{6,0},{7,1},{8,10},{9,11},{10,... | collective-permute-start | bytes 1572872 | tf_op jit(solution)/shard_map/ppermute | solution.py:285
  33.3 32.5 %collective-permute-start.6 = (bf16[64,4096]{1,0:T(8,128)(2,1)S(1)}, bf16[64,4096]{1,0:T(8,128)(2,1)}, u32[]{:S(2)}, u32[]{:S(2)}) collective-permute-start(bf16[64,4096]{1,0:T(8,128)(2,1)S(1)} %constant_dynamic-update-slice_fusion.rest_0_), channel_id=1, source_target_pairs={{0,1},{1,0},{2,3},{3,2},{4,5},{5,4},{6,7},{7,6},{8,9},{9,8},{10,11... | collective-permute-start | bytes 1572872 | tf_op jit(solution)/shard_map/ppermute | solution.py:287
  49.8 16.0 %collective-permute-start.9 = (bf16[64,4096]{1,0:T(8,128)(2,1)S(1)}, bf16[64,4096]{1,0:T(8,128)(2,1)}, u32[]{:S(2)}, u32[]{:S(2)}) collective-permute-start(bf16[64,4096]{1,0:T(8,128)(2,1)S(1)} %collective-permute-done.5.rest_3_), channel_id=1, source_target_pairs={{0,1},{1,0},{2,3},{3,2},{4,5},{5,4},{6,7},{7,6},{8,9},{9,8},{10,11... | collective-permute-start | bytes 1572872 | tf_op jit(solution)/shard_map/ppermute | solution.py:287
  52.8 13.0 %collective-permute-start.8 = (bf16[64,4096]{1,0:T(8,128)(2,1)S(1)}, bf16[64,4096]{1,0:T(8,128)(2,1)}, u32[]{:S(2)}, u32[]{:S(2)}) collective-permute-start(bf16[64,4096]{1,0:T(8,128)(2,1)S(1)} %collective-permute-done.4.rest_2_), channel_id=1, source_target_pairs={{0,1},{1,0},{2,3},{3,2},{4,5},{5,4},{6,7},{7,6},{8,9},{9,8},{10,11... | collective-permute-start | bytes 1572872 | tf_op jit(solution)/shard_map/ppermute | solution.py:287
  64.0 2.3 %collective-permute-start.7 = (bf16[64,4096]{1,0:T(8,128)(2,1)S(1)}, bf16[64,4096]{1,0:T(8,128)(2,1)}, u32[]{:S(2)}, u32[]{:S(2)}) collective-permute-start(bf16[64,4096]{1,0:T(8,128)(2,1)S(1)} %collective-permute-done.3.rest_1_), channel_id=1, source_target_pairs={{0,1},{1,0},{2,3},{3,2},{4,5},{5,4},{6,7},{7,6},{8,9},{9,8},{10,11... | collective-permute-start | bytes 1572872 | tf_op jit(solution)/shard_map/ppermute | solution.py:287
  76.8 22.0 %collective-permute-start.10 = (bf16[12,128,128]{2,1,0:T(8,128)(2,1)S(1)}, bf16[12,128,128]{2,1,0:T(8,128)(2,1)S(1)}, u32[]{:S(2)}, u32[]{:S(2)}) collective-permute-start(bf16[12,128,128]{2,1,0:T(8,128)(2,1)S(1)} %get-tuple-element.34), channel_id=1, source_target_pairs={{0,64},{32,96},{64,128},{96,160},{128,192},{160,224},{192,0},{224,... | collective-permute-start | bytes 1179656 | tf_op jit(solution)/shard_map/ppermute | solution.py:326
  78.3 20.6 %collective-permute-start.11 = (bf16[12,128,128]{2,1,0:T(8,128)(2,1)S(1)}, bf16[12,128,128]{2,1,0:T(8,128)(2,1)S(1)}, u32[]{:S(2)}, u32[]{:S(2)}) collective-permute-start(bf16[12,128,128]{2,1,0:T(8,128)(2,1)S(1)} %get-tuple-element.35), channel_id=1, source_target_pairs={{0,128},{32,160},{64,192},{96,224},{128,0},{160,32},{192,64},{224,... | collective-permute-start | bytes 1179656 | tf_op jit(solution)/shard_map/ppermute | solution.py:326
  80.7 18.1 %collective-permute-start.12 = (bf16[12,128,128]{2,1,0:T(8,128)(2,1)S(1)}, bf16[12,128,128]{2,1,0:T(8,128)(2,1)S(1)}, u32[]{:S(2)}, u32[]{:S(2)}) collective-permute-start(bf16[12,128,128]{2,1,0:T(8,128)(2,1)S(1)} %get-tuple-element.36), channel_id=1, source_target_pairs={{0,192},{32,224},{64,0},{96,32},{128,64},{160,96},{192,128},{224,1... | collective-permute-start | bytes 1179656 | tf_op jit(solution)/shard_map/ppermute | solution.py:326
  98.8 28.2 %copy-start.2 = (bf16[256,4096]{1,0:T(8,128)(2,1)}, bf16[256,4096]{1,0:T(8,128)(2,1)S(1)}, u32[]{:S(2)}) copy-start(bf16[256,4096]{1,0:T(8,128)(2,1)S(1)} %get-tuple-element.31) | copy-start | bytes 6291460
  99.2 42.3 %collective-permute-start.13 = (bf16[256,4096]{1,0:T(8,128)(2,1)}, bf16[256,4096]{1,0:T(8,128)(2,1)}, u32[]{:S(2)}, u32[]{:S(2)}) collective-permute-start(bf16[256,4096]{1,0:T(8,128)(2,1)} %get-tuple-element.37), channel_id=1, source_target_pairs={{0,1},{1,0},{2,3},{3,2},{4,5},{5,4},{6,7},{7,6},{8,9},{9,8},{10,11... | collective-permute-start | bytes 6291464 | tf_op jit(solution)/shard_map/ppermute | solution.py:347
  100.4 15.1 %collective-permute-start.21 = (bf16[16,128,128]{2,1,0:T(8,128)(2,1)S(1)}, bf16[16,128,128]{2,1,0:T(8,128)(2,1)S(1)}, u32[]{:S(2)}, u32[]{:S(2)}) collective-permute-start(bf16[16,128,128]{2,1,0:T(8,128)(2,1)S(1)} %get-tuple-element.45), channel_id=1, source_target_pairs={{0,64},{32,96},{64,128},{96,160},{128,192},{160,224},{192,0},{224,... | collective-permute-start | bytes 1572872 | tf_op jit(solution)/shard_map/ppermute | solution.py:326
  100.8 25.3 %collective-permute-start.22 = (bf16[16,128,128]{2,1,0:T(8,128)(2,1)S(1)}, bf16[16,128,128]{2,1,0:T(8,128)(2,1)S(1)}, u32[]{:S(2)}, u32[]{:S(2)}) collective-permute-start(bf16[16,128,128]{2,1,0:T(8,128)(2,1)S(1)} %get-tuple-element.46), channel_id=1, source_target_pairs={{0,128},{32,160},{64,192},{96,224},{128,0},{160,32},{192,64},{224,... | collective-permute-start | bytes 1572872 | tf_op jit(solution)/shard_map/ppermute | solution.py:326
  102.8 23.9 %collective-permute-start.23 = (bf16[16,128,128]{2,1,0:T(8,128)(2,1)S(1)}, bf16[16,128,128]{2,1,0:T(8,128)(2,1)S(1)}, u32[]{:S(2)}, u32[]{:S(2)}) collective-permute-start(bf16[16,128,128]{2,1,0:T(8,128)(2,1)S(1)} %get-tuple-element.47), channel_id=1, source_target_pairs={{0,192},{32,224},{64,0},{96,32},{128,64},{160,96},{192,128},{224,1... | collective-permute-start | bytes 1572872 | tf_op jit(solution)/shard_map/ppermute | solution.py:326
  104.1 28.2 %collective-permute-start.17 = (bf16[12,128,128]{2,1,0:T(8,128)(2,1)S(1)}, bf16[12,128,128]{2,1,0:T(8,128)(2,1)S(1)}, u32[]{:S(2)}, u32[]{:S(2)}) collective-permute-start(bf16[12,128,128]{2,1,0:T(8,128)(2,1)S(1)} %add_along_x.2), channel_id=1, source_target_pairs={{0,32},{32,0},{64,96},{96,64},{128,160},{160,128},{192,224},{224,1... | collective-permute-start | bytes 1179656 | tf_op jit(solution)/shard_map/ppermute | solution.py:331
  127.0 21.6 %collective-permute-start.24 = (bf16[16,128,128]{2,1,0:T(8,128)(2,1)S(1)}, bf16[16,128,128]{2,1,0:T(8,128)(2,1)}, u32[]{:S(2)}, u32[]{:S(2)}) collective-permute-start(bf16[16,128,128]{2,1,0:T(8,128)(2,1)S(1)} %add_along_x.3), channel_id=1, source_target_pairs={{0,32},{32,0},{64,96},{96,64},{128,160},{160,128},{192,224},{224,1... | collective-permute-start | bytes 1572872 | tf_op jit(solution)/shard_map/ppermute | solution.py:331
  133.2 47.3 %all-to-all-start.1 = ((bf16[32,7,16,128]{3,2,1,0:T(8,128)(2,1)}), bf16[32,7,16,128]{3,2,1,0:T(8,128)(2,1)}, u32[]{:S(2)}, u32[]{:S(2)}) async-start(bf16[32,7,16,128]{3,2,1,0:T(8,128)(2,1)} %pad_maximum_fusion), calls=%async_computation.1 | async-start | bytes 1835008 | tf_op jit(solution)/shard_map/all_to_all | solution.py:346
  144.0 16.1 %collective-permute-start.14 = (bf16[64,4096]{1,0:T(8,128)(2,1)S(1)}, bf16[64,4096]{1,0:T(8,128)(2,1)S(1)}, u32[]{:S(2)}, u32[]{:S(2)}) collective-permute-start(bf16[64,4096]{1,0:T(8,128)(2,1)S(1)} %get-tuple-element.55), channel_id=1, source_target_pairs={{0,6},{1,7},{2,0},{3,1},{4,2},{5,3},{6,4},{7,5},{8,14},{9,15},{10,... | collective-permute-start | bytes 1572872 | tf_op jit(solution)/shard_map/ppermute | solution.py:350
  146.9 17.7 %collective-permute-start.16 = (bf16[64,4096]{1,0:T(8,128)(2,1)S(1)}, bf16[64,4096]{1,0:T(8,128)(2,1)S(1)}, u32[]{:S(2)}, u32[]{:S(2)}) collective-permute-start(bf16[64,4096]{1,0:T(8,128)(2,1)S(1)} %get-tuple-element.56), channel_id=1, source_target_pairs={{0,2},{1,3},{2,4},{3,5},{4,6},{5,7},{6,0},{7,1},{8,10},{9,11},{10,... | collective-permute-start | bytes 1572872 | tf_op jit(solution)/shard_map/ppermute | solution.py:350
  146.9 32.5 %collective-permute-start.15 = (bf16[64,4096]{1,0:T(8,128)(2,1)S(1)}, bf16[64,4096]{1,0:T(8,128)(2,1)S(1)}, u32[]{:S(2)}, u32[]{:S(2)}) collective-permute-start(bf16[64,4096]{1,0:T(8,128)(2,1)S(1)} %get-tuple-element.57), channel_id=1, source_target_pairs={{0,4},{1,5},{2,6},{3,7},{4,0},{5,1},{6,2},{7,3},{8,12},{9,13},{10,... | collective-permute-start | bytes 1572872 | tf_op jit(solution)/shard_map/ppermute | solution.py:350
  149.9 36.1 %collective-permute-start.27 = (bf16[16,128,128]{2,1,0:T(8,128)(2,1)S(1)}, bf16[16,128,128]{2,1,0:T(8,128)(2,1)S(1)}, u32[]{:S(2)}, u32[]{:S(2)}) collective-permute-start(bf16[16,128,128]{2,1,0:T(8,128)(2,1)S(1)} %multiply_convert_fusion.refs_1_), channel_id=1, source_target_pairs={{0,192},{32,224},{64,0},{96,32},{128,64},{160,96},{192,128},{224,1... | collective-permute-start | bytes 1572872 | tf_op jit(solution)/shard_map/ppermute | solution.py:343
  152.3 37.5 %collective-permute-start.26 = (bf16[16,128,128]{2,1,0:T(8,128)(2,1)S(1)}, bf16[16,128,128]{2,1,0:T(8,128)(2,1)}, u32[]{:S(2)}, u32[]{:S(2)}) collective-permute-start(bf16[16,128,128]{2,1,0:T(8,128)(2,1)S(1)} %multiply_convert_fusion.refs_1_), channel_id=1, source_target_pairs={{0,128},{32,160},{64,192},{96,224},{128,0},{160,32},{192,64},{224,... | collective-permute-start | bytes 1572872 | tf_op jit(solution)/shard_map/ppermute | solution.py:343
  160.1 29.8 %collective-permute-start.25 = (bf16[16,128,128]{2,1,0:T(8,128)(2,1)S(1)}, bf16[16,128,128]{2,1,0:T(8,128)(2,1)}, u32[]{:S(2)}, u32[]{:S(2)}) collective-permute-start(bf16[16,128,128]{2,1,0:T(8,128)(2,1)S(1)} %multiply_convert_fusion.refs_1_), channel_id=1, source_target_pairs={{0,64},{32,96},{64,128},{96,160},{128,192},{160,224},{192,0},{224,... | collective-permute-start | bytes 1572872 | tf_op jit(solution)/shard_map/ppermute | solution.py:343
  182.4 10.0 %collective-permute-start.18 = (bf16[16,4096]{1,0:T(8,128)(2,1)}, bf16[16,4096]{1,0:T(8,128)(2,1)}, u32[]{:S(2)}, u32[]{:S(2)}) collective-permute-start(bf16[16,4096]{1,0:T(8,128)(2,1)} %get-tuple-element.58), channel_id=1, source_target_pairs={{0,24},{1,25},{2,26},{3,27},{4,28},{5,29},{6,30},{7,31},{8,0},{9,1... | collective-permute-start | bytes 393224 | tf_op jit(solution)/shard_map/ppermute | solution.py:356
  184.2 8.3 %collective-permute-start.20 = (bf16[16,4096]{1,0:T(8,128)(2,1)}, bf16[16,4096]{1,0:T(8,128)(2,1)}, u32[]{:S(2)}, u32[]{:S(2)}) collective-permute-start(bf16[16,4096]{1,0:T(8,128)(2,1)} %get-tuple-element.59), channel_id=1, source_target_pairs={{0,8},{1,9},{2,10},{3,11},{4,12},{5,13},{6,14},{7,15},{8,16},{9,17... | collective-permute-start | bytes 393224 | tf_op jit(solution)/shard_map/ppermute | solution.py:356
  186.0 11.0 %collective-permute-start.19 = (bf16[16,4096]{1,0:T(8,128)(2,1)}, bf16[16,4096]{1,0:T(8,128)(2,1)S(1)}, u32[]{:S(2)}, u32[]{:S(2)}) collective-permute-start(bf16[16,4096]{1,0:T(8,128)(2,1)} %get-tuple-element.60), channel_id=1, source_target_pairs={{0,16},{1,17},{2,18},{3,19},{4,20},{5,21},{6,22},{7,23},{8,24},{9,... | collective-permute-start | bytes 393224 | tf_op jit(solution)/shard_map/ppermute | solution.py:356
  (6 other events, 41.5 us)
Sparse Core Ops, SparseCore 0:
  133.3 33.3 all-gather.1

commit v4 on v3

--- a/solution.py
+++ b/solution.py
@@ -329,21 +329,6 @@
     along = [add_transposed([piece[0]] + parts) for piece, parts in zip(pieces, got)]
     grad_sib, along[0] = lax.optimization_barrier((grad_sib, along[0]))
     other = [lax.ppermute(part, "rep", swap_h()) for part in along]
-    mines = [
-        ((part.astype(f32) + more.astype(f32)) * scale).astype(bf16)
-        for part, more in zip(along, other)
-    ]
-    gathered = lax.all_gather(
-        mines[0],
-        "rep",
-        axis=0,
-        tiled=True,
-        axis_index_groups=[[x * NH + h for x in range(NX)] for h in range(NH)],
-    )
-    rest = [mines[1]] + [lax.ppermute(mines[1], "rep", shift_x(d)) for d in range(1, NX)]
-    acts = jnp.concatenate(acts, axis=1)
-    acts, mines[0] = lax.optimization_barrier((acts, mines[0]))
-    returned = lax.all_to_all(acts, "fsdp", split_axis=0, concat_axis=0, tiled=True)
     from_sib = lax.ppermute(grad_sib, "fsdp", swap_c())
     pair = (grad_own.astype(f32) + from_sib.astype(f32)).astype(bf16)
     pair = pair.reshape(NY, NZ * tok_dev, model_width)
@@ -352,12 +337,25 @@
     for part in parts:
         total = total + part.astype(f32)
     total = total.astype(bf16).reshape(NZ, tok_dev, model_width)
-    total, gathered, returned = lax.optimization_barrier((total, gathered, returned))
+
+    acts, total = lax.optimization_barrier((jnp.concatenate(acts, axis=1), total))
+    mines, gathered = [], []
+    for part, more in zip(along, other):
+        if gathered:
+            more, gathered[0], total = lax.optimization_barrier((more, gathered[0], total))
+        mine = ((part.astype(f32) + more.astype(f32)) * scale).astype(bf16)
+        mines.append(mine)
+        gathered.append(
+            [mine] + [lax.ppermute(mine, "rep", shift_x(d)) for d in range(1, NX)]
+        )
+    returned = lax.all_to_all(acts, "fsdp", split_axis=0, concat_axis=0, tiled=True)
     parts = [lax.ppermute(total[d], "fsdp", shift_zl(-d)) for d in range(1, NZ)]
+    parts, gathered[1], returned = lax.optimization_barrier((parts, gathered[1], returned))
     input_grad = total[0].astype(f32)
     for part in parts:
         input_grad = input_grad + part.astype(f32)
     input_grad = input_grad.astype(bf16)
+
 
     panel_first = jnp.sum(member * first_panel[None, :], axis=1)
     panel_slot = panel_owner * slot_count + panel_ids - panel_first
@@ -366,11 +364,13 @@
     )
     activation_out = jnp.transpose(act_panels, (1, 0, 2)).reshape(tok_dev, panel_count * block_size)
 
-    blocks_all = slot_count * keep_count
-    block_grad = place(jnp.zeros((1,), jnp.int32), blocks_all, [gathered])
+    block_grad = None
     away = jnp.arange(NX, dtype=jnp.int32)
-    starts = sets[1][0] * keep_count + ((x_index - away) % NX) * rest[0].shape[0]
-    block_grad = place(starts.astype(jnp.int32), blocks_all, rest, block_grad)
+    for (lo, hi), parts in zip(sets, gathered):
+        starts = lo * keep_count + ((x_index - away) % NX) * parts[0].shape[0]
+        block_grad = place(
+            starts.astype(jnp.int32), slot_count * keep_count, parts, block_grad
+        )
     return (activation_out, input_grad, block_grad.reshape(blocks.shape))
 
 

time: 206 us -> 191 us (0.927)
  between operations: 14.5 us -> 1.31 us
  starting transfers between devices: 64.7 us -> 77.2 us
  waiting for transfers between devices: 73.3 us -> 61.2 us
  other arithmetic: 16.1 us -> 12.7 us
    ppermute x3, waiting for transfers between devices: 25.9 us -> 4.56 us  [per_device(): parts = [lax.ppermute(pair[d], 'fsdp', shift_y(-d)) for d in range(1, NY)]]
    ppermute x3, starting transfers between devices: 3.45 us -> 20.6 us  [per_device(): parts = [lax.ppermute(total[d], 'fsdp', shift_zl(-d)) for d in range(1, NZ)]]
    ppermute x3 -> x6, waiting for transfers between devices: 0.01 us -> 5.04 us  [per_device(): lax.ppermute(mine, 'rep', shift_x(d))]
    ppermute x3, starting transfers between devices: 4.65 us -> 0.65 us  [per_device(): parts = [lax.ppermute(pair[d], 'fsdp', shift_y(-d)) for d in range(1, NY)]]
    ppermute x3 -> x6, starting transfers between devices: 3.66 us -> 7.66 us  [per_device(): lax.ppermute(mine, 'rep', shift_x(d))]
    ppermute x4, starting transfers between devices: 6.4 us -> 2.78 us  [per_device(): runs = along_y + [lax.ppermute(run, 'fsdp', swap_c()) for run in along_y]]
    ppermute x3, waiting for transfers between devices: 4.62 us -> 7.28 us  [per_device(): parts = [lax.ppermute(total[d], 'fsdp', shift_zl(-d)) for d in range(1, NZ)]]
    all_to_all x1, starting transfers between devices: 8.29 us -> 5.91 us  [per_device(): lax.all_to_all(acts, 'fsdp', split_axis=0, concat_axis=0, tiled=True)]
  transfers between devices with their start and end apart: 31 -> 33, of which waited for: 12 -> 9; matrix products, arithmetic and copies ran while one was open for 7% -> 4% of each run, Pallas kernels for 10% -> 10%
where the time goes in v4:
time: 191 us; the launch traced here: 190 us
  starting transfers between devices  77.2 us (40%)
  waiting for transfers between devices  61.2 us (32%)
  Pallas kernels  28.9 us (15%)
  other arithmetic  12.7 us (7%)
  local copies, waits for them, and re-layouts  8.79 us (5%)
    ppermute x3, waiting for transfers between devices, per_device(): lax.ppermute(line, 'fsdp', shift_y(d))  27.1 us
    pallas_call x2, Pallas kernels, per_device(): pl.pallas_call(functools.partial(forward_kernel, lo, slots, len(runs)), o...  24.7 us
    ppermute x3, starting transfers between devices, per_device(): parts = [lax.ppermute(total[d], 'fsdp', shift_zl(-d)) for d in range(1, NZ)]  20.6 us
    ppermute x6, waiting for transfers between devices, per_device(): lax.ppermute(piece[d], 'rep', shift_x(d))  14.9 us
    ppermute x2, starting transfers between devices, per_device(): other = [lax.ppermute(part, 'rep', swap_h()) for part in along]  11.2 us
    ppermute x6, starting transfers between devices, per_device(): lax.ppermute(piece[d], 'rep', shift_x(d))  9.39 us
    ppermute x6, starting transfers between devices, per_device(): lax.ppermute(mine, 'rep', shift_x(d))  7.66 us
    ppermute x3, waiting for transfers between devices, per_device(): parts = [lax.ppermute(total[d], 'fsdp', shift_zl(-d)) for d in range(1, NZ)]  7.28 us
  transfers between devices with their start and end apart: 33, of which 9 were waited for; matrix products, arithmetic and copies ran while one was open for 4% of the time, Pallas kernels for 10%

profile of v4, /device:TPU:1, one launch (start us, length us, event | category | flops | bytes accessed | tf_op | source)
XLA Modules:
  0.0 190.1 jit_solution(1900199323371626361)
XLA Ops:
  6.3 2.5 %collective-permute-start = (bf16[16,4096]{1,0:T(8,128)(2,1)S(1)}, bf16[16,4096]{1,0:T(8,128)(2,1)S(1)}, u32[]{:S(2)}, u32[]{:S(2)}) collective-permute-start(bf16[16,4096]{1,0:T(8,128)(2,1)S(1)} %copy-done.6), channel_id=1, source_target_pairs={{0,8},{1,9},{2,10},{3,11},{4,12},{5,13},{6,14},{7,15},{8,16},{9,17... | collective-permute-start | bytes 393224 | tf_op jit(solution)/shard_map/ppermute | solution.py:283
  8.7 3.0 %collective-permute-start.1 = (bf16[16,4096]{1,0:T(8,128)(2,1)S(1)}, bf16[16,4096]{1,0:T(8,128)(2,1)S(1)}, u32[]{:S(2)}, u32[]{:S(2)}) collective-permute-start(bf16[16,4096]{1,0:T(8,128)(2,1)S(1)} %copy-done.6), channel_id=1, source_target_pairs={{0,16},{1,17},{2,18},{3,19},{4,20},{5,21},{6,22},{7,23},{8,24},{9,... | collective-permute-start | bytes 393224 | tf_op jit(solution)/shard_map/ppermute | solution.py:283
  12.5 6.6 %all-to-all-start = ((bf16[32,7,16,128]{3,2,1,0:T(8,128)(2,1)}), bf16[32,7,16,128]{3,2,1,0:T(8,128)(2,1)S(1)}, u32[]{:S(2)}, u32[]{:S(2)}) async-start(bf16[32,7,16,128]{3,2,1,0:T(8,128)(2,1)} %broadcast_select_fusion), calls=%async_computation | async-start | bytes 1835008 | tf_op jit(solution)/shard_map/all_to_all | solution.py:281
  21.1 1.3 collective-permute-start.3
  22.4 2.6 %collective-permute-start.4 = (bf16[64,4096]{1,0:T(8,128)(2,1)S(1)}, bf16[64,4096]{1,0:T(8,128)(2,1)S(1)}, u32[]{:S(2)}, u32[]{:S(2)}) collective-permute-start(bf16[64,4096]{1,0:T(8,128)(2,1)S(1)} %constant_dynamic-update-slice_fusion.rest_0_), channel_id=1, source_target_pairs={{0,4},{1,5},{2,6},{3,7},{4,0},{5,1},{6,2},{7,3},{8,12},{9,13},{10,... | collective-permute-start | bytes 1572872 | tf_op jit(solution)/shard_map/ppermute | solution.py:285
  26.6 1.5 collective-permute-start.6
  28.1 27.1 %collective-permute-done.4.rest_2_ = bf16[64,4096]{1,0:T(8,128)(2,1)S(1)} collective-permute-done((bf16[64,4096]{1,0:T(8,128)(2,1)S(1)}, bf16[64,4096]{1,0:T(8,128)(2,1)S(1)}, u32[]{:S(2)}, u32[]{:S(2)}) %collective-permute-start.4) | collective-permute-done | bytes 524320 | tf_op jit(solution)/shard_map/ppermute | solution.py:285
  59.2 2.0 %copy-done.1 = bf16[7,16,128,128]{3,2,1,0:T(8,128)(2,1)S(1)} copy-done((bf16[7,16,128,128]{3,2,1,0:T(8,128)(2,1)S(1)}, bf16[7,16,128,128]{3,2,1,0:T(8,128)(2,1)}, u32[]{:S(2)}) %copy-start.1) | copy-done | bytes 3670040
  61.2 8.4 %forward_and_block_grad.1 = (bf16[32,3,16,128]{3,2,1,0:T(8,128)(2,1)S(1)}, bf16[512,384]{1,0:T(8,128)(2,1)S(1)}, bf16[12,128,128]{2,1,0:T(8,128)(2,1)S(1)}, bf16...) custom-call(s32[112]{0:T(128)S(1)} %reshape.260.rows_ref, ...), custom_call_target="tpu_custom_call" | custom-call | flops 1000 | bytes 1000 | tf_op jit(solution)/shard_map/forward_and_block_grad/pallas_call | solution.py:295
  69.6 1.5 collective-permute-start.14
  71.1 2.5 %collective-permute-start.15 = (bf16[12,128,128]{2,1,0:T(8,128)(2,1)S(1)}, bf16[12,128,128]{2,1,0:T(8,128)(2,1)S(1)}, u32[]{:S(2)}, u32[]{:S(2)}) collective-permute-start(bf16[12,128,128]{2,1,0:T(8,128)(2,1)S(1)} %get-tuple-element.50), channel_id=1, source_target_pairs={{0,128},{32,160},{64,192},{96,224},{128,0},{160,32},{192,64},{224,... | collective-permute-start | bytes 1179656 | tf_op jit(solution)/shard_map/ppermute | solution.py:326
  74.7 16.2 %forward_and_grads.1 = (bf16[32,4,16,128]{3,2,1,0:T(8,128)(2,1)S(1)}, bf16[512,512]{1,0:T(8,128)(2,1)}, bf16[16,128,128]{2,1,0:T(8,128)(2,1)S(1)}, bf16[16,128,1...) custom-call(s32[112]{0:T(128)S(1)} %reshape.260.rows_ref, ...), custom_call_target="tpu_custom_call" | custom-call | flops 1000 | bytes 1000 | tf_op jit(solution)/shard_map/forward_and_grads/pallas_call | solution.py:295
  91.3 1.3 collective-permute-start.21
  93.5 2.1 %collective-permute-start.11 = (bf16[16,128,128]{2,1,0:T(8,128)(2,1)S(1)}, bf16[16,128,128]{2,1,0:T(8,128)(2,1)S(1)}, u32[]{:S(2)}, u32[]{:S(2)}) collective-permute-start(bf16[16,128,128]{2,1,0:T(8,128)(2,1)S(1)} %get-tuple-element.45), channel_id=1, source_target_pairs={{0,128},{32,160},{64,192},{96,224},{128,0},{160,32},{192,64},{224,... | collective-permute-start | bytes 1572872 | tf_op jit(solution)/shard_map/ppermute | solution.py:326
  96.9 5.5 %collective-permute-start.17 = (bf16[12,128,128]{2,1,0:T(8,128)(2,1)S(1)}, bf16[12,128,128]{2,1,0:T(8,128)(2,1)S(1)}, u32[]{:S(2)}, u32[]{:S(2)}) collective-permute-start(bf16[12,128,128]{2,1,0:T(8,128)(2,1)S(1)} %add_along_x.3), channel_id=1, source_target_pairs={{0,32},{32,0},{64,96},{96,64},{128,160},{160,128},{192,224},{224,1... | collective-permute-start | bytes 1179656 | tf_op jit(solution)/shard_map/ppermute | solution.py:331
  103.4 3.8 %collective-permute-done.10.refs_1_ = bf16[16,128,128]{2,1,0:T(8,128)(2,1)S(1)} collective-permute-done((bf16[16,128,128]{2,1,0:T(8,128)(2,1)S(1)}, bf16[16,128,128]{2,1,0:T(8,128)(2,1)S(1)}, u32[]{:S(2)}, u32[]{:S(2)}) %collective-permute-start.10) | collective-permute-done | bytes 524320 | tf_op jit(solution)/shard_map/ppermute | solution.py:326
  107.8 11.0 %collective-permute-done.11.refs_2_ = bf16[16,128,128]{2,1,0:T(8,128)(2,1)S(1)} collective-permute-done((bf16[16,128,128]{2,1,0:T(8,128)(2,1)S(1)}, bf16[16,128,128]{2,1,0:T(8,128)(2,1)S(1)}, u32[]{:S(2)}, u32[]{:S(2)}) %collective-permute-start.11) | collective-permute-done | bytes 524320 | tf_op jit(solution)/shard_map/ppermute | solution.py:326
  120.2 5.6 %collective-permute-start.13 = (bf16[16,128,128]{2,1,0:T(8,128)(2,1)S(1)}, bf16[16,128,128]{2,1,0:T(8,128)(2,1)S(1)}, u32[]{:S(2)}, u32[]{:S(2)}) collective-permute-start(bf16[16,128,128]{2,1,0:T(8,128)(2,1)S(1)} %add_along_x.2), channel_id=1, source_target_pairs={{0,32},{32,0},{64,96},{96,64},{128,160},{160,128},{192,224},{224,1... | collective-permute-start | bytes 1572872 | tf_op jit(solution)/shard_map/ppermute | solution.py:331
  127.0 2.3 %collective-permute-start.19 = (bf16[12,128,128]{2,1,0:T(8,128)(2,1)S(1)}, bf16[12,128,128]{2,1,0:T(8,128)(2,1)S(1)}, u32[]{:S(2)}, u32[]{:S(2)}) collective-permute-start(bf16[12,128,128]{2,1,0:T(8,128)(2,1)S(1)} %multiply_convert_fusion.1.refs_1_), channel_id=1, source_target_pairs={{0,128},{32,160},{64,192},{96,224},{128,0},{160,32},{192,64},{224,... | collective-permute-start | bytes 1179656 | tf_op jit(solution)/shard_map/ppermute | solution.py:349
  129.5 4.6 %collective-permute-done.24 = bf16[64,4096]{1,0:T(8,128)(2,1)S(1)} collective-permute-done((bf16[64,4096]{1,0:T(8,128)(2,1)S(1)}, bf16[64,4096]{1,0:T(8,128)(2,1)S(1)}, u32[]{:S(2)}, u32[]{:S(2)}) %collective-permute-start.24) | collective-permute-done | bytes 524320 | tf_op jit(solution)/shard_map/ppermute | solution.py:335
  135.1 5.9 %all-to-all-start.1 = ((bf16[32,7,16,128]{3,2,1,0:T(8,128)(2,1)}), bf16[32,7,16,128]{3,2,1,0:T(8,128)(2,1)}, u32[]{:S(2)}, u32[]{:S(2)}) async-start(bf16[32,7,16,128]{3,2,1,0:T(8,128)(2,1)} %pad_maximum_fusion), calls=%async_computation.1 | async-start | bytes 1835008 | tf_op jit(solution)/shard_map/all_to_all | solution.py:351
  141.0 5.0 %collective-permute-done.19.refs_3_ = bf16[12,128,128]{2,1,0:T(8,128)(2,1)S(1)} collective-permute-done((bf16[12,128,128]{2,1,0:T(8,128)(2,1)S(1)}, bf16[12,128,128]{2,1,0:T(8,128)(2,1)S(1)}, u32[]{:S(2)}, u32[]{:S(2)}) %collective-permute-start.19) | collective-permute-done | bytes 393248 | tf_op jit(solution)/shard_map/ppermute | solution.py:349
  147.6 1.3 collective-permute-start.28
  148.9 2.9 %collective-permute-start.29 = (bf16[16,128,128]{2,1,0:T(8,128)(2,1)S(1)}, bf16[16,128,128]{2,1,0:T(8,128)(2,1)S(1)}, u32[]{:S(2)}, u32[]{:S(2)}) collective-permute-start(bf16[16,128,128]{2,1,0:T(8,128)(2,1)S(1)} %multiply_convert_fusion.refs_1_), channel_id=1, source_target_pairs={{0,128},{32,160},{64,192},{96,224},{128,0},{160,32},{192,64},{224,... | collective-permute-start | bytes 1572872 | tf_op jit(solution)/shard_map/ppermute | solution.py:349
  152.8 3.1 %collective-permute-start.25 = (bf16[16,4096]{1,0:T(8,128)(2,1)S(1)}, bf16[16,4096]{1,0:T(8,128)(2,1)S(1)}, u32[]{:S(2)}, u32[]{:S(2)}) collective-permute-start(bf16[16,4096]{1,0:T(8,128)(2,1)S(1)} %get-tuple-element.84), channel_id=1, source_target_pairs={{0,24},{1,25},{2,26},{3,27},{4,28},{5,29},{6,30},{7,31},{8,0},{9,1... | collective-permute-start | bytes 393224 | tf_op jit(solution)/shard_map/ppermute | solution.py:352
  155.9 3.4 %collective-permute-start.26 = (bf16[16,4096]{1,0:T(8,128)(2,1)S(1)}, bf16[16,4096]{1,0:T(8,128)(2,1)}, u32[]{:S(2)}, u32[]{:S(2)}) collective-permute-start(bf16[16,4096]{1,0:T(8,128)(2,1)S(1)} %get-tuple-element.83), channel_id=1, source_target_pairs={{0,16},{1,17},{2,18},{3,19},{4,20},{5,21},{6,22},{7,23},{8,24},{9,... | collective-permute-start | bytes 393224 | tf_op jit(solution)/shard_map/ppermute | solution.py:352
  159.3 7.3 %collective-permute-done.25 = bf16[16,4096]{1,0:T(8,128)(2,1)S(1)} collective-permute-done((bf16[16,4096]{1,0:T(8,128)(2,1)S(1)}, bf16[16,4096]{1,0:T(8,128)(2,1)S(1)}, u32[]{:S(2)}, u32[]{:S(2)}) %collective-permute-start.25) | collective-permute-done | bytes 131104 | tf_op jit(solution)/shard_map/ppermute | solution.py:352
  166.6 14.0 %collective-permute-start.27 = (bf16[16,4096]{1,0:T(8,128)(2,1)S(1)}, bf16[16,4096]{1,0:T(8,128)(2,1)}, u32[]{:S(2)}, u32[]{:S(2)}) collective-permute-start(bf16[16,4096]{1,0:T(8,128)(2,1)S(1)} %get-tuple-element.82), channel_id=1, source_target_pairs={{0,8},{1,9},{2,10},{3,11},{4,12},{5,13},{6,14},{7,15},{8,16},{9,17... | collective-permute-start | bytes 393224 | tf_op jit(solution)/shard_map/ppermute | solution.py:352
  181.7 1.7 place_blocks.2.refs_5_
  183.5 1.9 gather_fusion.1
  186.3 1.8 fusion.2
  188.1 1.9 place_blocks.3
  (107 shorter events, 27.1 us)
Async XLA Ops:
  6.3 14.0 %collective-permute-start = (bf16[16,4096]{1,0:T(8,128)(2,1)S(1)}, bf16[16,4096]{1,0:T(8,128)(2,1)S(1)}, u32[]{:S(2)}, u32[]{:S(2)}) collective-permute-start(bf16[16,4096]{1,0:T(8,128)(2,1)S(1)} %copy-done.6), channel_id=1, source_target_pairs={{0,8},{1,9},{2,10},{3,11},{4,12},{5,13},{6,14},{7,15},{8,16},{9,17... | collective-permute-start | bytes 393224 | tf_op jit(solution)/shard_map/ppermute | solution.py:283
  8.7 12.3 %collective-permute-start.1 = (bf16[16,4096]{1,0:T(8,128)(2,1)S(1)}, bf16[16,4096]{1,0:T(8,128)(2,1)S(1)}, u32[]{:S(2)}, u32[]{:S(2)}) collective-permute-start(bf16[16,4096]{1,0:T(8,128)(2,1)S(1)} %copy-done.6), channel_id=1, source_target_pairs={{0,16},{1,17},{2,18},{3,19},{4,20},{5,21},{6,22},{7,23},{8,24},{9,... | collective-permute-start | bytes 393224 | tf_op jit(solution)/shard_map/ppermute | solution.py:283
  11.7 9.4 %collective-permute-start.2 = (bf16[16,4096]{1,0:T(8,128)(2,1)S(1)}, bf16[16,4096]{1,0:T(8,128)(2,1)S(1)}, u32[]{:S(2)}, u32[]{:S(2)}) collective-permute-start(bf16[16,4096]{1,0:T(8,128)(2,1)S(1)} %copy-done.6), channel_id=1, source_target_pairs={{0,24},{1,25},{2,26},{3,27},{4,28},{5,29},{6,30},{7,31},{8,0},{9,1... | collective-permute-start | bytes 393224 | tf_op jit(solution)/shard_map/ppermute | solution.py:283
  12.5 43.5 %all-to-all-start = ((bf16[32,7,16,128]{3,2,1,0:T(8,128)(2,1)}), bf16[32,7,16,128]{3,2,1,0:T(8,128)(2,1)S(1)}, u32[]{:S(2)}, u32[]{:S(2)}) async-start(bf16[32,7,16,128]{3,2,1,0:T(8,128)(2,1)} %broadcast_select_fusion), calls=%async_computation | async-start | bytes 1835008 | tf_op jit(solution)/shard_map/all_to_all | solution.py:281
  21.1 34.9 %collective-permute-start.3 = (bf16[64,4096]{1,0:T(8,128)(2,1)S(1)}, bf16[64,4096]{1,0:T(8,128)(2,1)S(1)}, u32[]{:S(2)}, u32[]{:S(2)}) collective-permute-start(bf16[64,4096]{1,0:T(8,128)(2,1)S(1)} %constant_dynamic-update-slice_fusion.rest_0_), channel_id=1, source_target_pairs={{0,2},{1,3},{2,4},{3,5},{4,6},{5,7},{6,0},{7,1},{8,10},{9,11},{10,... | collective-permute-start | bytes 1572872 | tf_op jit(solution)/shard_map/ppermute | solution.py:285
  22.4 32.8 %collective-permute-start.4 = (bf16[64,4096]{1,0:T(8,128)(2,1)S(1)}, bf16[64,4096]{1,0:T(8,128)(2,1)S(1)}, u32[]{:S(2)}, u32[]{:S(2)}) collective-permute-start(bf16[64,4096]{1,0:T(8,128)(2,1)S(1)} %constant_dynamic-update-slice_fusion.rest_0_), channel_id=1, source_target_pairs={{0,4},{1,5},{2,6},{3,7},{4,0},{5,1},{6,2},{7,3},{8,12},{9,13},{10,... | collective-permute-start | bytes 1572872 | tf_op jit(solution)/shard_map/ppermute | solution.py:285
  25.1 30.9 %collective-permute-start.5 = (bf16[64,4096]{1,0:T(8,128)(2,1)S(1)}, bf16[64,4096]{1,0:T(8,128)(2,1)S(1)}, u32[]{:S(2)}, u32[]{:S(2)}) collective-permute-start(bf16[64,4096]{1,0:T(8,128)(2,1)S(1)} %constant_dynamic-update-slice_fusion.rest_0_), channel_id=1, source_target_pairs={{0,6},{1,7},{2,0},{3,1},{4,2},{5,3},{6,4},{7,5},{8,14},{9,15},{10,... | collective-permute-start | bytes 1572872 | tf_op jit(solution)/shard_map/ppermute | solution.py:285
  26.6 31.0 %collective-permute-start.6 = (bf16[64,4096]{1,0:T(8,128)(2,1)S(1)}, bf16[64,4096]{1,0:T(8,128)(2,1)}, u32[]{:S(2)}, u32[]{:S(2)}) collective-permute-start(bf16[64,4096]{1,0:T(8,128)(2,1)S(1)} %constant_dynamic-update-slice_fusion.rest_0_), channel_id=1, source_target_pairs={{0,1},{1,0},{2,3},{3,2},{4,5},{5,4},{6,7},{7,6},{8,9},{9,8},{10,11... | collective-permute-start | bytes 1572872 | tf_op jit(solution)/shard_map/ppermute | solution.py:287
  55.2 2.4 %collective-permute-start.8 = (bf16[64,4096]{1,0:T(8,128)(2,1)S(1)}, bf16[64,4096]{1,0:T(8,128)(2,1)}, u32[]{:S(2)}, u32[]{:S(2)}) collective-permute-start(bf16[64,4096]{1,0:T(8,128)(2,1)S(1)} %collective-permute-done.4.rest_2_), channel_id=1, source_target_pairs={{0,1},{1,0},{2,3},{3,2},{4,5},{5,4},{6,7},{7,6},{8,9},{9,8},{10,11... | collective-permute-start | bytes 1572872 | tf_op jit(solution)/shard_map/ppermute | solution.py:287
  56.0 3.1 %collective-permute-start.7 = (bf16[64,4096]{1,0:T(8,128)(2,1)S(1)}, bf16[64,4096]{1,0:T(8,128)(2,1)}, u32[]{:S(2)}, u32[]{:S(2)}) collective-permute-start(bf16[64,4096]{1,0:T(8,128)(2,1)S(1)} %collective-permute-done.3.rest_1_), channel_id=1, source_target_pairs={{0,1},{1,0},{2,3},{3,2},{4,5},{5,4},{6,7},{7,6},{8,9},{9,8},{10,11... | collective-permute-start | bytes 1572872 | tf_op jit(solution)/shard_map/ppermute | solution.py:287
  69.6 21.3 %collective-permute-start.14 = (bf16[12,128,128]{2,1,0:T(8,128)(2,1)S(1)}, bf16[12,128,128]{2,1,0:T(8,128)(2,1)S(1)}, u32[]{:S(2)}, u32[]{:S(2)}) collective-permute-start(bf16[12,128,128]{2,1,0:T(8,128)(2,1)S(1)} %get-tuple-element.49), channel_id=1, source_target_pairs={{0,64},{32,96},{64,128},{96,160},{128,192},{160,224},{192,0},{224,... | collective-permute-start | bytes 1179656 | tf_op jit(solution)/shard_map/ppermute | solution.py:326
  71.1 19.9 %collective-permute-start.15 = (bf16[12,128,128]{2,1,0:T(8,128)(2,1)S(1)}, bf16[12,128,128]{2,1,0:T(8,128)(2,1)S(1)}, u32[]{:S(2)}, u32[]{:S(2)}) collective-permute-start(bf16[12,128,128]{2,1,0:T(8,128)(2,1)S(1)} %get-tuple-element.50), channel_id=1, source_target_pairs={{0,128},{32,160},{64,192},{96,224},{128,0},{160,32},{192,64},{224,... | collective-permute-start | bytes 1179656 | tf_op jit(solution)/shard_map/ppermute | solution.py:326
  73.5 17.4 %collective-permute-start.16 = (bf16[12,128,128]{2,1,0:T(8,128)(2,1)S(1)}, bf16[12,128,128]{2,1,0:T(8,128)(2,1)S(1)}, u32[]{:S(2)}, u32[]{:S(2)}) collective-permute-start(bf16[12,128,128]{2,1,0:T(8,128)(2,1)S(1)} %get-tuple-element.51), channel_id=1, source_target_pairs={{0,192},{32,224},{64,0},{96,32},{128,64},{160,96},{192,128},{224,1... | collective-permute-start | bytes 1179656 | tf_op jit(solution)/shard_map/ppermute | solution.py:326
  91.3 11.2 %collective-permute-start.21 = (bf16[256,4096]{1,0:T(8,128)(2,1)S(1)}, bf16[256,4096]{1,0:T(8,128)(2,1)S(1)}, u32[]{:S(2)}, u32[]{:S(2)}) collective-permute-start(bf16[256,4096]{1,0:T(8,128)(2,1)S(1)} %get-tuple-element.56), channel_id=1, source_target_pairs={{0,1},{1,0},{2,3},{3,2},{4,5},{5,4},{6,7},{7,6},{8,9},{9,8},{10,11... | collective-permute-start | bytes 6291464 | tf_op jit(solution)/shard_map/ppermute | solution.py:332
  92.6 14.7 %collective-permute-start.10 = (bf16[16,128,128]{2,1,0:T(8,128)(2,1)S(1)}, bf16[16,128,128]{2,1,0:T(8,128)(2,1)S(1)}, u32[]{:S(2)}, u32[]{:S(2)}) collective-permute-start(bf16[16,128,128]{2,1,0:T(8,128)(2,1)S(1)} %get-tuple-element.44), channel_id=1, source_target_pairs={{0,64},{32,96},{64,128},{96,160},{128,192},{160,224},{192,0},{224,... | collective-permute-start | bytes 1572872 | tf_op jit(solution)/shard_map/ppermute | solution.py:326
  93.5 25.4 %collective-permute-start.11 = (bf16[16,128,128]{2,1,0:T(8,128)(2,1)S(1)}, bf16[16,128,128]{2,1,0:T(8,128)(2,1)S(1)}, u32[]{:S(2)}, u32[]{:S(2)}) collective-permute-start(bf16[16,128,128]{2,1,0:T(8,128)(2,1)S(1)} %get-tuple-element.45), channel_id=1, source_target_pairs={{0,128},{32,160},{64,192},{96,224},{128,0},{160,32},{192,64},{224,... | collective-permute-start | bytes 1572872 | tf_op jit(solution)/shard_map/ppermute | solution.py:326
  95.6 24.3 %collective-permute-start.12 = (bf16[16,128,128]{2,1,0:T(8,128)(2,1)S(1)}, bf16[16,128,128]{2,1,0:T(8,128)(2,1)S(1)}, u32[]{:S(2)}, u32[]{:S(2)}) collective-permute-start(bf16[16,128,128]{2,1,0:T(8,128)(2,1)S(1)} %get-tuple-element.46), channel_id=1, source_target_pairs={{0,192},{32,224},{64,0},{96,32},{128,64},{160,96},{192,128},{224,1... | collective-permute-start | bytes 1572872 | tf_op jit(solution)/shard_map/ppermute | solution.py:326
  96.9 29.0 %collective-permute-start.17 = (bf16[12,128,128]{2,1,0:T(8,128)(2,1)S(1)}, bf16[12,128,128]{2,1,0:T(8,128)(2,1)S(1)}, u32[]{:S(2)}, u32[]{:S(2)}) collective-permute-start(bf16[12,128,128]{2,1,0:T(8,128)(2,1)S(1)} %add_along_x.3), channel_id=1, source_target_pairs={{0,32},{32,0},{64,96},{96,64},{128,160},{160,128},{192,224},{224,1... | collective-permute-start | bytes 1179656 | tf_op jit(solution)/shard_map/ppermute | solution.py:331
  103.3 23.6 %collective-permute-start.22 = (bf16[64,4096]{1,0:T(8,128)(2,1)S(1)}, bf16[64,4096]{1,0:T(8,128)(2,1)S(1)}, u32[]{:S(2)}, u32[]{:S(2)}) collective-permute-start(bf16[64,4096]{1,0:T(8,128)(2,1)S(1)} %get-tuple-element.79), channel_id=1, source_target_pairs={{0,6},{1,7},{2,0},{3,1},{4,2},{5,3},{6,4},{7,5},{8,14},{9,15},{10,... | collective-permute-start | bytes 1572872 | tf_op jit(solution)/shard_map/ppermute | solution.py:335
  107.3 22.0 %collective-permute-start.23 = (bf16[64,4096]{1,0:T(8,128)(2,1)S(1)}, bf16[64,4096]{1,0:T(8,128)(2,1)S(1)}, u32[]{:S(2)}, u32[]{:S(2)}) collective-permute-start(bf16[64,4096]{1,0:T(8,128)(2,1)S(1)} %get-tuple-element.81), channel_id=1, source_target_pairs={{0,4},{1,5},{2,6},{3,7},{4,0},{5,1},{6,2},{7,3},{8,12},{9,13},{10,... | collective-permute-start | bytes 1572872 | tf_op jit(solution)/shard_map/ppermute | solution.py:335
  118.8 15.2 %collective-permute-start.24 = (bf16[64,4096]{1,0:T(8,128)(2,1)S(1)}, bf16[64,4096]{1,0:T(8,128)(2,1)S(1)}, u32[]{:S(2)}, u32[]{:S(2)}) collective-permute-start(bf16[64,4096]{1,0:T(8,128)(2,1)S(1)} %get-tuple-element.80), channel_id=1, source_target_pairs={{0,2},{1,3},{2,4},{3,5},{4,6},{5,7},{6,0},{7,1},{8,10},{9,11},{10,... | collective-permute-start | bytes 1572872 | tf_op jit(solution)/shard_map/ppermute | solution.py:335
  120.2 20.8 %collective-permute-start.13 = (bf16[16,128,128]{2,1,0:T(8,128)(2,1)S(1)}, bf16[16,128,128]{2,1,0:T(8,128)(2,1)S(1)}, u32[]{:S(2)}, u32[]{:S(2)}) collective-permute-start(bf16[16,128,128]{2,1,0:T(8,128)(2,1)S(1)} %add_along_x.2), channel_id=1, source_target_pairs={{0,32},{32,0},{64,96},{96,64},{128,160},{160,128},{192,224},{224,1... | collective-permute-start | bytes 1572872 | tf_op jit(solution)/shard_map/ppermute | solution.py:331
  126.0 15.0 %collective-permute-start.18 = (bf16[12,128,128]{2,1,0:T(8,128)(2,1)S(1)}, bf16[12,128,128]{2,1,0:T(8,128)(2,1)S(1)}, u32[]{:S(2)}, u32[]{:S(2)}) collective-permute-start(bf16[12,128,128]{2,1,0:T(8,128)(2,1)S(1)} %multiply_convert_fusion.1.refs_1_), channel_id=1, source_target_pairs={{0,64},{32,96},{64,128},{96,160},{128,192},{160,224},{192,0},{224,... | collective-permute-start | bytes 1179656 | tf_op jit(solution)/shard_map/ppermute | solution.py:349
  127.0 19.1 %collective-permute-start.19 = (bf16[12,128,128]{2,1,0:T(8,128)(2,1)S(1)}, bf16[12,128,128]{2,1,0:T(8,128)(2,1)S(1)}, u32[]{:S(2)}, u32[]{:S(2)}) collective-permute-start(bf16[12,128,128]{2,1,0:T(8,128)(2,1)S(1)} %multiply_convert_fusion.1.refs_1_), channel_id=1, source_target_pairs={{0,128},{32,160},{64,192},{96,224},{128,0},{160,32},{192,64},{224,... | collective-permute-start | bytes 1179656 | tf_op jit(solution)/shard_map/ppermute | solution.py:349
  129.2 17.6 %collective-permute-start.20 = (bf16[12,128,128]{2,1,0:T(8,128)(2,1)S(1)}, bf16[12,128,128]{2,1,0:T(8,128)(2,1)S(1)}, u32[]{:S(2)}, u32[]{:S(2)}) collective-permute-start(bf16[12,128,128]{2,1,0:T(8,128)(2,1)S(1)} %multiply_convert_fusion.1.refs_1_), channel_id=1, source_target_pairs={{0,192},{32,224},{64,0},{96,32},{128,64},{160,96},{192,128},{224,1... | collective-permute-start | bytes 1179656 | tf_op jit(solution)/shard_map/ppermute | solution.py:349
  135.1 48.4 %all-to-all-start.1 = ((bf16[32,7,16,128]{3,2,1,0:T(8,128)(2,1)}), bf16[32,7,16,128]{3,2,1,0:T(8,128)(2,1)}, u32[]{:S(2)}, u32[]{:S(2)}) async-start(bf16[32,7,16,128]{3,2,1,0:T(8,128)(2,1)} %pad_maximum_fusion), calls=%async_computation.1 | async-start | bytes 1835008 | tf_op jit(solution)/shard_map/all_to_all | solution.py:351
  147.6 35.9 %collective-permute-start.28 = (bf16[16,128,128]{2,1,0:T(8,128)(2,1)S(1)}, bf16[16,128,128]{2,1,0:T(8,128)(2,1)S(1)}, u32[]{:S(2)}, u32[]{:S(2)}) collective-permute-start(bf16[16,128,128]{2,1,0:T(8,128)(2,1)S(1)} %multiply_convert_fusion.refs_1_), channel_id=1, source_target_pairs={{0,64},{32,96},{64,128},{96,160},{128,192},{160,224},{192,0},{224,... | collective-permute-start | bytes 1572872 | tf_op jit(solution)/shard_map/ppermute | solution.py:349
  148.9 34.6 %collective-permute-start.29 = (bf16[16,128,128]{2,1,0:T(8,128)(2,1)S(1)}, bf16[16,128,128]{2,1,0:T(8,128)(2,1)S(1)}, u32[]{:S(2)}, u32[]{:S(2)}) collective-permute-start(bf16[16,128,128]{2,1,0:T(8,128)(2,1)S(1)} %multiply_convert_fusion.refs_1_), channel_id=1, source_target_pairs={{0,128},{32,160},{64,192},{96,224},{128,0},{160,32},{192,64},{224,... | collective-permute-start | bytes 1572872 | tf_op jit(solution)/shard_map/ppermute | solution.py:349
  151.8 31.7 %collective-permute-start.30 = (bf16[16,128,128]{2,1,0:T(8,128)(2,1)S(1)}, bf16[16,128,128]{2,1,0:T(8,128)(2,1)S(1)}, u32[]{:S(2)}, u32[]{:S(2)}) collective-permute-start(bf16[16,128,128]{2,1,0:T(8,128)(2,1)S(1)} %multiply_convert_fusion.refs_1_), channel_id=1, source_target_pairs={{0,192},{32,224},{64,0},{96,32},{128,64},{160,96},{192,128},{224,1... | collective-permute-start | bytes 1572872 | tf_op jit(solution)/shard_map/ppermute | solution.py:349
  152.8 13.8 %collective-permute-start.25 = (bf16[16,4096]{1,0:T(8,128)(2,1)S(1)}, bf16[16,4096]{1,0:T(8,128)(2,1)S(1)}, u32[]{:S(2)}, u32[]{:S(2)}) collective-permute-start(bf16[16,4096]{1,0:T(8,128)(2,1)S(1)} %get-tuple-element.84), channel_id=1, source_target_pairs={{0,24},{1,25},{2,26},{3,27},{4,28},{5,29},{6,30},{7,31},{8,0},{9,1... | collective-permute-start | bytes 393224 | tf_op jit(solution)/shard_map/ppermute | solution.py:352
  155.9 27.5 %collective-permute-start.26 = (bf16[16,4096]{1,0:T(8,128)(2,1)S(1)}, bf16[16,4096]{1,0:T(8,128)(2,1)}, u32[]{:S(2)}, u32[]{:S(2)}) collective-permute-start(bf16[16,4096]{1,0:T(8,128)(2,1)S(1)} %get-tuple-element.83), channel_id=1, source_target_pairs={{0,16},{1,17},{2,18},{3,19},{4,20},{5,21},{6,22},{7,23},{8,24},{9,... | collective-permute-start | bytes 393224 | tf_op jit(solution)/shard_map/ppermute | solution.py:352
  166.6 16.8 %collective-permute-start.27 = (bf16[16,4096]{1,0:T(8,128)(2,1)S(1)}, bf16[16,4096]{1,0:T(8,128)(2,1)}, u32[]{:S(2)}, u32[]{:S(2)}) collective-permute-start(bf16[16,4096]{1,0:T(8,128)(2,1)S(1)} %get-tuple-element.82), channel_id=1, source_target_pairs={{0,8},{1,9},{2,10},{3,11},{4,12},{5,13},{6,14},{7,15},{8,16},{9,17... | collective-permute-start | bytes 393224 | tf_op jit(solution)/shard_map/ppermute | solution.py:352
  (9 other events, 61.6 us)

commit v5 on v4

--- a/solution.py
+++ b/solution.py
@@ -70,7 +70,7 @@
     rows, width = tok_ref.shape
     row_blocks = width // bs
     part = rows // pieces
-    tile, span = 512, 1024
+    tile, span = 512, 2048
 
     get_blocks = pltpu.make_async_copy(
         blocks_hbm.at[pl.ds(first - base, base + slots)], blocks_ref, in_sems.at[0]
@@ -142,7 +142,7 @@
     if first > 0:
         dzs_ref[:, : base * bs] = earlier_ref[...]
         dzs_ref[:, base * bs :] = dz_ref[...]
-        half, wide = rows // 2, 512
+        half, wide = rows // 2, 1024
 
         def back_step(t, carry):
             at = pl.multiple_of(t * wide, wide)

time: 191 us -> 190 us (level)
  transfers between devices with their start and end apart: 33 -> 33, of which waited for: 9 -> 10; matrix products, arithmetic and copies ran while one was open for 4% -> 4% of each run, Pallas kernels for 10% -> 9%
where the time goes in v5:
time: 190 us
  starting transfers between devices  77.3 us (41%)
  waiting for transfers between devices  62.2 us (33%)
  Pallas kernels  27.5 us (14%)
  other arithmetic  12.7 us (7%)
  local copies, waits for them, and re-layouts  8.79 us (5%)
    ppermute x3, waiting for transfers between devices, per_device(): lax.ppermute(line, 'fsdp', shift_y(d))  27.1 us
    pallas_call x2, Pallas kernels, per_device(): pl.pallas_call(functools.partial(forward_kernel, lo, slots, len(runs)), o...  23.2 us
    ppermute x3, starting transfers between devices, per_device(): parts = [lax.ppermute(total[d], 'fsdp', shift_zl(-d)) for d in range(1, NZ)]  20.4 us
    ppermute x6, waiting for transfers between devices, per_device(): lax.ppermute(piece[d], 'rep', shift_x(d))  15.8 us
    ppermute x2, starting transfers between devices, per_device(): other = [lax.ppermute(part, 'rep', swap_h()) for part in along]  11.2 us
    ppermute x6, starting transfers between devices, per_device(): lax.ppermute(piece[d], 'rep', shift_x(d))  9.53 us
    ppermute x6, starting transfers between devices, per_device(): lax.ppermute(mine, 'rep', shift_x(d))  7.66 us
    ppermute x3, waiting for transfers between devices, per_device(): parts = [lax.ppermute(total[d], 'fsdp', shift_zl(-d)) for d in range(1, NZ)]  7.43 us
  transfers between devices with their start and end apart: 33, of which 10 were waited for; matrix products, arithmetic and copies ran while one was open for 4% of the time, Pallas kernels for 9%

profile of v5, /device:TPU:1, one launch (start us, length us, event | category | flops | bytes accessed | tf_op | source)
XLA Modules:
  0.0 189.8 jit_solution(15101206083443846879)
XLA Ops:
  6.3 2.5 %collective-permute-start = (bf16[16,4096]{1,0:T(8,128)(2,1)S(1)}, bf16[16,4096]{1,0:T(8,128)(2,1)S(1)}, u32[]{:S(2)}, u32[]{:S(2)}) collective-permute-start(bf16[16,4096]{1,0:T(8,128)(2,1)S(1)} %copy-done.6), channel_id=1, source_target_pairs={{0,8},{1,9},{2,10},{3,11},{4,12},{5,13},{6,14},{7,15},{8,16},{9,17... | collective-permute-start | bytes 393224 | tf_op jit(solution)/shard_map/ppermute | solution.py:283
  8.7 3.0 %collective-permute-start.1 = (bf16[16,4096]{1,0:T(8,128)(2,1)S(1)}, bf16[16,4096]{1,0:T(8,128)(2,1)S(1)}, u32[]{:S(2)}, u32[]{:S(2)}) collective-permute-start(bf16[16,4096]{1,0:T(8,128)(2,1)S(1)} %copy-done.6), channel_id=1, source_target_pairs={{0,16},{1,17},{2,18},{3,19},{4,20},{5,21},{6,22},{7,23},{8,24},{9,... | collective-permute-start | bytes 393224 | tf_op jit(solution)/shard_map/ppermute | solution.py:283
  12.5 6.6 %all-to-all-start = ((bf16[32,7,16,128]{3,2,1,0:T(8,128)(2,1)}), bf16[32,7,16,128]{3,2,1,0:T(8,128)(2,1)S(1)}, u32[]{:S(2)}, u32[]{:S(2)}) async-start(bf16[32,7,16,128]{3,2,1,0:T(8,128)(2,1)} %broadcast_select_fusion), calls=%async_computation | async-start | bytes 1835008 | tf_op jit(solution)/shard_map/all_to_all | solution.py:281
  21.1 1.3 collective-permute-start.3
  22.4 2.6 %collective-permute-start.4 = (bf16[64,4096]{1,0:T(8,128)(2,1)S(1)}, bf16[64,4096]{1,0:T(8,128)(2,1)S(1)}, u32[]{:S(2)}, u32[]{:S(2)}) collective-permute-start(bf16[64,4096]{1,0:T(8,128)(2,1)S(1)} %constant_dynamic-update-slice_fusion.rest_0_), channel_id=1, source_target_pairs={{0,4},{1,5},{2,6},{3,7},{4,0},{5,1},{6,2},{7,3},{8,12},{9,13},{10,... | collective-permute-start | bytes 1572872 | tf_op jit(solution)/shard_map/ppermute | solution.py:285
  26.6 1.5 collective-permute-start.6
  28.1 27.1 %collective-permute-done.4.rest_2_ = bf16[64,4096]{1,0:T(8,128)(2,1)S(1)} collective-permute-done((bf16[64,4096]{1,0:T(8,128)(2,1)S(1)}, bf16[64,4096]{1,0:T(8,128)(2,1)S(1)}, u32[]{:S(2)}, u32[]{:S(2)}) %collective-permute-start.4) | collective-permute-done | bytes 524320 | tf_op jit(solution)/shard_map/ppermute | solution.py:285
  59.2 2.0 %copy-done.1 = bf16[7,16,128,128]{3,2,1,0:T(8,128)(2,1)S(1)} copy-done((bf16[7,16,128,128]{3,2,1,0:T(8,128)(2,1)S(1)}, bf16[7,16,128,128]{3,2,1,0:T(8,128)(2,1)}, u32[]{:S(2)}) %copy-start.1) | copy-done | bytes 3670040
  61.2 8.1 %forward_and_block_grad.1 = (bf16[32,3,16,128]{3,2,1,0:T(8,128)(2,1)S(1)}, bf16[512,384]{1,0:T(8,128)(2,1)S(1)}, bf16[12,128,128]{2,1,0:T(8,128)(2,1)S(1)}, bf16...) custom-call(s32[112]{0:T(128)S(1)} %reshape.260.rows_ref, ...), custom_call_target="tpu_custom_call" | custom-call | flops 1000 | bytes 1000 | tf_op jit(solution)/shard_map/forward_and_block_grad/pallas_call | solution.py:295
  69.3 1.5 collective-permute-start.14
  70.8 2.4 %collective-permute-start.15 = (bf16[12,128,128]{2,1,0:T(8,128)(2,1)S(1)}, bf16[12,128,128]{2,1,0:T(8,128)(2,1)S(1)}, u32[]{:S(2)}, u32[]{:S(2)}) collective-permute-start(bf16[12,128,128]{2,1,0:T(8,128)(2,1)S(1)} %get-tuple-element.50), channel_id=1, source_target_pairs={{0,128},{32,160},{64,192},{96,224},{128,0},{160,32},{192,64},{224,... | collective-permute-start | bytes 1179656 | tf_op jit(solution)/shard_map/ppermute | solution.py:326
  74.4 15.1 %forward_and_grads.1 = (bf16[32,4,16,128]{3,2,1,0:T(8,128)(2,1)S(1)}, bf16[512,512]{1,0:T(8,128)(2,1)}, bf16[16,128,128]{2,1,0:T(8,128)(2,1)S(1)}, bf16[16,128,1...) custom-call(s32[112]{0:T(128)S(1)} %reshape.260.rows_ref, ...), custom_call_target="tpu_custom_call" | custom-call | flops 1000 | bytes 1000 | tf_op jit(solution)/shard_map/forward_and_grads/pallas_call | solution.py:295
  90.8 1.3 collective-permute-start.21
  93.2 2.1 %collective-permute-start.11 = (bf16[16,128,128]{2,1,0:T(8,128)(2,1)S(1)}, bf16[16,128,128]{2,1,0:T(8,128)(2,1)S(1)}, u32[]{:S(2)}, u32[]{:S(2)}) collective-permute-start(bf16[16,128,128]{2,1,0:T(8,128)(2,1)S(1)} %get-tuple-element.45), channel_id=1, source_target_pairs={{0,128},{32,160},{64,192},{96,224},{128,0},{160,32},{192,64},{224,... | collective-permute-start | bytes 1572872 | tf_op jit(solution)/shard_map/ppermute | solution.py:326
  96.6 5.5 %collective-permute-start.17 = (bf16[12,128,128]{2,1,0:T(8,128)(2,1)S(1)}, bf16[12,128,128]{2,1,0:T(8,128)(2,1)S(1)}, u32[]{:S(2)}, u32[]{:S(2)}) collective-permute-start(bf16[12,128,128]{2,1,0:T(8,128)(2,1)S(1)} %add_along_x.3), channel_id=1, source_target_pairs={{0,32},{32,0},{64,96},{96,64},{128,160},{160,128},{192,224},{224,1... | collective-permute-start | bytes 1179656 | tf_op jit(solution)/shard_map/ppermute | solution.py:331
  103.1 3.7 %collective-permute-done.10.refs_1_ = bf16[16,128,128]{2,1,0:T(8,128)(2,1)S(1)} collective-permute-done((bf16[16,128,128]{2,1,0:T(8,128)(2,1)S(1)}, bf16[16,128,128]{2,1,0:T(8,128)(2,1)S(1)}, u32[]{:S(2)}, u32[]{:S(2)}) %collective-permute-start.10) | collective-permute-done | bytes 524320 | tf_op jit(solution)/shard_map/ppermute | solution.py:326
  107.4 11.2 %collective-permute-done.11.refs_2_ = bf16[16,128,128]{2,1,0:T(8,128)(2,1)S(1)} collective-permute-done((bf16[16,128,128]{2,1,0:T(8,128)(2,1)S(1)}, bf16[16,128,128]{2,1,0:T(8,128)(2,1)S(1)}, u32[]{:S(2)}, u32[]{:S(2)}) %collective-permute-start.11) | collective-permute-done | bytes 524320 | tf_op jit(solution)/shard_map/ppermute | solution.py:326
  119.9 5.6 %collective-permute-start.13 = (bf16[16,128,128]{2,1,0:T(8,128)(2,1)S(1)}, bf16[16,128,128]{2,1,0:T(8,128)(2,1)S(1)}, u32[]{:S(2)}, u32[]{:S(2)}) collective-permute-start(bf16[16,128,128]{2,1,0:T(8,128)(2,1)S(1)} %add_along_x.2), channel_id=1, source_target_pairs={{0,32},{32,0},{64,96},{96,64},{128,160},{160,128},{192,224},{224,1... | collective-permute-start | bytes 1572872 | tf_op jit(solution)/shard_map/ppermute | solution.py:331
  126.3 2.4 %collective-permute-start.19 = (bf16[12,128,128]{2,1,0:T(8,128)(2,1)S(1)}, bf16[12,128,128]{2,1,0:T(8,128)(2,1)S(1)}, u32[]{:S(2)}, u32[]{:S(2)}) collective-permute-start(bf16[12,128,128]{2,1,0:T(8,128)(2,1)S(1)} %multiply_convert_fusion.1.refs_1_), channel_id=1, source_target_pairs={{0,128},{32,160},{64,192},{96,224},{128,0},{160,32},{192,64},{224,... | collective-permute-start | bytes 1179656 | tf_op jit(solution)/shard_map/ppermute | solution.py:349
  129.0 4.5 %collective-permute-done.24 = bf16[64,4096]{1,0:T(8,128)(2,1)S(1)} collective-permute-done((bf16[64,4096]{1,0:T(8,128)(2,1)S(1)}, bf16[64,4096]{1,0:T(8,128)(2,1)S(1)}, u32[]{:S(2)}, u32[]{:S(2)}) %collective-permute-start.24) | collective-permute-done | bytes 524320 | tf_op jit(solution)/shard_map/ppermute | solution.py:335
  134.5 6.0 %all-to-all-start.1 = ((bf16[32,7,16,128]{3,2,1,0:T(8,128)(2,1)}), bf16[32,7,16,128]{3,2,1,0:T(8,128)(2,1)}, u32[]{:S(2)}, u32[]{:S(2)}) async-start(bf16[32,7,16,128]{3,2,1,0:T(8,128)(2,1)} %pad_maximum_fusion), calls=%async_computation.1 | async-start | bytes 1835008 | tf_op jit(solution)/shard_map/all_to_all | solution.py:351
  140.6 5.0 %collective-permute-done.19.refs_3_ = bf16[12,128,128]{2,1,0:T(8,128)(2,1)S(1)} collective-permute-done((bf16[12,128,128]{2,1,0:T(8,128)(2,1)S(1)}, bf16[12,128,128]{2,1,0:T(8,128)(2,1)S(1)}, u32[]{:S(2)}, u32[]{:S(2)}) %collective-permute-start.19) | collective-permute-done | bytes 393248 | tf_op jit(solution)/shard_map/ppermute | solution.py:349
  147.1 1.3 collective-permute-start.28
  148.4 3.0 %collective-permute-start.29 = (bf16[16,128,128]{2,1,0:T(8,128)(2,1)S(1)}, bf16[16,128,128]{2,1,0:T(8,128)(2,1)S(1)}, u32[]{:S(2)}, u32[]{:S(2)}) collective-permute-start(bf16[16,128,128]{2,1,0:T(8,128)(2,1)S(1)} %multiply_convert_fusion.refs_1_), channel_id=1, source_target_pairs={{0,128},{32,160},{64,192},{96,224},{128,0},{160,32},{192,64},{224,... | collective-permute-start | bytes 1572872 | tf_op jit(solution)/shard_map/ppermute | solution.py:349
  152.5 3.1 %collective-permute-start.25 = (bf16[16,4096]{1,0:T(8,128)(2,1)S(1)}, bf16[16,4096]{1,0:T(8,128)(2,1)S(1)}, u32[]{:S(2)}, u32[]{:S(2)}) collective-permute-start(bf16[16,4096]{1,0:T(8,128)(2,1)S(1)} %get-tuple-element.84), channel_id=1, source_target_pairs={{0,24},{1,25},{2,26},{3,27},{4,28},{5,29},{6,30},{7,31},{8,0},{9,1... | collective-permute-start | bytes 393224 | tf_op jit(solution)/shard_map/ppermute | solution.py:352
  155.6 3.3 %collective-permute-start.26 = (bf16[16,4096]{1,0:T(8,128)(2,1)S(1)}, bf16[16,4096]{1,0:T(8,128)(2,1)}, u32[]{:S(2)}, u32[]{:S(2)}) collective-permute-start(bf16[16,4096]{1,0:T(8,128)(2,1)S(1)} %get-tuple-element.83), channel_id=1, source_target_pairs={{0,16},{1,17},{2,18},{3,19},{4,20},{5,21},{6,22},{7,23},{8,24},{9,... | collective-permute-start | bytes 393224 | tf_op jit(solution)/shard_map/ppermute | solution.py:352
  158.9 7.4 %collective-permute-done.25 = bf16[16,4096]{1,0:T(8,128)(2,1)S(1)} collective-permute-done((bf16[16,4096]{1,0:T(8,128)(2,1)S(1)}, bf16[16,4096]{1,0:T(8,128)(2,1)S(1)}, u32[]{:S(2)}, u32[]{:S(2)}) %collective-permute-start.25) | collective-permute-done | bytes 131104 | tf_op jit(solution)/shard_map/ppermute | solution.py:352
  166.3 14.0 %collective-permute-start.27 = (bf16[16,4096]{1,0:T(8,128)(2,1)S(1)}, bf16[16,4096]{1,0:T(8,128)(2,1)}, u32[]{:S(2)}, u32[]{:S(2)}) collective-permute-start(bf16[16,4096]{1,0:T(8,128)(2,1)S(1)} %get-tuple-element.82), channel_id=1, source_target_pairs={{0,8},{1,9},{2,10},{3,11},{4,12},{5,13},{6,14},{7,15},{8,16},{9,17... | collective-permute-start | bytes 393224 | tf_op jit(solution)/shard_map/ppermute | solution.py:352
  181.4 1.7 place_blocks.2.refs_5_
  183.2 1.9 gather_fusion.1
  186.0 1.8 fusion.2
  187.8 1.9 place_blocks.3
  (107 shorter events, 28.0 us)
Async XLA Ops:
  6.3 14.0 %collective-permute-start = (bf16[16,4096]{1,0:T(8,128)(2,1)S(1)}, bf16[16,4096]{1,0:T(8,128)(2,1)S(1)}, u32[]{:S(2)}, u32[]{:S(2)}) collective-permute-start(bf16[16,4096]{1,0:T(8,128)(2,1)S(1)} %copy-done.6), channel_id=1, source_target_pairs={{0,8},{1,9},{2,10},{3,11},{4,12},{5,13},{6,14},{7,15},{8,16},{9,17... | collective-permute-start | bytes 393224 | tf_op jit(solution)/shard_map/ppermute | solution.py:283
  8.7 12.3 %collective-permute-start.1 = (bf16[16,4096]{1,0:T(8,128)(2,1)S(1)}, bf16[16,4096]{1,0:T(8,128)(2,1)S(1)}, u32[]{:S(2)}, u32[]{:S(2)}) collective-permute-start(bf16[16,4096]{1,0:T(8,128)(2,1)S(1)} %copy-done.6), channel_id=1, source_target_pairs={{0,16},{1,17},{2,18},{3,19},{4,20},{5,21},{6,22},{7,23},{8,24},{9,... | collective-permute-start | bytes 393224 | tf_op jit(solution)/shard_map/ppermute | solution.py:283
  11.7 9.4 %collective-permute-start.2 = (bf16[16,4096]{1,0:T(8,128)(2,1)S(1)}, bf16[16,4096]{1,0:T(8,128)(2,1)S(1)}, u32[]{:S(2)}, u32[]{:S(2)}) collective-permute-start(bf16[16,4096]{1,0:T(8,128)(2,1)S(1)} %copy-done.6), channel_id=1, source_target_pairs={{0,24},{1,25},{2,26},{3,27},{4,28},{5,29},{6,30},{7,31},{8,0},{9,1... | collective-permute-start | bytes 393224 | tf_op jit(solution)/shard_map/ppermute | solution.py:283
  12.5 43.5 %all-to-all-start = ((bf16[32,7,16,128]{3,2,1,0:T(8,128)(2,1)}), bf16[32,7,16,128]{3,2,1,0:T(8,128)(2,1)S(1)}, u32[]{:S(2)}, u32[]{:S(2)}) async-start(bf16[32,7,16,128]{3,2,1,0:T(8,128)(2,1)} %broadcast_select_fusion), calls=%async_computation | async-start | bytes 1835008 | tf_op jit(solution)/shard_map/all_to_all | solution.py:281
  21.1 34.9 %collective-permute-start.3 = (bf16[64,4096]{1,0:T(8,128)(2,1)S(1)}, bf16[64,4096]{1,0:T(8,128)(2,1)S(1)}, u32[]{:S(2)}, u32[]{:S(2)}) collective-permute-start(bf16[64,4096]{1,0:T(8,128)(2,1)S(1)} %constant_dynamic-update-slice_fusion.rest_0_), channel_id=1, source_target_pairs={{0,2},{1,3},{2,4},{3,5},{4,6},{5,7},{6,0},{7,1},{8,10},{9,11},{10,... | collective-permute-start | bytes 1572872 | tf_op jit(solution)/shard_map/ppermute | solution.py:285
  22.4 32.8 %collective-permute-start.4 = (bf16[64,4096]{1,0:T(8,128)(2,1)S(1)}, bf16[64,4096]{1,0:T(8,128)(2,1)S(1)}, u32[]{:S(2)}, u32[]{:S(2)}) collective-permute-start(bf16[64,4096]{1,0:T(8,128)(2,1)S(1)} %constant_dynamic-update-slice_fusion.rest_0_), channel_id=1, source_target_pairs={{0,4},{1,5},{2,6},{3,7},{4,0},{5,1},{6,2},{7,3},{8,12},{9,13},{10,... | collective-permute-start | bytes 1572872 | tf_op jit(solution)/shard_map/ppermute | solution.py:285
  25.1 30.9 %collective-permute-start.5 = (bf16[64,4096]{1,0:T(8,128)(2,1)S(1)}, bf16[64,4096]{1,0:T(8,128)(2,1)S(1)}, u32[]{:S(2)}, u32[]{:S(2)}) collective-permute-start(bf16[64,4096]{1,0:T(8,128)(2,1)S(1)} %constant_dynamic-update-slice_fusion.rest_0_), channel_id=1, source_target_pairs={{0,6},{1,7},{2,0},{3,1},{4,2},{5,3},{6,4},{7,5},{8,14},{9,15},{10,... | collective-permute-start | bytes 1572872 | tf_op jit(solution)/shard_map/ppermute | solution.py:285
  26.6 31.0 %collective-permute-start.6 = (bf16[64,4096]{1,0:T(8,128)(2,1)S(1)}, bf16[64,4096]{1,0:T(8,128)(2,1)}, u32[]{:S(2)}, u32[]{:S(2)}) collective-permute-start(bf16[64,4096]{1,0:T(8,128)(2,1)S(1)} %constant_dynamic-update-slice_fusion.rest_0_), channel_id=1, source_target_pairs={{0,1},{1,0},{2,3},{3,2},{4,5},{5,4},{6,7},{7,6},{8,9},{9,8},{10,11... | collective-permute-start | bytes 1572872 | tf_op jit(solution)/shard_map/ppermute | solution.py:287
  55.2 2.4 %collective-permute-start.8 = (bf16[64,4096]{1,0:T(8,128)(2,1)S(1)}, bf16[64,4096]{1,0:T(8,128)(2,1)}, u32[]{:S(2)}, u32[]{:S(2)}) collective-permute-start(bf16[64,4096]{1,0:T(8,128)(2,1)S(1)} %collective-permute-done.4.rest_2_), channel_id=1, source_target_pairs={{0,1},{1,0},{2,3},{3,2},{4,5},{5,4},{6,7},{7,6},{8,9},{9,8},{10,11... | collective-permute-start | bytes 1572872 | tf_op jit(solution)/shard_map/ppermute | solution.py:287
  56.0 3.1 %collective-permute-start.7 = (bf16[64,4096]{1,0:T(8,128)(2,1)S(1)}, bf16[64,4096]{1,0:T(8,128)(2,1)}, u32[]{:S(2)}, u32[]{:S(2)}) collective-permute-start(bf16[64,4096]{1,0:T(8,128)(2,1)S(1)} %collective-permute-done.3.rest_1_), channel_id=1, source_target_pairs={{0,1},{1,0},{2,3},{3,2},{4,5},{5,4},{6,7},{7,6},{8,9},{9,8},{10,11... | collective-permute-start | bytes 1572872 | tf_op jit(solution)/shard_map/ppermute | solution.py:287
  69.3 20.2 %collective-permute-start.14 = (bf16[12,128,128]{2,1,0:T(8,128)(2,1)S(1)}, bf16[12,128,128]{2,1,0:T(8,128)(2,1)S(1)}, u32[]{:S(2)}, u32[]{:S(2)}) collective-permute-start(bf16[12,128,128]{2,1,0:T(8,128)(2,1)S(1)} %get-tuple-element.49), channel_id=1, source_target_pairs={{0,64},{32,96},{64,128},{96,160},{128,192},{160,224},{192,0},{224,... | collective-permute-start | bytes 1179656 | tf_op jit(solution)/shard_map/ppermute | solution.py:326
  70.8 19.7 %collective-permute-start.15 = (bf16[12,128,128]{2,1,0:T(8,128)(2,1)S(1)}, bf16[12,128,128]{2,1,0:T(8,128)(2,1)S(1)}, u32[]{:S(2)}, u32[]{:S(2)}) collective-permute-start(bf16[12,128,128]{2,1,0:T(8,128)(2,1)S(1)} %get-tuple-element.50), channel_id=1, source_target_pairs={{0,128},{32,160},{64,192},{96,224},{128,0},{160,32},{192,64},{224,... | collective-permute-start | bytes 1179656 | tf_op jit(solution)/shard_map/ppermute | solution.py:326
  73.2 17.3 %collective-permute-start.16 = (bf16[12,128,128]{2,1,0:T(8,128)(2,1)S(1)}, bf16[12,128,128]{2,1,0:T(8,128)(2,1)S(1)}, u32[]{:S(2)}, u32[]{:S(2)}) collective-permute-start(bf16[12,128,128]{2,1,0:T(8,128)(2,1)S(1)} %get-tuple-element.51), channel_id=1, source_target_pairs={{0,192},{32,224},{64,0},{96,32},{128,64},{160,96},{192,128},{224,1... | collective-permute-start | bytes 1179656 | tf_op jit(solution)/shard_map/ppermute | solution.py:326
  90.8 11.3 %collective-permute-start.21 = (bf16[256,4096]{1,0:T(8,128)(2,1)S(1)}, bf16[256,4096]{1,0:T(8,128)(2,1)S(1)}, u32[]{:S(2)}, u32[]{:S(2)}) collective-permute-start(bf16[256,4096]{1,0:T(8,128)(2,1)S(1)} %get-tuple-element.56), channel_id=1, source_target_pairs={{0,1},{1,0},{2,3},{3,2},{4,5},{5,4},{6,7},{7,6},{8,9},{9,8},{10,11... | collective-permute-start | bytes 6291464 | tf_op jit(solution)/shard_map/ppermute | solution.py:332
  92.1 14.7 %collective-permute-start.10 = (bf16[16,128,128]{2,1,0:T(8,128)(2,1)S(1)}, bf16[16,128,128]{2,1,0:T(8,128)(2,1)S(1)}, u32[]{:S(2)}, u32[]{:S(2)}) collective-permute-start(bf16[16,128,128]{2,1,0:T(8,128)(2,1)S(1)} %get-tuple-element.44), channel_id=1, source_target_pairs={{0,64},{32,96},{64,128},{96,160},{128,192},{160,224},{192,0},{224,... | collective-permute-start | bytes 1572872 | tf_op jit(solution)/shard_map/ppermute | solution.py:326
  93.2 25.4 %collective-permute-start.11 = (bf16[16,128,128]{2,1,0:T(8,128)(2,1)S(1)}, bf16[16,128,128]{2,1,0:T(8,128)(2,1)S(1)}, u32[]{:S(2)}, u32[]{:S(2)}) collective-permute-start(bf16[16,128,128]{2,1,0:T(8,128)(2,1)S(1)} %get-tuple-element.45), channel_id=1, source_target_pairs={{0,128},{32,160},{64,192},{96,224},{128,0},{160,32},{192,64},{224,... | collective-permute-start | bytes 1572872 | tf_op jit(solution)/shard_map/ppermute | solution.py:326
  95.3 24.3 %collective-permute-start.12 = (bf16[16,128,128]{2,1,0:T(8,128)(2,1)S(1)}, bf16[16,128,128]{2,1,0:T(8,128)(2,1)S(1)}, u32[]{:S(2)}, u32[]{:S(2)}) collective-permute-start(bf16[16,128,128]{2,1,0:T(8,128)(2,1)S(1)} %get-tuple-element.46), channel_id=1, source_target_pairs={{0,192},{32,224},{64,0},{96,32},{128,64},{160,96},{192,128},{224,1... | collective-permute-start | bytes 1572872 | tf_op jit(solution)/shard_map/ppermute | solution.py:326
  96.6 29.0 %collective-permute-start.17 = (bf16[12,128,128]{2,1,0:T(8,128)(2,1)S(1)}, bf16[12,128,128]{2,1,0:T(8,128)(2,1)S(1)}, u32[]{:S(2)}, u32[]{:S(2)}) collective-permute-start(bf16[12,128,128]{2,1,0:T(8,128)(2,1)S(1)} %add_along_x.3), channel_id=1, source_target_pairs={{0,32},{32,0},{64,96},{96,64},{128,160},{160,128},{192,224},{224,1... | collective-permute-start | bytes 1179656 | tf_op jit(solution)/shard_map/ppermute | solution.py:331
  103.0 23.3 %collective-permute-start.22 = (bf16[64,4096]{1,0:T(8,128)(2,1)S(1)}, bf16[64,4096]{1,0:T(8,128)(2,1)S(1)}, u32[]{:S(2)}, u32[]{:S(2)}) collective-permute-start(bf16[64,4096]{1,0:T(8,128)(2,1)S(1)} %get-tuple-element.79), channel_id=1, source_target_pairs={{0,6},{1,7},{2,0},{3,1},{4,2},{5,3},{6,4},{7,5},{8,14},{9,15},{10,... | collective-permute-start | bytes 1572872 | tf_op jit(solution)/shard_map/ppermute | solution.py:335
  106.8 22.0 %collective-permute-start.23 = (bf16[64,4096]{1,0:T(8,128)(2,1)S(1)}, bf16[64,4096]{1,0:T(8,128)(2,1)S(1)}, u32[]{:S(2)}, u32[]{:S(2)}) collective-permute-start(bf16[64,4096]{1,0:T(8,128)(2,1)S(1)} %get-tuple-element.81), channel_id=1, source_target_pairs={{0,4},{1,5},{2,6},{3,7},{4,0},{5,1},{6,2},{7,3},{8,12},{9,13},{10,... | collective-permute-start | bytes 1572872 | tf_op jit(solution)/shard_map/ppermute | solution.py:335
  118.5 14.9 %collective-permute-start.24 = (bf16[64,4096]{1,0:T(8,128)(2,1)S(1)}, bf16[64,4096]{1,0:T(8,128)(2,1)S(1)}, u32[]{:S(2)}, u32[]{:S(2)}) collective-permute-start(bf16[64,4096]{1,0:T(8,128)(2,1)S(1)} %get-tuple-element.80), channel_id=1, source_target_pairs={{0,2},{1,3},{2,4},{3,5},{4,6},{5,7},{6,0},{7,1},{8,10},{9,11},{10,... | collective-permute-start | bytes 1572872 | tf_op jit(solution)/shard_map/ppermute | solution.py:335
  119.9 20.6 %collective-permute-start.13 = (bf16[16,128,128]{2,1,0:T(8,128)(2,1)S(1)}, bf16[16,128,128]{2,1,0:T(8,128)(2,1)S(1)}, u32[]{:S(2)}, u32[]{:S(2)}) collective-permute-start(bf16[16,128,128]{2,1,0:T(8,128)(2,1)S(1)} %add_along_x.2), channel_id=1, source_target_pairs={{0,32},{32,0},{64,96},{96,64},{128,160},{160,128},{192,224},{224,1... | collective-permute-start | bytes 1572872 | tf_op jit(solution)/shard_map/ppermute | solution.py:331
  125.7 14.9 %collective-permute-start.18 = (bf16[12,128,128]{2,1,0:T(8,128)(2,1)S(1)}, bf16[12,128,128]{2,1,0:T(8,128)(2,1)S(1)}, u32[]{:S(2)}, u32[]{:S(2)}) collective-permute-start(bf16[12,128,128]{2,1,0:T(8,128)(2,1)S(1)} %multiply_convert_fusion.1.refs_1_), channel_id=1, source_target_pairs={{0,64},{32,96},{64,128},{96,160},{128,192},{160,224},{192,0},{224,... | collective-permute-start | bytes 1179656 | tf_op jit(solution)/shard_map/ppermute | solution.py:349
  126.3 19.2 %collective-permute-start.19 = (bf16[12,128,128]{2,1,0:T(8,128)(2,1)S(1)}, bf16[12,128,128]{2,1,0:T(8,128)(2,1)S(1)}, u32[]{:S(2)}, u32[]{:S(2)}) collective-permute-start(bf16[12,128,128]{2,1,0:T(8,128)(2,1)S(1)} %multiply_convert_fusion.1.refs_1_), channel_id=1, source_target_pairs={{0,128},{32,160},{64,192},{96,224},{128,0},{160,32},{192,64},{224,... | collective-permute-start | bytes 1179656 | tf_op jit(solution)/shard_map/ppermute | solution.py:349
  128.8 17.6 %collective-permute-start.20 = (bf16[12,128,128]{2,1,0:T(8,128)(2,1)S(1)}, bf16[12,128,128]{2,1,0:T(8,128)(2,1)S(1)}, u32[]{:S(2)}, u32[]{:S(2)}) collective-permute-start(bf16[12,128,128]{2,1,0:T(8,128)(2,1)S(1)} %multiply_convert_fusion.1.refs_1_), channel_id=1, source_target_pairs={{0,192},{32,224},{64,0},{96,32},{128,64},{160,96},{192,128},{224,1... | collective-permute-start | bytes 1179656 | tf_op jit(solution)/shard_map/ppermute | solution.py:349
  134.5 48.6 %all-to-all-start.1 = ((bf16[32,7,16,128]{3,2,1,0:T(8,128)(2,1)}), bf16[32,7,16,128]{3,2,1,0:T(8,128)(2,1)}, u32[]{:S(2)}, u32[]{:S(2)}) async-start(bf16[32,7,16,128]{3,2,1,0:T(8,128)(2,1)} %pad_maximum_fusion), calls=%async_computation.1 | async-start | bytes 1835008 | tf_op jit(solution)/shard_map/all_to_all | solution.py:351
  147.1 36.0 %collective-permute-start.28 = (bf16[16,128,128]{2,1,0:T(8,128)(2,1)S(1)}, bf16[16,128,128]{2,1,0:T(8,128)(2,1)S(1)}, u32[]{:S(2)}, u32[]{:S(2)}) collective-permute-start(bf16[16,128,128]{2,1,0:T(8,128)(2,1)S(1)} %multiply_convert_fusion.refs_1_), channel_id=1, source_target_pairs={{0,64},{32,96},{64,128},{96,160},{128,192},{160,224},{192,0},{224,... | collective-permute-start | bytes 1572872 | tf_op jit(solution)/shard_map/ppermute | solution.py:349
  148.4 34.7 %collective-permute-start.29 = (bf16[16,128,128]{2,1,0:T(8,128)(2,1)S(1)}, bf16[16,128,128]{2,1,0:T(8,128)(2,1)S(1)}, u32[]{:S(2)}, u32[]{:S(2)}) collective-permute-start(bf16[16,128,128]{2,1,0:T(8,128)(2,1)S(1)} %multiply_convert_fusion.refs_1_), channel_id=1, source_target_pairs={{0,128},{32,160},{64,192},{96,224},{128,0},{160,32},{192,64},{224,... | collective-permute-start | bytes 1572872 | tf_op jit(solution)/shard_map/ppermute | solution.py:349
  151.4 31.7 %collective-permute-start.30 = (bf16[16,128,128]{2,1,0:T(8,128)(2,1)S(1)}, bf16[16,128,128]{2,1,0:T(8,128)(2,1)S(1)}, u32[]{:S(2)}, u32[]{:S(2)}) collective-permute-start(bf16[16,128,128]{2,1,0:T(8,128)(2,1)S(1)} %multiply_convert_fusion.refs_1_), channel_id=1, source_target_pairs={{0,192},{32,224},{64,0},{96,32},{128,64},{160,96},{192,128},{224,1... | collective-permute-start | bytes 1572872 | tf_op jit(solution)/shard_map/ppermute | solution.py:349
  152.5 13.8 %collective-permute-start.25 = (bf16[16,4096]{1,0:T(8,128)(2,1)S(1)}, bf16[16,4096]{1,0:T(8,128)(2,1)S(1)}, u32[]{:S(2)}, u32[]{:S(2)}) collective-permute-start(bf16[16,4096]{1,0:T(8,128)(2,1)S(1)} %get-tuple-element.84), channel_id=1, source_target_pairs={{0,24},{1,25},{2,26},{3,27},{4,28},{5,29},{6,30},{7,31},{8,0},{9,1... | collective-permute-start | bytes 393224 | tf_op jit(solution)/shard_map/ppermute | solution.py:352
  155.6 27.5 %collective-permute-start.26 = (bf16[16,4096]{1,0:T(8,128)(2,1)S(1)}, bf16[16,4096]{1,0:T(8,128)(2,1)}, u32[]{:S(2)}, u32[]{:S(2)}) collective-permute-start(bf16[16,4096]{1,0:T(8,128)(2,1)S(1)} %get-tuple-element.83), channel_id=1, source_target_pairs={{0,16},{1,17},{2,18},{3,19},{4,20},{5,21},{6,22},{7,23},{8,24},{9,... | collective-permute-start | bytes 393224 | tf_op jit(solution)/shard_map/ppermute | solution.py:352
  166.3 16.8 %collective-permute-start.27 = (bf16[16,4096]{1,0:T(8,128)(2,1)S(1)}, bf16[16,4096]{1,0:T(8,128)(2,1)}, u32[]{:S(2)}, u32[]{:S(2)}) collective-permute-start(bf16[16,4096]{1,0:T(8,128)(2,1)S(1)} %get-tuple-element.82), channel_id=1, source_target_pairs={{0,8},{1,9},{2,10},{3,11},{4,12},{5,13},{6,14},{7,15},{8,16},{9,17... | collective-permute-start | bytes 393224 | tf_op jit(solution)/shard_map/ppermute | solution.py:352
  (9 other events, 61.7 us)
